TPU v7x, 128 devices: a whole 4x4x4 slice. The times are simulated.
128 devices in a mesh: row: 16 (over x, z), col: 8 (over y, core).
Axes of the slice: x: 4, y: 4, z: 4, core: 2. Of those that a mesh axis runs over, the one named last changes fastest.
Arguments:
- rhs_first: bfloat16 [2, 2048, 1024], P(None, 'row', 'col'), may hold values from -6 to 6
- rhs_last: bfloat16 [2, 2048, 1024], P(None, 'row', 'col'), may hold values from -6 to 6
- inv_first: bfloat16 [2, 2048, 2048], P(None, 'row', 'col'), may hold values from -0.09375 to 0.09375
- coupling: bfloat16 [2, 2048, 2048], P(None, 'row', 'col'), may hold values from -0.09375 to 0.09375
- inv_last: bfloat16 [2, 2048, 2048], P(None, 'row', 'col'), may hold values from -0.09375 to 0.09375
- earlier: bfloat16 [2, 49152, 1024], P(None, 'row', 'col'), may hold values from -6 to 6
- patch_old: int32 [49152], P('row'), may hold values from 0 to 4095
- weight_old: bfloat16 [49152], P('row'), may hold values from -4 to 4
- patch_new: int32 [2, 2048], P(None, 'row'), may hold values from 0 to 4095
- weight_new: bfloat16 [2, 2048], P(None, 'row'), may hold values from -4 to 4
- stress_map: bfloat16 [2, 16384, 4096], P(None, 'row', 'col'), may hold values from -0.03125 to 0.03125
Outputs:
- pressures: bfloat16 [2, 2, 2048, 1024], P(None, None, 'row', 'col')
- stress_rao: bfloat16 [2, 16384, 1024], P(None, 'row', 'col')
All inputs are finite; a program needn't handle non-finite values.
Results may differ from a plain program's by a relative error of at most 0.006.
Values may be sent and summed in bfloat16 or wider, within the bound.
No kernel may reach another device: no remote copies, remote signals or barrier semaphores. Data moves between devices by JAX's collectives and lax.ppermute only.
A program may use at most 128 MiB of HBM per device.

v0:
```python
import math

import jax
import jax.numpy as jnp
from jax import lax
from jax.sharding import PartitionSpec as P

PATCHES = 4096


def complex_dot(matrix, vectors):
    real_real = jnp.dot(matrix[0], vectors[0], preferred_element_type=jnp.float32)
    imag_imag = jnp.dot(matrix[1], vectors[1], preferred_element_type=jnp.float32)
    real_imag = jnp.dot(matrix[0], vectors[1], preferred_element_type=jnp.float32)
    imag_real = jnp.dot(matrix[1], vectors[0], preferred_element_type=jnp.float32)
    return jnp.stack([real_real - imag_imag, real_imag + imag_real])


def block_product(matrix, vectors):
    gathered = lax.all_gather(vectors, "row", axis=1, tiled=True)
    return complex_dot(lax.all_gather(matrix, "col", axis=2, tiled=True), gathered)


def on_device(
    rhs_first,
    rhs_last,
    inv_first,
    coupling,
    inv_last,
    earlier,
    patch_old,
    weight_old,
    patch_new,
    weight_new,
    stress_map,
):
    x_first = block_product(inv_first, rhs_first).astype(jnp.bfloat16)
    reduced = (rhs_last.astype(jnp.float32) - block_product(coupling, x_first)).astype(jnp.bfloat16)
    x_last = block_product(inv_last, reduced).astype(jnp.bfloat16)
    pressures = jnp.stack([x_first, x_last])
    pressures_all = jnp.concatenate([earlier, x_first, x_last], axis=1)
    patch_ids = jnp.concatenate([patch_old, patch_new[0], patch_new[1]])
    panel_weights = jnp.concatenate([weight_old, weight_new[0], weight_new[1]])
    panel_count = pressures_all.shape[1]
    right_sides = pressures_all.shape[2]
    block_size = math.gcd(panel_count, 256)
    block_count = panel_count // block_size
    patch_index = lax.broadcasted_iota(jnp.int32, (PATCHES, block_size), 0)
    nothing = jnp.zeros((), jnp.bfloat16)

    def add_block(step_index, running):
        offset = step_index * block_size
        block_ids = lax.dynamic_slice_in_dim(patch_ids, offset, block_size, 0)
        block_weights = lax.dynamic_slice_in_dim(panel_weights, offset, block_size, 0)
        onehot_block = jnp.where(block_ids[None, :] == patch_index, block_weights[None, :], nothing)
        block_values = lax.dynamic_slice_in_dim(pressures_all, offset, block_size, 1)
        real_part = jnp.dot(onehot_block, block_values[0], preferred_element_type=jnp.float32)
        imag_part = jnp.dot(onehot_block, block_values[1], preferred_element_type=jnp.float32)
        return running + jnp.stack([real_part, imag_part])

    partial_loads = lax.fori_loop(
        0, block_count, add_block, jnp.zeros((2, PATCHES, right_sides), jnp.float32)
    )
    turned = lax.all_to_all(partial_loads, "col", split_axis=1, concat_axis=2, tiled=True)
    patch_loads = lax.psum(turned, "row").astype(jnp.bfloat16)
    partial_terms = complex_dot(stress_map, patch_loads)
    stress_rao = lax.psum_scatter(partial_terms, "col", scatter_dimension=2, tiled=True).astype(
        jnp.bfloat16
    )
    return (pressures, stress_rao)


def solution(mesh):
    in_specs = (
        P(None, "row", "col"),
        P(None, "row", "col"),
        P(None, "row", "col"),
        P(None, "row", "col"),
        P(None, "row", "col"),
        P(None, "row", "col"),
        P("row"),
        P("row"),
        P(None, "row"),
        P(None, "row"),
        P(None, "row", "col"),
    )
    out_specs = (P(None, None, "row", "col"), P(None, "row", "col"))
    return jax.shard_map(
        on_device, mesh=mesh, in_specs=in_specs, out_specs=out_specs, check_vma=False
    )
```

profile of v0, /device:TPU:0, one launch (start us, length us, event | category | flops | bytes accessed | tf_op | source)
XLA Modules:
  0.0 550.8 jit_solution(11382676276613227303)
XLA Ops:
  9.4 26.1 %all-gather.7.cloned.1.call-done = bf16[2,128,2048]{2,1,0:T(8,128)(2,1)} async-done(((bf16[2,128,256]{2,1,0:T(8,128)(2,1)}), bf16[2,128,2048]{2,1,0:T(8,128)(2,1)}) %all-gather.7.cloned.1.call-update) | async-done | bytes 1048592 | tf_op jit(solution)/shard_map/all_gather | solution.py:21
  35.6 46.0 %all-gather.9.cloned.1.call-done = bf16[2,2048,128]{2,1,0:T(8,128)(2,1)} async-done(((bf16[2,128,128]{2,1,0:T(8,128)(2,1)}), bf16[2,2048,128]{2,1,0:T(8,128)(2,1)}) %all-gather.9.cloned.1.call-update) | async-done | bytes 1048592 | tf_op jit(solution)/shard_map/all_gather | solution.py:20
  81.6 1.6 fusion.31
  83.2 1.5 fusion.32
  84.7 1.5 fusion.18
  88.0 18.0 %all-gather.13.cloned.1.call-done = bf16[2,128,2048]{2,1,0:T(8,128)(2,1)} async-done(((bf16[2,128,256]{2,1,0:T(8,128)(2,1)}), bf16[2,128,2048]{2,1,0:T(8,128)(2,1)}) %all-gather.13.cloned.1.call-update) | async-done | bytes 1048592 | tf_op jit(solution)/shard_map/all_gather | solution.py:21
  105.9 46.5 %all-gather.11.cloned.1.call-done = bf16[2,2048,128]{2,1,0:T(8,128)(2,1)} async-done(((bf16[2,128,128]{2,1,0:T(8,128)(2,1)}), bf16[2,2048,128]{2,1,0:T(8,128)(2,1)}) %all-gather.11.cloned.1.call-update) | async-done | bytes 1048592 | tf_op jit(solution)/shard_map/all_gather | solution.py:20
  152.4 1.6 fusion.34
  154.0 1.5 fusion.15
  155.6 1.5 fusion.33
  158.3 18.3 %all-gather.17.cloned.1.call-done = bf16[2,128,2048]{2,1,0:T(8,128)(2,1)} async-done(((bf16[2,128,256]{2,1,0:T(8,128)(2,1)}), bf16[2,128,2048]{2,1,0:T(8,128)(2,1)}) %all-gather.17.cloned.1.call-update) | async-done | bytes 1048592 | tf_op jit(solution)/shard_map/all_gather | solution.py:21
  176.6 47.0 %all-gather.15.cloned.1.call-done = bf16[2,2048,128]{1,2,0:T(8,128)(2,1)} async-done(((bf16[2,128,128]{1,2,0:T(8,128)(2,1)}), bf16[2,2048,128]{1,2,0:T(8,128)(2,1)}) %all-gather.15.cloned.1.call-update) | async-done | bytes 1048592 | tf_op jit(solution)/shard_map/all_gather | solution.py:20
  223.6 1.6 fusion.36
  225.2 1.5 fusion.35
  226.7 1.5 fusion.20
  228.7 80.4 %while.14 = (s32[]{:T(128)}, f32[2,4096,128]{2,1,0:T(8,128)}, s32[3328]{0:T(1024)S(1)}, bf16[3328]{0:T(1024)(128)(2,1)S(1)}, bf16[2,3328,128]{2,1,0:T(8,128)(2,1...) while((s32[]{:T(128)}, f32[2,4096,128]{2,1,0:T(8,128)}, s32[3328]{0:T(1024)S(1)}, ...), condition=%wide.region_1.2_spmd.clone, body=%wide.region_0.1_spmd.clone.sunk | while | flops 544210944 | bytes 50469116 | solution.py:61
  230.3 1.5 copy-done
  231.8 1.2 maximum_add_fusion.2
  232.9 1.9 copy-done.1
  236.5 1.5 copy-done
  237.9 1.2 maximum_add_fusion.2
  239.1 1.9 copy-done.1
  242.7 1.5 copy-done
  244.1 1.2 maximum_add_fusion.2
  245.3 1.9 copy-done.1
  248.8 1.5 copy-done
  250.3 1.2 maximum_add_fusion.2
  251.5 1.9 copy-done.1
  255.0 1.5 copy-done
  256.5 1.2 maximum_add_fusion.2
  257.7 1.9 copy-done.1
  261.2 1.5 copy-done
  262.7 1.2 maximum_add_fusion.2
  263.9 1.9 copy-done.1
  267.4 1.5 copy-done
  268.9 1.2 maximum_add_fusion.2
  270.0 1.9 copy-done.1
  273.6 1.5 copy-done
  276.2 1.9 copy-done.1
  279.8 1.5 copy-done
  281.2 1.2 maximum_add_fusion.2
  282.4 1.9 copy-done.1
  285.9 1.5 copy-done
  287.4 1.2 maximum_add_fusion.2
  288.6 1.9 copy-done.1
  292.1 1.5 copy-done
  293.6 1.2 maximum_add_fusion.2
  294.8 1.9 copy-done.1
  298.3 1.5 copy-done
  301.0 1.9 copy-done.1
  304.5 1.5 copy-done
  307.2 1.9 copy-done.1
  309.1 7.8 %copy.21 = f32[2,4096,128]{2,0,1:T(2,128)S(1)} copy(f32[2,4096,128]{2,1,0:T(8,128)} %get-tuple-element.111) | data formatting | bytes 8388608 | tf_op jit(solution)/shard_map/while | solution.py:61
  316.9 54.4 %all_to_all.18 = f32[2,4096,128]{2,0,1:T(2,128)S(1)} all-to-all(f32[2,4096,128]{2,0,1:T(2,128)S(1)} %copy.21), channel_id=1, replica_groups=mesh['row'=16,'col'=8] {'col'}, dimensions={1} | all-to-all | bytes 8388608 | tf_op jit(solution)/shard_map/all_to_all | solution.py:64
  371.3 2.2 copy.22
  373.6 5.4 copy.23
  379.0 102.4 %all-reduce.1 = bf16[2,512,1024]{1,2,0:T(8,128)(2,1)S(1)} all-reduce(f32[2,512,1024]{1,2,0:T(8,128)} %bitcast.127), channel_id=1, replica_groups=mesh['row'=16,'col'=8] {'row'}, use_global_device_ids=true, to_apply=%region_2.3 | all-reduce | flops 1048576 | bytes 6291456 | tf_op jit(solution)/shard_map/psum | solution.py:65
  481.4 2.7 fusion.25
  484.1 1.3 fusion.23
  485.4 1.4 subtract_bitcast_fusion
  486.8 1.4 add_bitcast_fusion
  488.1 4.1 pad_maximum_fusion
  493.0 48.7 %reduce-scatter.2.cloned.1.call-done = f32[2,1024,128]{1,2,0:T(8,128)} async-done(((f32[2,1024,1024]{1,2,0:T(8,128)}), f32[2,1024,128]{1,2,0:T(8,128)}) %reduce-scatter.2.cloned.1.call-update) | async-done | bytes 1048592 | tf_op jit(solution)/shard_map/reduce_scatter | solution.py:67
  541.7 1.3 convert_element_type.31
  (135 shorter events, 30.9 us)
Async XLA Ops:
  7.2 80.7 %copy-start.4 = (bf16[2,128,128]{2,1,0:T(8,128)(2,1)S(1)}, bf16[2,128,128]{2,1,0:T(8,128)(2,1)}, u32[]{:S(2)}) copy-start(bf16[2,128,128]{2,1,0:T(8,128)(2,1)} %param.14) | copy-start | bytes 196612
  7.2 28.4 %all-gather.7.cloned.1.call-start = ((), (), s32[]{:S(2)}) async-start(), calls=%async_computation.2 | async-start | bytes 1179648 | tf_op jit(solution)/shard_map/all_gather | solution.py:21
  7.9 73.7 %all-gather.9.cloned.1.call-start = ((), (), s32[]{:S(2)}) async-start(), calls=%async_computation.3 | async-start | bytes 1114112 | tf_op jit(solution)/shard_map/all_gather | solution.py:20
  8.7 97.3 %all-gather.13.cloned.1.call-start = ((), (), s32[]{:S(2)}) async-start(), calls=%async_computation.5 | async-start | bytes 1179648 | tf_op jit(solution)/shard_map/all_gather | solution.py:21
  9.4 143.0 %all-gather.11.cloned.1.call-start = ((), (), s32[]{:S(2)}) async-start(), calls=%async_computation.4 | async-start | bytes 1114112 | tf_op jit(solution)/shard_map/all_gather | solution.py:20
  35.6 50.6 %copy-start.12 = (bf16[2,128,2048]{2,1,0:T(8,128)(2,1)S(1)}, bf16[2,128,2048]{2,1,0:T(8,128)(2,1)}, u32[]{:S(2)}) copy-start(bf16[2,128,2048]{2,1,0:T(8,128)(2,1)} %all-gather.7.cloned.1.call-done) | copy-start | bytes 3145732
  81.6 4.6 copy-start.14
  86.5 71.7 %copy-start.7 = (bf16[2,128]{1,0:T(2,128)(2,1)S(1)}, bf16[2,128]{1,0:T(2,128)(2,1)}, u32[]{:S(2)}) copy-start(bf16[2,128]{1,0:T(2,128)(2,1)} %param.22) | copy-start | bytes 1540
  86.5 71.8 %copy-start.6 = (bf16[3072]{0:T(1024)(128)(2,1)S(1)}, bf16[3072]{0:T(1024)(128)(2,1)}, u32[]{:S(2)}) copy-start(bf16[3072]{0:T(1024)(128)(2,1)} %param.20) | copy-start | bytes 18436
  86.5 71.8 %copy-start.8 = (s32[2,128]{1,0:T(2,128)S(1)}, s32[2,128]{1,0:T(2,128)}, u32[]{:S(2)}) copy-start(s32[2,128]{1,0:T(2,128)} %param.21) | copy-start | bytes 3076
  86.5 71.8 %copy-start.5 = (s32[3072]{0:T(1024)S(1)}, s32[3072]{0:T(1024)}, u32[]{:S(2)}) copy-start(s32[3072]{0:T(1024)} %param.19) | copy-start | bytes 36868
  87.2 89.4 %all-gather.17.cloned.1.call-start = ((), (), s32[]{:S(2)}) async-start(), calls=%async_computation.7 | async-start | bytes 1179648 | tf_op jit(solution)/shard_map/all_gather | solution.py:21
  87.8 135.8 %all-gather.15.cloned.1.call-start = ((), (), s32[]{:S(2)}) async-start(), calls=%async_computation.6 | async-start | bytes 1114112 | tf_op jit(solution)/shard_map/all_gather | solution.py:20
  105.9 51.2 %copy-start.10 = (bf16[2,128,2048]{2,1,0:T(8,128)(2,1)S(1)}, bf16[2,128,2048]{2,1,0:T(8,128)(2,1)}, u32[]{:S(2)}) copy-start(bf16[2,128,2048]{2,1,0:T(8,128)(2,1)} %all-gather.13.cloned.1.call-done) | copy-start | bytes 3145732
  152.4 4.7 copy-start.13
  157.1 71.4 %copy-start.3 = (bf16[2,3072,128]{2,1,0:T(8,128)(2,1)S(1)}, bf16[2,3072,128]{2,1,0:T(8,128)(2,1)}, u32[]{:S(2)}) copy-start(bf16[2,3072,128]{2,1,0:T(8,128)(2,1)} %param.18) | copy-start | bytes 4718596
  158.2 383.5 %reduce-scatter.2.cloned.1.call-start = ((), (), s32[]{:S(2)}) async-start(), calls=%async_computation.8 | async-start | bytes 9437184 | tf_op jit(solution)/shard_map/reduce_scatter | solution.py:67
  176.6 51.6 %copy-start.9 = (bf16[2,128,2048]{2,1,0:T(8,128)(2,1)S(1)}, bf16[2,128,2048]{2,1,0:T(8,128)(2,1)}, u32[]{:S(2)}) copy-start(bf16[2,128,2048]{2,1,0:T(8,128)(2,1)} %all-gather.17.cloned.1.call-done) | copy-start | bytes 3145732
  223.6 4.6 copy-start.11
  229.6 2.2 copy-start
  232.9 2.0 copy-start.1
  235.7 2.2 copy-start
  239.1 2.0 copy-start.1
  241.9 2.2 copy-start
  245.3 2.0 copy-start.1
  248.1 2.2 copy-start
  251.5 2.0 copy-start.1
  254.3 2.2 copy-start
  257.7 2.0 copy-start.1
  260.5 2.2 copy-start
  263.9 2.0 copy-start.1
  266.7 2.2 copy-start
  270.0 2.0 copy-start.1
  272.9 2.2 copy-start
  276.2 2.0 copy-start.1
  279.0 2.2 copy-start
  282.4 2.0 copy-start.1
  285.2 2.2 copy-start
  288.6 2.0 copy-start.1
  291.4 2.2 copy-start
  294.8 2.0 copy-start.1
  297.6 2.2 copy-start
  301.0 2.0 copy-start.1
  303.8 2.2 copy-start
  307.1 2.0 copy-start.1
  481.4 2.7 copy-start.2
Sparse Core Ops, SparseCore 0:
  9.7 25.8 all-gather.6
  37.8 43.7 all-gather.8
  83.3 22.6 all-gather.12
  108.6 43.7 all-gather.10
  153.9 22.6 all-gather.16
  179.1 44.4 all-gather.14
  492.4 49.2 reduce-scatter.1
where the time goes:
time: 552 us; the launch traced here: 551 us
  waiting for transfers between devices  253 us (46%)
  blocking collectives  157 us (28%)
  local copies, waits for them, and re-layouts  63.2 us (11%)
  matrix products  39.7 us (7%)
  other arithmetic  22.7 us (4%)
  between operations  14.4 us (3%)
    all_gather x3, waiting for transfers between devices, block_product(): gathered = lax.all_gather(vectors, 'row', axis=1, tiled=True)  140 us
    psum x1, blocking collectives, on_device(): patch_loads = lax.psum(turned, 'row').astype(jnp.bfloat16)  102 us
    all_gather x3, waiting for transfers between devices, block_product(): lax.all_gather(matrix, 'col', axis=2, tiled=True)  62.4 us
    all_to_all x1, blocking collectives, on_device(): lax.all_to_all(partial_loads, 'col', split_axis=1, concat_axis=2, tiled=T...  54.4 us
    reduce_scatter x1, waiting for transfers between devices, on_device(): lax.psum_scatter(partial_terms, 'col', scatter_dimension=2, tiled=True)  48.7 us
    while x52, local copies, waits for them, and re-layouts  44.6 us
    add x13, other arithmetic, add_block(): return running + jnp.stack([real_part, imag_part])  15.2 us
  transfers between devices with their start and end apart: 7, of which 7 were waited for; matrix products, arithmetic and copies ran while one was open for 2% of the time, Pallas kernels for 0%

commit v1 on v0

v1 whole, which is shorter than its diff:
```python
import functools

import jax
import jax.numpy as jnp
from jax import lax
from jax.experimental import pallas as pl
from jax.experimental.pallas import tpu as pltpu
from jax.sharding import PartitionSpec as P

PATCHES = 4096
ROWS = 16
COLS = 8
BF16 = jnp.bfloat16
F32 = jnp.float32
PARAMS = pltpu.CompilerParams(vmem_limit_bytes=48 * 2**20)


def weighted_onehot(ids, weights, first, count):
    patch = lax.broadcasted_iota(jnp.int32, (count, ids.shape[1]), 0)
    return jnp.where(patch == ids - first, weights, jnp.zeros((), BF16))


def old_loads_kernel(ids_ref, weights_ref, earlier_ref, out_ref, side, *, tile, chunk):
    step = pl.program_id(0)

    @pl.when(step == 0)
    def _():
        side[:, :128] = earlier_ref[0]
        side[:, 128:] = earlier_ref[1]

    total = jnp.zeros((tile, 256), F32)
    for start in range(0, side.shape[0], chunk):
        panels = slice(start, start + chunk)
        onehot = weighted_onehot(ids_ref[:, panels], weights_ref[:, panels], step * tile, tile)
        total += jnp.dot(onehot, side[panels], preferred_element_type=F32)
    for block in range(tile // 256):
        rows = slice(block * 256, (block + 1) * 256)
        out_ref[block, :256] = total[rows, :128].astype(BF16)
        out_ref[block, 256:] = total[rows, 128:].astype(BF16)


def old_loads(ids, weights, earlier):
    panels = earlier.shape[1]
    tile = 1024
    whole = lambda step: (0, 0)
    return pl.pallas_call(
        functools.partial(old_loads_kernel, tile=tile, chunk=512),
        out_shape=jax.ShapeDtypeStruct((ROWS, 512, 128), BF16),
        grid=(PATCHES // tile,),
        in_specs=[
            pl.BlockSpec((1, panels), whole),
            pl.BlockSpec((1, panels), whole),
            pl.BlockSpec((2, panels, 128), lambda step: (0, 0, 0)),
        ],
        out_specs=pl.BlockSpec((tile // 256, 512, 128), lambda step: (step, 0, 0)),
        scratch_shapes=[pltpu.VMEM((panels, 256), BF16)],
        compiler_params=PARAMS,
        name="old_loads",
    )(ids, weights, earlier)


def sum_loads_kernel(parts_ref, out_ref):
    total = parts_ref[0].astype(F32)
    for source in range(1, ROWS):
        total += parts_ref[source].astype(F32)
    total = total.astype(BF16)
    for target in range(ROWS):
        out_ref[target] = total


def sum_loads(parts):
    return pl.pallas_call(
        sum_loads_kernel,
        out_shape=jax.ShapeDtypeStruct(parts.shape, BF16),
        compiler_params=PARAMS,
        name="sum_loads",
    )(parts)


def rows_kernel(order_ref, own_matrix_ref, other_matrix_ref, gathered_ref, *rest, pick, subtract, extra):
    rest = list(rest)
    base_ref = rest.pop(0) if subtract else None
    extra_ref = rest.pop(0) if extra else None
    own_ref, copies_ref, side = rest
    for source in range(ROWS):
        rows = slice(source * 128, (source + 1) * 128)
        side[rows, :128] = gathered_ref[source, :128]
        side[rows, 128:] = gathered_ref[source, 128:256]
    real = jnp.zeros((128, 256), F32)
    imag = jnp.zeros((128, 256), F32)
    for core, matrix_ref in enumerate((own_matrix_ref, other_matrix_ref)):
        for hop in range(4):
            block = order_ref[core * 4 + hop]
            part = side[pl.ds(pl.multiple_of(block * 256, 256), 256)]
            real += jnp.dot(matrix_ref[hop, pick, 0], part, preferred_element_type=F32)
            imag += jnp.dot(matrix_ref[hop, pick, 1], part, preferred_element_type=F32)
    out_real = real[:, :128] - imag[:, 128:]
    out_imag = real[:, 128:] + imag[:, :128]
    if subtract:
        out_real = base_ref[0].astype(F32) - out_real
        out_imag = base_ref[1].astype(F32) - out_imag
    out_real = out_real.astype(BF16)
    out_imag = out_imag.astype(BF16)
    own_ref[0] = out_real
    own_ref[1] = out_imag
    for target in range(ROWS):
        copies_ref[target, :128] = out_real
        copies_ref[target, 128:256] = out_imag
        if extra:
            copies_ref[target, 256:] = extra_ref[...]


def rows_product(name, order, matrix, pick, gathered, base=None, extra=None):
    vmem = pl.BlockSpec(memory_space=pltpu.VMEM)
    operands = [*matrix, gathered]
    operands += [value for value in (base, extra) if value is not None]
    height = 256 if extra is None else 256 + extra.shape[0]
    return pl.pallas_call(
        functools.partial(
            rows_kernel, pick=pick, subtract=base is not None, extra=extra is not None
        ),
        out_shape=(
            jax.ShapeDtypeStruct((2, 128, 128), BF16),
            jax.ShapeDtypeStruct((ROWS, height, 128), BF16),
        ),
        in_specs=[pl.BlockSpec(memory_space=pltpu.SMEM)] + [vmem] * len(operands),
        out_specs=(vmem, vmem),
        scratch_shapes=[pltpu.VMEM((2048, 256), BF16)],
        compiler_params=PARAMS,
        name=name,
    )(order, *operands)


def read_panels(gathered_ref, notes_ref, block, side, ids, weights):
    for source in range(ROWS):
        rows = slice(source * 128, (source + 1) * 128)
        side[rows, :128] = gathered_ref[source, :128]
        side[rows, 128:] = gathered_ref[source, 128:256]
        notes = notes_ref[source, 256:].astype(F32)
        high, low, weight = (notes[block * 3 + k : block * 3 + k + 1] for k in range(3))
        ids[:, rows] = (high * 64.0 + low).astype(jnp.int32)
        weights[:, rows] = weight


def panel_loads(side, ids, weights, first, tile, chunk):
    total = jnp.zeros((tile, 256), F32)
    for start in range(0, 2048, chunk):
        panels = slice(start, start + chunk)
        onehot = weighted_onehot(ids[:, panels], weights[:, panels].astype(BF16), first, tile)
        total += jnp.dot(onehot, side[panels], preferred_element_type=F32)
    return total


def first_loads_kernel(old_ref, gathered_ref, out_ref, side, ids, weights, *, tile, chunk):
    step = pl.program_id(0)

    @pl.when(step == 0)
    def _():
        read_panels(gathered_ref, gathered_ref, 0, side, ids, weights)

    total = panel_loads(side, ids, weights, step * tile, tile, chunk)
    for block in range(tile // 256):
        rows = slice(block * 256, (block + 1) * 256)
        out_ref[rows, :128] = total[rows, :128] + old_ref[block, :256].astype(F32)
        out_ref[rows, 128:] = total[rows, 128:] + old_ref[block, 256:].astype(F32)


def first_loads(old, gathered):
    tile = 1024
    return pl.pallas_call(
        functools.partial(first_loads_kernel, tile=tile, chunk=512),
        out_shape=jax.ShapeDtypeStruct((PATCHES, 256), F32),
        grid=(PATCHES // tile,),
        in_specs=[
            pl.BlockSpec((tile // 256, 512, 128), lambda step: (step, 0, 0)),
            pl.BlockSpec(gathered.shape, lambda step: (0, 0, 0)),
        ],
        out_specs=pl.BlockSpec((tile, 256), lambda step: (step, 0)),
        scratch_shapes=[
            pltpu.VMEM((2048, 256), BF16),
            pltpu.VMEM((1, 2048), jnp.int32),
            pltpu.VMEM((1, 2048), F32),
        ],
        compiler_params=PARAMS,
        name="first_loads",
    )(old, gathered)


def stress_kernel(order_ref, loads_ref, notes_ref, gathered_ref, *rest, tile, chunk):
    maps = rest[:COLS]
    out_ref, held, loads, side, ids, weights, sems = rest[COLS:]
    copies = [
        pltpu.make_async_copy(maps[k], held.at[k], sems.at[k]) for k in range(COLS)
    ]
    for copy in copies:
        copy.start()
    read_panels(gathered_ref, notes_ref, 1, side, ids, weights)
    for first in range(0, PATCHES, tile):
        rows = slice(first, first + tile)
        total = loads_ref[rows] + panel_loads(side, ids, weights, first, tile, chunk)
        loads[rows] = total.astype(BF16)
    for copy in copies:
        copy.wait()
    for first in range(0, 1024, 256):
        rows = slice(first, first + 256)
        real = jnp.zeros((256, 256), F32)
        imag = jnp.zeros((256, 256), F32)
        for k in range(COLS):
            part = loads[pl.ds(pl.multiple_of(order_ref[k] * 512, 512), 512)]
            real += jnp.dot(held[k, 0, rows], part, preferred_element_type=F32)
            imag += jnp.dot(held[k, 1, rows], part, preferred_element_type=F32)
        out_ref[0, rows] = (real[:, :128] - imag[:, 128:]).astype(BF16)
        out_ref[1, rows] = (real[:, 128:] + imag[:, :128]).astype(BF16)


def stress(order, loads, notes, gathered, maps):
    vmem = pl.BlockSpec(memory_space=pltpu.VMEM)
    return pl.pallas_call(
        functools.partial(stress_kernel, tile=1024, chunk=512),
        out_shape=jax.ShapeDtypeStruct((2, 1024, 128), BF16),
        in_specs=[pl.BlockSpec(memory_space=pltpu.SMEM)]
        + [vmem] * 3
        + [pl.BlockSpec(memory_space=pl.ANY)] * COLS,
        out_specs=vmem,
        scratch_shapes=[
            pltpu.VMEM((COLS, 2, 1024, 512), BF16),
            pltpu.VMEM((PATCHES, 256), BF16),
            pltpu.VMEM((2048, 256), BF16),
            pltpu.VMEM((1, 2048), jnp.int32),
            pltpu.VMEM((1, 2048), F32),
            pltpu.SemaphoreType.DMA((COLS,)),
        ],
        compiler_params=PARAMS,
        name="stress",
    )(order, loads, notes, gathered, *maps)


def from_chip(value, hop):
    pairs = [(i, (i // 2 + hop) % 4 * 2 + i % 2) for i in range(COLS)]
    return lax.ppermute(value, "col", pairs)


def other_core(value):
    return lax.ppermute(value, "col", [(i, i ^ 1) for i in range(COLS)])


def all_columns(matrix):
    own = jnp.stack([matrix] + [from_chip(matrix, hop) for hop in (1, 2, 3)])
    return own, other_core(own)


def to_rows(copies):
    return lax.all_to_all(copies, "row", 0, 0, tiled=True)


def on_device(
    rhs_first,
    rhs_last,
    inv_first,
    coupling,
    inv_last,
    earlier,
    patch_old,
    weight_old,
    patch_new,
    weight_new,
    stress_map,
):
    col = lax.axis_index("col")
    chips = [(col // 2 - hop) % 4 for hop in range(4)]
    core = col % 2
    order = jnp.stack(
        [chip * 2 + core for chip in chips] + [chip * 2 + 1 - core for chip in chips]
    ).astype(jnp.int32)

    first_all = all_columns(inv_first[None])
    later_all = all_columns(jnp.stack([coupling, inv_last]))
    own_core = [stress_map] + [from_chip(stress_map, hop) for hop in (1, 2, 3)]
    maps = own_core + [other_core(value) for value in own_core]

    rhs_all = to_rows(jnp.broadcast_to(rhs_first.reshape(1, 256, 128), (ROWS, 256, 128)))
    old_parts = to_rows(old_loads(patch_old[None], weight_old[None], earlier))

    notes = jnp.stack(
        [
            value
            for block in range(2)
            for value in (
                (patch_new[block] // 64).astype(BF16),
                (patch_new[block] % 64).astype(BF16),
                weight_new[block],
            )
        ]
    )
    notes = jnp.pad(notes, ((0, 10), (0, 0)))
    x_first, copies = rows_product("first_rows", order, first_all, 0, rhs_all, extra=notes)
    x_first_all = to_rows(copies)
    old_all = to_rows(sum_loads(old_parts))
    _, copies = rows_product("reduced_rows", order, later_all, 0, x_first_all, base=rhs_last)
    reduced_all = to_rows(copies)
    x_last, copies = rows_product("last_rows", order, later_all, 1, reduced_all)
    x_last_all = to_rows(copies)
    loads = first_loads(old_all, x_first_all)
    stress_rao = stress(order, loads, x_first_all, x_last_all, maps)
    return (jnp.stack([x_first, x_last]), stress_rao)


def solution(mesh):
    in_specs = (
        P(None, "row", "col"),
        P(None, "row", "col"),
        P(None, "row", "col"),
        P(None, "row", "col"),
        P(None, "row", "col"),
        P(None, "row", "col"),
        P("row"),
        P("row"),
        P(None, "row"),
        P(None, "row"),
        P(None, "row", "col"),
    )
    out_specs = (P(None, None, "row", "col"), P(None, "row", "col"))
    return jax.shard_map(
        on_device, mesh=mesh, in_specs=in_specs, out_specs=out_specs, check_vma=False
    )
```

time: 552 us -> 214 us (0.39)
  blocking collectives: 157 us -> 0 us
  waiting for transfers between devices: 253 us -> 119 us
  local copies, waits for them, and re-layouts: 63.2 us -> 6.59 us
  starting transfers between devices: 0.27 us -> 46.8 us
  matrix products: 39.7 us -> 0 us
  Pallas kernels: 0 us -> 38.7 us
  other arithmetic: 22.7 us -> 0.95 us
  between operations: 14.4 us -> 1.2 us
    all_gather x6 -> x0, waiting for transfers between devices: 202 us -> none  [the longest x3 140 us: block_product(): gathered = lax.all_gather(vectors, 'row', axis=1, tiled=True)]
    psum x1 -> x0, blocking collectives: 102 us -> none  [on_device(): patch_loads = lax.psum(turned, 'row').astype(jnp.bfloat16)]
    ppermute x0 -> x15, waiting for transfers between devices: none -> 67.3 us  [the longest x9 65.6 us: from_chip(): return lax.ppermute(value, 'col', pairs)]
    all_to_all x1 -> x0, blocking collectives: 54.4 us -> none  [on_device(): lax.all_to_all(partial_loads, 'col', split_axis=1, concat_axis=2, tiled=T...]
    while x53 -> x0, local copies, waits for them, and re-layouts: 52.4 us -> none
    all_to_all x0 -> x6, waiting for transfers between devices: none -> 51.2 us  [to_rows(): return lax.all_to_all(copies, 'row', 0, 0, tiled=True)]
    reduce_scatter x1 -> x0, waiting for transfers between devices: 48.7 us -> none  [on_device(): lax.psum_scatter(partial_terms, 'col', scatter_dimension=2, tiled=True)]
    dot_general x42 -> x0, matrix products: 39.7 us -> none  [the longest x13 9.12 us: add_block(): jnp.dot(onehot_block, block_values[1], preferred_element_type=jnp.float32)]
  transfers between devices with their start and end apart: 7 -> 21, of which waited for: 7 -> 10; matrix products, arithmetic and copies ran while one was open for 2% -> 1% of each run, Pallas kernels for 0% -> 10%
where the time goes in v1:
time: 214 us; the launch traced here: 213 us
  waiting for transfers between devices  119 us (56%)
  starting transfers between devices  46.8 us (22%)
  Pallas kernels  38.7 us (18%)
  local copies, waits for them, and re-layouts  6.59 us (3%)
    ppermute x9, waiting for transfers between devices, from_chip(): return lax.ppermute(value, 'col', pairs)  65.6 us
    all_to_all x6, waiting for transfers between devices, to_rows(): return lax.all_to_all(copies, 'row', 0, 0, tiled=True)  51.2 us
    all_to_all x6, starting transfers between devices, to_rows(): return lax.all_to_all(copies, 'row', 0, 0, tiled=True)  31.7 us
    pallas_call x1, Pallas kernels, stress(): pl.pallas_call(functools.partial(stress_kernel, tile=1024, chunk=512), ou...  15.4 us
    ppermute x9, starting transfers between devices, from_chip(): return lax.ppermute(value, 'col', pairs)  14.4 us
    pallas_call x1, Pallas kernels, old_loads(): pl.pallas_call(functools.partial(old_loads_kernel, tile=tile, chunk=512),...  8.33 us
    pallas_call x1, Pallas kernels, first_loads(): pl.pallas_call(functools.partial(first_loads_kernel, tile=tile, chunk=512...  7.46 us
    pallas_call x3, Pallas kernels, rows_product(): pl.pallas_call(functools.partial(rows_kernel, pick=pick, subtract=base is...  5.55 us
  transfers between devices with their start and end apart: 21, of which 10 were waited for; matrix products, arithmetic and copies ran while one was open for 1% of the time, Pallas kernels for 10%

profile of v1, /device:TPU:0, one launch (start us, length us, event | category | flops | bytes accessed | tf_op | source)
XLA Modules:
  0.0 212.8 jit_solution(14206823202911300564)
XLA Ops:
  0.6 0.0 copy-start.9
  0.6 0.0 copy-start.12
  0.7 3.2 %collective-permute-start.2 = (bf16[1,2,128,256]{3,2,1,0:T(8,128)(2,1)}, bf16[1,2,128,256]{3,2,1,0:T(8,128)(2,1)S(1)}, u32[]{:S(2)}, u32[]{:S(2)}) collective-permute-start(bf16[1,2,128,256]{3,2,1,0:T(8,128)(2,1)} %bitcast.32), channel_id=1, source_target_pairs={{0,6},{1,7},{2,0},{3,1},{4,2},{5,3},{6,4},{7,5},{8,14},{9,15},{10,... | collective-permute-start | bytes 393224 | tf_op jit(solution)/shard_map/ppermute | solution.py:240
  3.8 0.6 collective-permute-start.1
  4.4 1.0 collective-permute-start
  5.4 2.1 broadcast_in_dim.18
  7.5 7.9 %all-to-all-start = ((bf16[16,256,128]{2,1,0:T(8,128)(2,1)}), bf16[16,256,128]{2,1,0:T(8,128)(2,1)S(1)}, u32[]{:S(2)}, u32[]{:S(2)}) async-start(bf16[16,256,128]{2,1,0:T(8,128)(2,1)} %broadcast_in_dim.18), calls=%async_computation | async-start | bytes 2097152 | tf_op jit(solution)/shard_map/all_to_all | solution.py:253
  15.4 0.0 collective-permute-done.2
  15.4 0.0 collective-permute-done.1
  15.4 0.0 collective-permute-done
  15.4 0.1 pad_maximum_fusion.1.own_matrix_ref
  15.5 0.1 collective-permute-start.3
  15.6 0.0 copy-done.11
  15.8 0.1 stack.87.order_ref
  15.9 0.0 copy-start.6
  15.9 1.7 collective-permute-done.3.other_matrix_ref
  17.6 14.1 %all-to-all-done.gathered_ref = bf16[16,256,128]{2,1,0:T(8,128)(2,1)S(1)} async-done(((bf16[16,256,128]{2,1,0:T(8,128)(2,1)}), bf16[16,256,128]{2,1,0:T(8,128)(2,1)S(1)}, u32[]{:S(2)}, u32[]{:S(2)}) %all-to-all-start) | async-done | bytes 1048608 | tf_op jit(solution)/shard_map/all_to_all | solution.py:253
  31.7 1.7 first_rows.1
  33.4 1.0 copy-done.2
  34.4 3.7 %all-to-all-start.1 = ((bf16[16,272,128]{2,1,0:T(8,128)(2,1)}), bf16[16,272,128]{2,1,0:T(8,128)(2,1)S(1)}, u32[]{:S(2)}, u32[]{:S(2)}) async-start(bf16[16,272,128]{2,1,0:T(8,128)(2,1)} %copy-done.2), calls=%async_computation.1 | async-start | bytes 2228224 | tf_op jit(solution)/shard_map/all_to_all | solution.py:253
  38.2 0.0 copy-done.1
  38.2 8.3 %old_loads.1 = bf16[16,512,128]{2,1,0:T(8,128)(2,1)} custom-call(s32[1,3072]{1,0:T(1,128)S(1)} %bitcast.26, bf16[1,3072]{1,0:T(2,128)(2,1)S(1)} %broadcast_in_dim.20.weights_ref, bf16[2,3072,128]{2,1,0:T(8,128)(2,1)S(1)} %copy-done.1), custom_call_target="tpu_custom_call" | custom-call | tf_op jit(solution)/shard_map/old_loads/pallas_call | solution.py:46
  46.5 7.7 %all-to-all-done.1.gathered_ref.notes_ref = bf16[16,272,128]{2,1,0:T(8,128)(2,1)S(1)} async-done(((bf16[16,272,128]{2,1,0:T(8,128)(2,1)}), bf16[16,272,128]{2,1,0:T(8,128)(2,1)S(1)}, u32[]{:S(2)}, u32[]{:S(2)}) %all-to-all-start.1) | async-done | bytes 1114144 | tf_op jit(solution)/shard_map/all_to_all | solution.py:253
  54.3 4.4 %all-to-all-start.3 = ((bf16[16,512,128]{2,1,0:T(8,128)(2,1)}), bf16[16,512,128]{2,1,0:T(8,128)(2,1)}, u32[]{:S(2)}, u32[]{:S(2)}) async-start(bf16[16,512,128]{2,1,0:T(8,128)(2,1)} %old_loads.1), calls=%async_computation.3 | async-start | bytes 4194304 | tf_op jit(solution)/shard_map/all_to_all | solution.py:253
  58.7 0.0 copy-start.5
  58.8 2.3 %collective-permute-start.5 = (bf16[2,2,128,256]{3,2,1,0:T(8,128)(2,1)S(1)}, bf16[2,2,128,256]{3,2,1,0:T(8,128)(2,1)S(1)}, u32[]{:S(2)}, u32[]{:S(2)}) collective-permute-start(bf16[2,2,128,256]{3,2,1,0:T(8,128)(2,1)S(1)} %get-tuple-element.17), channel_id=1, source_target_pairs={{0,4},{1,5},{2,6},{3,7},{4,0},{5,1},{6,2},{7,3},{8,12},{9,13},{10,... | collective-permute-start | bytes 786440 | tf_op jit(solution)/shard_map/ppermute | solution.py:240
  61.1 0.9 collective-permute-start.4
  62.0 2.3 %collective-permute-start.6 = (bf16[2,2,128,256]{3,2,1,0:T(8,128)(2,1)S(1)}, bf16[2,2,128,256]{3,2,1,0:T(8,128)(2,1)S(1)}, u32[]{:S(2)}, u32[]{:S(2)}) collective-permute-start(bf16[2,2,128,256]{3,2,1,0:T(8,128)(2,1)S(1)} %get-tuple-element.17), channel_id=1, source_target_pairs={{0,6},{1,7},{2,0},{3,1},{4,2},{5,3},{6,4},{7,5},{8,14},{9,15},{10,... | collective-permute-start | bytes 786440 | tf_op jit(solution)/shard_map/ppermute | solution.py:240
  64.3 4.7 %collective-permute-done.5 = bf16[2,2,128,256]{3,2,1,0:T(8,128)(2,1)S(1)} collective-permute-done((bf16[2,2,128,256]{3,2,1,0:T(8,128)(2,1)S(1)}, bf16[2,2,128,256]{3,2,1,0:T(8,128)(2,1)S(1)}, u32[]{:S(2)}, u32[]{:S(2)}) %collective-permute-start.5) | collective-permute-done | bytes 262176 | tf_op jit(solution)/shard_map/ppermute | solution.py:240
  69.0 2.7 %collective-permute-done.4 = bf16[2,2,128,256]{3,2,1,0:T(8,128)(2,1)S(1)} collective-permute-done((bf16[2,2,128,256]{3,2,1,0:T(8,128)(2,1)S(1)}, bf16[2,2,128,256]{3,2,1,0:T(8,128)(2,1)S(1)}, u32[]{:S(2)}, u32[]{:S(2)}) %collective-permute-start.4) | collective-permute-done | bytes 262176 | tf_op jit(solution)/shard_map/ppermute | solution.py:240
  71.8 0.0 collective-permute-done.6
  71.8 0.1 pad_maximum_fusion.own_matrix_ref
  71.9 0.1 collective-permute-start.7
  72.0 2.4 %collective-permute-start.10 = (bf16[2,1024,512]{2,1,0:T(8,128)(2,1)}, bf16[2,1024,512]{2,1,0:T(8,128)(2,1)}, u32[]{:S(2)}, u32[]{:S(2)}) collective-permute-start(bf16[2,1024,512]{2,1,0:T(8,128)(2,1)} %rest_0_.3), channel_id=1, source_target_pairs={{0,6},{1,7},{2,0},{3,1},{4,2},{5,3},{6,4},{7,5},{8,14},{9,15},{10,... | collective-permute-start | bytes 6291464 | tf_op jit(solution)/shard_map/ppermute | solution.py:240
  74.4 1.7 collective-permute-start.9
  76.1 0.0 collective-permute-start.8
  76.1 0.0 collective-permute-done.7.other_matrix_ref
  76.1 1.9 reduced_rows.1
  78.0 1.0 copy-done.4
  79.0 7.7 %all-to-all-done.3.parts_ref = bf16[16,512,128]{2,1,0:T(8,128)(2,1)} async-done(((bf16[16,512,128]{2,1,0:T(8,128)(2,1)}), bf16[16,512,128]{2,1,0:T(8,128)(2,1)}, u32[]{:S(2)}, u32[]{:S(2)}) %all-to-all-start.3) | async-done | bytes 2097184 | tf_op jit(solution)/shard_map/all_to_all | solution.py:253
  86.6 4.3 %all-to-all-start.2 = ((bf16[16,256,128]{2,1,0:T(8,128)(2,1)}), bf16[16,256,128]{2,1,0:T(8,128)(2,1)}, u32[]{:S(2)}, u32[]{:S(2)}) async-start(bf16[16,256,128]{2,1,0:T(8,128)(2,1)} %copy-done.4), calls=%async_computation.2 | async-start | bytes 2097152 | tf_op jit(solution)/shard_map/all_to_all | solution.py:253
  91.0 1.9 sum_loads.1
  92.9 1.3 copy-done
  94.3 11.4 %all-to-all-done.2.gathered_ref = bf16[16,256,128]{2,1,0:T(8,128)(2,1)} async-done(((bf16[16,256,128]{2,1,0:T(8,128)(2,1)}), bf16[16,256,128]{2,1,0:T(8,128)(2,1)}, u32[]{:S(2)}, u32[]{:S(2)}) %all-to-all-start.2) | async-done | bytes 1048608 | tf_op jit(solution)/shard_map/all_to_all | solution.py:253
  105.6 4.4 %all-to-all-start.4 = ((bf16[16,512,128]{2,1,0:T(8,128)(2,1)}), bf16[16,512,128]{2,1,0:T(8,128)(2,1)}, u32[]{:S(2)}, u32[]{:S(2)}) async-start(bf16[16,512,128]{2,1,0:T(8,128)(2,1)} %copy-done), calls=%async_computation.4 | async-start | bytes 4194304 | tf_op jit(solution)/shard_map/all_to_all | solution.py:253
  110.1 0.1 collective-permute-start.11
  110.2 55.0 %collective-permute-done.10.rest_3_ = bf16[2,1024,512]{2,1,0:T(8,128)(2,1)} collective-permute-done((bf16[2,1024,512]{2,1,0:T(8,128)(2,1)}, bf16[2,1024,512]{2,1,0:T(8,128)(2,1)}, u32[]{:S(2)}, u32[]{:S(2)}) %collective-permute-start.10) | collective-permute-done | bytes 2097184 | tf_op jit(solution)/shard_map/ppermute | solution.py:240
  165.2 0.0 collective-permute-start.14
  165.2 0.0 collective-permute-done.9.rest_2_
  165.2 0.5 collective-permute-start.13
  165.7 3.2 %collective-permute-done.8.rest_1_ = bf16[2,1024,512]{2,1,0:T(8,128)(2,1)} collective-permute-done((bf16[2,1024,512]{2,1,0:T(8,128)(2,1)}, bf16[2,1024,512]{2,1,0:T(8,128)(2,1)}, u32[]{:S(2)}, u32[]{:S(2)}) %collective-permute-start.8) | collective-permute-done | bytes 2097184 | tf_op jit(solution)/shard_map/ppermute | solution.py:240
  168.8 0.0 collective-permute-start.12
  168.9 1.9 last_rows.1
  170.8 1.0 copy-done.3
  171.8 0.0 all-to-all-done.4.old_ref
  171.8 6.9 %all-to-all-start.5 = ((bf16[16,256,128]{2,1,0:T(8,128)(2,1)}), bf16[16,256,128]{2,1,0:T(8,128)(2,1)S(1)}, u32[]{:S(2)}, u32[]{:S(2)}) async-start(bf16[16,256,128]{2,1,0:T(8,128)(2,1)} %copy-done.3), calls=%async_computation.5 | async-start | bytes 2097152 | tf_op jit(solution)/shard_map/all_to_all | solution.py:253
  178.7 0.7 pad_maximum_fusion.3
  179.4 7.5 %first_loads.1.loads_ref = f32[4096,256]{1,0:T(8,128)} custom-call(bf16[16,512,128]{2,1,0:T(8,128)(2,1)} %all-to-all-done.4.old_ref, bf16[16,272,128]{2,1,0:T(8,128)(2,1)S(1)} %all-to-all-done.1.gathered_ref.notes_ref), custom_call_target="tpu_custom_call" | custom-call | tf_op jit(solution)/shard_map/first_loads/pallas_call | solution.py:170
  186.9 0.0 collective-permute-done.11.rest_4_
  186.9 10.3 %all-to-all-done.5.gathered_ref = bf16[16,256,128]{2,1,0:T(8,128)(2,1)S(1)} async-done(((bf16[16,256,128]{2,1,0:T(8,128)(2,1)}), bf16[16,256,128]{2,1,0:T(8,128)(2,1)S(1)}, u32[]{:S(2)}, u32[]{:S(2)}) %all-to-all-start.5) | async-done | bytes 1048608 | tf_op jit(solution)/shard_map/all_to_all | solution.py:253
  197.2 0.0 collective-permute-done.14.rest_7_
  197.2 0.0 collective-permute-done.13.rest_6_
  197.2 0.0 collective-permute-done.12.rest_5_
  197.2 15.4 %stress.1 = bf16[2,1024,128]{2,1,0:T(8,128)(2,1)} custom-call(s32[8]{0:T(128)S(1)} %stack.87.order_ref, f32[4096,256]{1,0:T(8,128)} %first_loads.1.loads_ref, bf16[16,272,128]{2,1,0:T(8,128)(2,1)S(1)} %all-to-all-done.1.gathered_ref.notes_ref, bf16[16,256,128]{2,1,0:T(8,128)(2,1)S(1)} %all-to-all-done.5.gathered_ref, bf16[2,1024,512]{2,1,0:T(8,128)(2,1)} %rest_0_.3, ...), custom_call_target="tpu_custom_call" | custom-call | tf_op jit(solution)/shard_map/stress/pallas_call | solution.py:218
  (24 shorter events, 0.2 us)
Async XLA Ops:
  0.6 14.8 %copy-start.9 = (bf16[2,128,256]{2,1,0:T(8,128)(2,1)S(1)}, bf16[2,128,256]{2,1,0:T(8,128)(2,1)}, u32[]{:S(2)}) copy-start(bf16[2,128,256]{2,1,0:T(8,128)(2,1)} %param.13) | copy-start | bytes 393220
  0.6 14.7 %copy-start.12 = (s32[2,128]{1,0:T(2,128)S(1)}, s32[2,128]{1,0:T(2,128)}, u32[]{:S(2)}) copy-start(s32[2,128]{1,0:T(2,128)} %param.19) | copy-start | bytes 3076
  0.7 14.8 %collective-permute-start.2 = (bf16[1,2,128,256]{3,2,1,0:T(8,128)(2,1)}, bf16[1,2,128,256]{3,2,1,0:T(8,128)(2,1)S(1)}, u32[]{:S(2)}, u32[]{:S(2)}) collective-permute-start(bf16[1,2,128,256]{3,2,1,0:T(8,128)(2,1)} %bitcast.32), channel_id=1, source_target_pairs={{0,6},{1,7},{2,0},{3,1},{4,2},{5,3},{6,4},{7,5},{8,14},{9,15},{10,... | collective-permute-start | bytes 393224 | tf_op jit(solution)/shard_map/ppermute | solution.py:240
  3.8 11.6 %collective-permute-start.1 = (bf16[1,2,128,256]{3,2,1,0:T(8,128)(2,1)}, bf16[1,2,128,256]{3,2,1,0:T(8,128)(2,1)S(1)}, u32[]{:S(2)}, u32[]{:S(2)}) collective-permute-start(bf16[1,2,128,256]{3,2,1,0:T(8,128)(2,1)} %bitcast.33), channel_id=1, source_target_pairs={{0,4},{1,5},{2,6},{3,7},{4,0},{5,1},{6,2},{7,3},{8,12},{9,13},{10,... | collective-permute-start | bytes 393224 | tf_op jit(solution)/shard_map/ppermute | solution.py:240
  4.4 11.0 %collective-permute-start = (bf16[1,2,128,256]{3,2,1,0:T(8,128)(2,1)}, bf16[1,2,128,256]{3,2,1,0:T(8,128)(2,1)S(1)}, u32[]{:S(2)}, u32[]{:S(2)}) collective-permute-start(bf16[1,2,128,256]{3,2,1,0:T(8,128)(2,1)} %bitcast.34), channel_id=1, source_target_pairs={{0,2},{1,3},{2,4},{3,5},{4,6},{5,7},{6,0},{7,1},{8,10},{9,11},{10,... | collective-permute-start | bytes 393224 | tf_op jit(solution)/shard_map/ppermute | solution.py:240
  5.4 10.2 %copy-start.11 = (bf16[2,128]{1,0:T(2,128)(2,1)S(1)}, bf16[2,128]{1,0:T(2,128)(2,1)}, u32[]{:S(2)}) copy-start(bf16[2,128]{1,0:T(2,128)(2,1)} %param.20) | copy-start | bytes 1540
  7.5 24.2 %all-to-all-start = ((bf16[16,256,128]{2,1,0:T(8,128)(2,1)}), bf16[16,256,128]{2,1,0:T(8,128)(2,1)S(1)}, u32[]{:S(2)}, u32[]{:S(2)}) async-start(bf16[16,256,128]{2,1,0:T(8,128)(2,1)} %broadcast_in_dim.18), calls=%async_computation | async-start | bytes 2097152 | tf_op jit(solution)/shard_map/all_to_all | solution.py:253
  15.5 2.1 collective-permute-start.3
  15.9 22.3 %copy-start.10 = (bf16[3072]{0:T(1024)(128)(2,1)S(1)}, bf16[3072]{0:T(1024)(128)(2,1)}, u32[]{:S(2)}) copy-start(bf16[3072]{0:T(1024)(128)(2,1)} %param.18) | copy-start | bytes 18436
  15.9 22.3 %copy-start.1 = (bf16[2,3072,128]{2,1,0:T(8,128)(2,1)S(1)}, bf16[2,3072,128]{2,1,0:T(8,128)(2,1)}, u32[]{:S(2)}) copy-start(bf16[2,3072,128]{2,1,0:T(8,128)(2,1)} %earlier_ref.1) | copy-start | bytes 4718596
  15.9 22.3 %copy-start.6 = (s32[3072]{0:T(1024)S(1)}, s32[3072]{0:T(1024)}, u32[]{:S(2)}) copy-start(s32[3072]{0:T(1024)} %param.17) | copy-start | bytes 36868
  33.4 1.0 copy-start.2
  34.4 19.8 %all-to-all-start.1 = ((bf16[16,272,128]{2,1,0:T(8,128)(2,1)}), bf16[16,272,128]{2,1,0:T(8,128)(2,1)S(1)}, u32[]{:S(2)}, u32[]{:S(2)}) async-start(bf16[16,272,128]{2,1,0:T(8,128)(2,1)} %copy-done.2), calls=%async_computation.1 | async-start | bytes 2228224 | tf_op jit(solution)/shard_map/all_to_all | solution.py:253
  46.5 12.2 %copy-start.7 = (bf16[2,128,256]{2,1,0:T(8,128)(2,1)S(1)}, bf16[2,128,256]{2,1,0:T(8,128)(2,1)}, u32[]{:S(2)}) copy-start(bf16[2,128,256]{2,1,0:T(8,128)(2,1)} %param.15) | copy-start | bytes 393220
  46.5 12.2 %copy-start.8 = (bf16[2,128,256]{2,1,0:T(8,128)(2,1)S(1)}, bf16[2,128,256]{2,1,0:T(8,128)(2,1)}, u32[]{:S(2)}) copy-start(bf16[2,128,256]{2,1,0:T(8,128)(2,1)} %param.14) | copy-start | bytes 393220
  54.3 32.4 %all-to-all-start.3 = ((bf16[16,512,128]{2,1,0:T(8,128)(2,1)}), bf16[16,512,128]{2,1,0:T(8,128)(2,1)}, u32[]{:S(2)}, u32[]{:S(2)}) async-start(bf16[16,512,128]{2,1,0:T(8,128)(2,1)} %old_loads.1), calls=%async_computation.3 | async-start | bytes 4194304 | tf_op jit(solution)/shard_map/all_to_all | solution.py:253
  58.7 17.4 %copy-start.5 = (bf16[2,128,128]{2,1,0:T(8,128)(2,1)S(1)}, bf16[2,128,128]{2,1,0:T(8,128)(2,1)}, u32[]{:S(2)}) copy-start(bf16[2,128,128]{2,1,0:T(8,128)(2,1)} %rest_0_.2) | copy-start | bytes 196612
  58.8 10.3 %collective-permute-start.5 = (bf16[2,2,128,256]{3,2,1,0:T(8,128)(2,1)S(1)}, bf16[2,2,128,256]{3,2,1,0:T(8,128)(2,1)S(1)}, u32[]{:S(2)}, u32[]{:S(2)}) collective-permute-start(bf16[2,2,128,256]{3,2,1,0:T(8,128)(2,1)S(1)} %get-tuple-element.17), channel_id=1, source_target_pairs={{0,4},{1,5},{2,6},{3,7},{4,0},{5,1},{6,2},{7,3},{8,12},{9,13},{10,... | collective-permute-start | bytes 786440 | tf_op jit(solution)/shard_map/ppermute | solution.py:240
  61.1 10.7 %collective-permute-start.4 = (bf16[2,2,128,256]{3,2,1,0:T(8,128)(2,1)S(1)}, bf16[2,2,128,256]{3,2,1,0:T(8,128)(2,1)S(1)}, u32[]{:S(2)}, u32[]{:S(2)}) collective-permute-start(bf16[2,2,128,256]{3,2,1,0:T(8,128)(2,1)S(1)} %get-tuple-element.17), channel_id=1, source_target_pairs={{0,2},{1,3},{2,4},{3,5},{4,6},{5,7},{6,0},{7,1},{8,10},{9,11},{10,... | collective-permute-start | bytes 786440 | tf_op jit(solution)/shard_map/ppermute | solution.py:240
  62.0 9.8 %collective-permute-start.6 = (bf16[2,2,128,256]{3,2,1,0:T(8,128)(2,1)S(1)}, bf16[2,2,128,256]{3,2,1,0:T(8,128)(2,1)S(1)}, u32[]{:S(2)}, u32[]{:S(2)}) collective-permute-start(bf16[2,2,128,256]{3,2,1,0:T(8,128)(2,1)S(1)} %get-tuple-element.17), channel_id=1, source_target_pairs={{0,6},{1,7},{2,0},{3,1},{4,2},{5,3},{6,4},{7,5},{8,14},{9,15},{10,... | collective-permute-start | bytes 786440 | tf_op jit(solution)/shard_map/ppermute | solution.py:240
  71.9 4.1 %collective-permute-start.7 = (bf16[4,2,2,128,256]{4,3,2,1,0:T(8,128)(2,1)S(1)}, bf16[4,2,2,128,256]{4,3,2,1,0:T(8,128)(2,1)S(1)}, u32[]{:S(2)}, u32[]{:S(2)}) collective-permute-start(bf16[4,2,2,128,256]{4,3,2,1,0:T(8,128)(2,1)S(1)} %pad_maximum_fusion.own_matrix_ref), channel_id=1, source_target_pairs={{0,1},{1,0},{2,3},{3,2},{4,5},{5,4},{6,7},{7,6},{8,9},{9,8},{10,11... | collective-permute-start | bytes 3145736 | tf_op jit(solution)/shard_map/ppermute | solution.py:244
  72.0 93.1 %collective-permute-start.10 = (bf16[2,1024,512]{2,1,0:T(8,128)(2,1)}, bf16[2,1024,512]{2,1,0:T(8,128)(2,1)}, u32[]{:S(2)}, u32[]{:S(2)}) collective-permute-start(bf16[2,1024,512]{2,1,0:T(8,128)(2,1)} %rest_0_.3), channel_id=1, source_target_pairs={{0,6},{1,7},{2,0},{3,1},{4,2},{5,3},{6,4},{7,5},{8,14},{9,15},{10,... | collective-permute-start | bytes 6291464 | tf_op jit(solution)/shard_map/ppermute | solution.py:240
  74.4 90.8 %collective-permute-start.9 = (bf16[2,1024,512]{2,1,0:T(8,128)(2,1)}, bf16[2,1024,512]{2,1,0:T(8,128)(2,1)}, u32[]{:S(2)}, u32[]{:S(2)}) collective-permute-start(bf16[2,1024,512]{2,1,0:T(8,128)(2,1)} %rest_0_.3), channel_id=1, source_target_pairs={{0,4},{1,5},{2,6},{3,7},{4,0},{5,1},{6,2},{7,3},{8,12},{9,13},{10,... | collective-permute-start | bytes 6291464 | tf_op jit(solution)/shard_map/ppermute | solution.py:240
  76.1 92.8 %collective-permute-start.8 = (bf16[2,1024,512]{2,1,0:T(8,128)(2,1)}, bf16[2,1024,512]{2,1,0:T(8,128)(2,1)}, u32[]{:S(2)}, u32[]{:S(2)}) collective-permute-start(bf16[2,1024,512]{2,1,0:T(8,128)(2,1)} %rest_0_.3), channel_id=1, source_target_pairs={{0,2},{1,3},{2,4},{3,5},{4,6},{5,7},{6,0},{7,1},{8,10},{9,11},{10,... | collective-permute-start | bytes 6291464 | tf_op jit(solution)/shard_map/ppermute | solution.py:240
  78.0 1.0 copy-start.4
  86.6 19.0 %all-to-all-start.2 = ((bf16[16,256,128]{2,1,0:T(8,128)(2,1)}), bf16[16,256,128]{2,1,0:T(8,128)(2,1)}, u32[]{:S(2)}, u32[]{:S(2)}) async-start(bf16[16,256,128]{2,1,0:T(8,128)(2,1)} %copy-done.4), calls=%async_computation.2 | async-start | bytes 2097152 | tf_op jit(solution)/shard_map/all_to_all | solution.py:253
  92.9 1.4 copy-start
  105.6 66.2 %all-to-all-start.4 = ((bf16[16,512,128]{2,1,0:T(8,128)(2,1)}), bf16[16,512,128]{2,1,0:T(8,128)(2,1)}, u32[]{:S(2)}, u32[]{:S(2)}) async-start(bf16[16,512,128]{2,1,0:T(8,128)(2,1)} %copy-done), calls=%async_computation.4 | async-start | bytes 4194304 | tf_op jit(solution)/shard_map/all_to_all | solution.py:253
  110.1 76.8 %collective-permute-start.11 = (bf16[2,1024,512]{2,1,0:T(8,128)(2,1)}, bf16[2,1024,512]{2,1,0:T(8,128)(2,1)}, u32[]{:S(2)}, u32[]{:S(2)}) collective-permute-start(bf16[2,1024,512]{2,1,0:T(8,128)(2,1)} %rest_0_.3), channel_id=1, source_target_pairs={{0,1},{1,0},{2,3},{3,2},{4,5},{5,4},{6,7},{7,6},{8,9},{9,8},{10,11... | collective-permute-start | bytes 6291464 | tf_op jit(solution)/shard_map/ppermute | solution.py:244
  165.2 32.0 %collective-permute-start.14 = (bf16[2,1024,512]{2,1,0:T(8,128)(2,1)}, bf16[2,1024,512]{2,1,0:T(8,128)(2,1)}, u32[]{:S(2)}, u32[]{:S(2)}) collective-permute-start(bf16[2,1024,512]{2,1,0:T(8,128)(2,1)} %collective-permute-done.10.rest_3_), channel_id=1, source_target_pairs={{0,1},{1,0},{2,3},{3,2},{4,5},{5,4},{6,7},{7,6},{8,9},{9,8},{10,11... | collective-permute-start | bytes 6291464 | tf_op jit(solution)/shard_map/ppermute | solution.py:244
  165.2 32.0 %collective-permute-start.13 = (bf16[2,1024,512]{2,1,0:T(8,128)(2,1)}, bf16[2,1024,512]{2,1,0:T(8,128)(2,1)}, u32[]{:S(2)}, u32[]{:S(2)}) collective-permute-start(bf16[2,1024,512]{2,1,0:T(8,128)(2,1)} %collective-permute-done.9.rest_2_), channel_id=1, source_target_pairs={{0,1},{1,0},{2,3},{3,2},{4,5},{5,4},{6,7},{7,6},{8,9},{9,8},{10,11... | collective-permute-start | bytes 6291464 | tf_op jit(solution)/shard_map/ppermute | solution.py:244
  168.8 28.4 %collective-permute-start.12 = (bf16[2,1024,512]{2,1,0:T(8,128)(2,1)}, bf16[2,1024,512]{2,1,0:T(8,128)(2,1)}, u32[]{:S(2)}, u32[]{:S(2)}) collective-permute-start(bf16[2,1024,512]{2,1,0:T(8,128)(2,1)} %collective-permute-done.8.rest_1_), channel_id=1, source_target_pairs={{0,1},{1,0},{2,3},{3,2},{4,5},{5,4},{6,7},{7,6},{8,9},{9,8},{10,11... | collective-permute-start | bytes 6291464 | tf_op jit(solution)/shard_map/ppermute | solution.py:244
  170.8 1.0 copy-start.3
  171.8 25.4 %all-to-all-start.5 = ((bf16[16,256,128]{2,1,0:T(8,128)(2,1)}), bf16[16,256,128]{2,1,0:T(8,128)(2,1)S(1)}, u32[]{:S(2)}, u32[]{:S(2)}) async-start(bf16[16,256,128]{2,1,0:T(8,128)(2,1)} %copy-done.3), calls=%async_computation.5 | async-start | bytes 2097152 | tf_op jit(solution)/shard_map/all_to_all | solution.py:253

commit v2 on v0

v2 whole, which is shorter than its diff:
```python
import functools

import jax
import jax.numpy as jnp
from jax import lax
from jax.experimental import pallas as pl
from jax.experimental.pallas import tpu as pltpu
from jax.sharding import PartitionSpec as P

PATCHES = 4096
ROWS = 16
COLS = 8
BF16 = jnp.bfloat16
F32 = jnp.float32
COST = pl.CostEstimate(flops=30_000_000_000, bytes_accessed=1000, transcendentals=0)
PARAMS = pltpu.CompilerParams(vmem_limit_bytes=20 * 2**20)


def weighted_onehot(ids, weights, first, count):
    patch = lax.broadcasted_iota(jnp.int32, (count, ids.shape[1]), 0)
    return jnp.where(patch == ids - first, weights, jnp.zeros((), BF16))


def old_loads_kernel(place_ref, ids_ref, weights_ref, earlier_ref, *rest, chunk):
    outs, side = rest[:4], rest[4]
    side[:, :128] = earlier_ref[0]
    side[:, 128:] = earlier_ref[1]
    ids = ids_ref[...]
    x, z = ids >> 10, (ids >> 8) & 3
    major = x + place_ref[2] * (z - x)
    minor = z + place_ref[2] * (x - z)
    labels = ((minor - place_ref[1]) & 3) * 1024 + major * 256 + (ids & 255)
    for k in range(4):
        total = jnp.zeros((1024, 256), F32)
        for start in range(0, side.shape[0], chunk):
            panels = slice(start, start + chunk)
            onehot = weighted_onehot(labels[:, panels], weights_ref[:, panels], k * 1024, 1024)
            total += jnp.dot(onehot, side[panels], preferred_element_type=F32)
        for block in range(4):
            rows = slice(block * 256, (block + 1) * 256)
            outs[k][block, :256] = total[rows, :128].astype(BF16)
            outs[k][block, 256:] = total[rows, 128:].astype(BF16)


def old_loads(place, ids, weights, earlier):
    panels = earlier.shape[1]
    vmem = pl.BlockSpec(memory_space=pltpu.VMEM)
    return pl.pallas_call(
        functools.partial(old_loads_kernel, chunk=512),
        out_shape=[jax.ShapeDtypeStruct((4, 512, 128), BF16)] * 4,
        in_specs=[pl.BlockSpec(memory_space=pltpu.SMEM)] + [vmem] * 3,
        out_specs=[vmem] * 4,
        scratch_shapes=[pltpu.VMEM((panels, 256), BF16)],
        compiler_params=PARAMS,
        name="old_loads",
    )(place, ids, weights, earlier)


def sum_loads_kernel(place_ref, *refs):
    parts, outs = refs[:4], refs[5:]
    for j in range(4):
        block = (place_ref[0] + j) % 4
        total = parts[0][block].astype(F32)
        for part in parts[1:]:
            total += part[block].astype(F32)
        outs[j][...] = total.astype(BF16)


def sum_loads(place, parts, tie):
    vmem = pl.BlockSpec(memory_space=pltpu.VMEM)
    return pl.pallas_call(
        sum_loads_kernel,
        out_shape=[jax.ShapeDtypeStruct((512, 128), BF16)] * 4,
        in_specs=[pl.BlockSpec(memory_space=pltpu.SMEM)]
        + [vmem] * 4
        + [pl.BlockSpec(memory_space=pl.ANY)],
        out_specs=[vmem] * 4,
        compiler_params=PARAMS,
        cost_estimate=COST,
        name="sum_loads",
    )(place, *parts, tie)


def add_loads_kernel(a_ref, b_ref, c_ref, d_ref, out_ref):
    total = a_ref[...].astype(F32) + b_ref[...].astype(F32)
    total += c_ref[...].astype(F32) + d_ref[...].astype(F32)
    out_ref[...] = total.astype(BF16)


def add_loads(parts):
    vmem = pl.BlockSpec(memory_space=pltpu.VMEM)
    return pl.pallas_call(
        add_loads_kernel,
        out_shape=jax.ShapeDtypeStruct((512, 128), BF16),
        in_specs=[vmem] * 4,
        out_specs=vmem,
        compiler_params=PARAMS,
        name="add_loads",
    )(*parts)


def pack_kernel(a_ref, b_ref, c_ref, d_ref, tie_ref, out_ref):
    for k, value_ref in enumerate((a_ref, b_ref, c_ref, d_ref)):
        out_ref[k] = value_ref[...]


def pack_loads(values, tie):
    vmem = pl.BlockSpec(memory_space=pltpu.VMEM)
    return pl.pallas_call(
        pack_kernel,
        out_shape=jax.ShapeDtypeStruct((4, *values[0].shape), BF16),
        in_specs=[vmem] * 4 + [pl.BlockSpec(memory_space=pl.ANY)],
        out_specs=vmem,
        compiler_params=PARAMS,
        cost_estimate=COST,
        name="pack_loads",
    )(*values, tie)


def send_copies(source, copies_ref, sems):
    copies = [
        pltpu.make_async_copy(source, copies_ref.at[k], sems.at[k]) for k in range(ROWS)
    ]
    for copy in copies:
        copy.start()
    for copy in copies:
        copy.wait()


def rows_kernel(factors_ref, gathered_ref, *rest, pick, base, extra, ties):
    rest = list(rest)
    base_ref = rest.pop(0) if base else None
    ids_ref, weights_ref = (rest.pop(0), rest.pop(0)) if extra else (None, None)
    out_ref, copies_ref, factor, side, send, notes, factor_sem, sems = rest[ties:]
    factor_copy = pltpu.make_async_copy(factors_ref.at[:, pick], factor, factor_sem)
    factor_copy.start()
    read_panels(gathered_ref, side)
    real = jnp.zeros((128, 256), F32)
    imag = jnp.zeros((128, 256), F32)
    factor_copy.wait()
    for block in range(COLS):
        part = side[block * 256 : (block + 1) * 256]
        real += jnp.dot(factor[block, 0], part, preferred_element_type=F32)
        imag += jnp.dot(factor[block, 1], part, preferred_element_type=F32)
    out_real = real[:, :128] - imag[:, 128:]
    out_imag = real[:, 128:] + imag[:, :128]
    if base:
        out_real = base_ref[0].astype(F32) - out_real
        out_imag = base_ref[1].astype(F32) - out_imag
    out_real = out_real.astype(BF16)
    out_imag = out_imag.astype(BF16)
    out_ref[0] = out_real
    out_ref[1] = out_imag
    send[:128] = out_real
    send[128:256] = out_imag
    if extra:
        notes[...] = jnp.zeros_like(notes)
        ids = ids_ref[...]
        notes[0:2] = (ids >> 6).astype(F32)
        notes[2:4] = (ids & 63).astype(F32)
        notes[4:6] = weights_ref[...].astype(F32)
        send[256:] = notes[...].astype(BF16)
    send_copies(send, copies_ref, sems)


def rows_product(name, factors, pick, gathered, base=None, extra=None, ties=()):
    vmem = pl.BlockSpec(memory_space=pltpu.VMEM)
    hbm = pl.BlockSpec(memory_space=pltpu.HBM)
    operands = [gathered]
    operands += [] if base is None else [base]
    operands += [] if extra is None else extra
    specs = [hbm] + [vmem] * len(operands)
    specs += [pl.BlockSpec(memory_space=pl.ANY)] * len(ties)
    height = 256 if extra is None else 272
    shapes = [jax.ShapeDtypeStruct((2, 128, 128), BF16), pltpu.HBM((ROWS, height, 128), BF16)]
    return pl.pallas_call(
        functools.partial(
            rows_kernel,
            pick=pick,
            base=base is not None,
            extra=extra is not None,
            ties=len(ties),
        ),
        out_shape=shapes,
        in_specs=specs,
        out_specs=[vmem, hbm],
        scratch_shapes=[
            pltpu.VMEM((COLS, 2, 128, 256), BF16),
            pltpu.VMEM((2048, 256), BF16),
            pltpu.VMEM((height, 128), BF16),
            pltpu.VMEM((16, 128), F32),
            pltpu.SemaphoreType.DMA,
            pltpu.SemaphoreType.DMA((ROWS,)),
        ],
        compiler_params=PARAMS,
        cost_estimate=COST,
        name=name,
    )(pltpu.with_memory_space_constraint(factors, pltpu.HBM), *operands, *ties)


def panel_loads(side, ids, weights, first, tile, chunk):
    total = jnp.zeros((tile, 256), F32)
    for start in range(0, 2048, chunk):
        panels = slice(start, start + chunk)
        onehot = weighted_onehot(ids[:, panels], weights[:, panels].astype(BF16), first, tile)
        total += jnp.dot(onehot, side[panels], preferred_element_type=F32)
    return total


def read_panels(gathered_ref, side):
    for source in range(ROWS):
        rows = slice(source * 128, (source + 1) * 128)
        side[rows, :128] = gathered_ref[source, :128]
        side[rows, 128:] = gathered_ref[source, 128:256]


def first_loads_kernel(place_ref, gathered_ref, *rest):
    old_refs = rest[:4]
    out_ref, ids_ref, weights_ref, side, ids, weights, old, total, old_sems, sems = rest[4:]
    old_copies = [
        pltpu.make_async_copy(old_refs[j], old.at[j], old_sems.at[j]) for j in range(4)
    ]
    for copy in old_copies:
        copy.start()
    read_panels(gathered_ref, side)
    for source in range(ROWS):
        rows = slice(source * 128, (source + 1) * 128)
        notes = gathered_ref[source, 256:].astype(F32)
        for block, (to_ids, to_weights) in enumerate(((ids, weights), (ids_ref, weights_ref))):
            high, low, weight = (notes[block + k : block + k + 1] for k in (0, 2, 4))
            to_ids[:, rows] = (high * 64.0 + low).astype(jnp.int32)
            to_weights[:, rows] = weight
    for first in range(0, PATCHES, 1024):
        total[first : first + 1024] = panel_loads(side, ids, weights, first, 1024, 512)
    copies = []
    for j in range(4):
        old_copies[j].wait()
        major = (place_ref[0] - j + 4) % 4
        for k in range(4):
            minor = (place_ref[1] - k + 4) % 4
            block = (major * 4 + minor) + place_ref[2] * 3 * (minor - major)
            rows = pl.ds(pl.multiple_of(block * 256, 256), 256)
            total[rows, :128] += old[j, k, :256].astype(F32)
            total[rows, 128:] += old[j, k, 256:].astype(F32)
            copies.append(
                pltpu.make_async_copy(total.at[rows], out_ref.at[rows], sems.at[j * 4 + k])
            )
            copies[-1].start()
    for copy in copies:
        copy.wait()


def first_loads(place, gathered, old):
    vmem = pl.BlockSpec(memory_space=pltpu.VMEM)
    hbm = pl.BlockSpec(memory_space=pltpu.HBM)
    return pl.pallas_call(
        first_loads_kernel,
        out_shape=(
            pltpu.HBM((PATCHES, 256), F32),
            jax.ShapeDtypeStruct((1, 2048), jnp.int32),
            jax.ShapeDtypeStruct((1, 2048), F32),
        ),
        in_specs=[pl.BlockSpec(memory_space=pltpu.SMEM), vmem]
        + [pl.BlockSpec(memory_space=pl.ANY)] * 4,
        out_specs=(hbm, vmem, vmem),
        scratch_shapes=[
            pltpu.VMEM((2048, 256), BF16),
            pltpu.VMEM((1, 2048), jnp.int32),
            pltpu.VMEM((1, 2048), F32),
            pltpu.VMEM((4, 4, 512, 128), BF16),
            pltpu.VMEM((PATCHES, 256), F32),
            pltpu.SemaphoreType.DMA((4,)),
            pltpu.SemaphoreType.DMA((ROWS,)),
        ],
        compiler_params=PARAMS,
        cost_estimate=COST,
        name="first_loads",
    )(place, gathered, *old)


def all_loads_kernel(
    ids, weights, gathered_ref, first_ref, maps_ref, out_ref, held_ref, side, first, first_sems, sems
):
    first_copies = []
    for part in range(4):
        rows = pl.ds(part * 1024, 1024)
        first_copies.append(
            pltpu.make_async_copy(first_ref.at[rows], first.at[rows], first_sems.at[part])
        )
    copies = [
        pltpu.make_async_copy(maps_ref.at[k], held_ref.at[k], sems.at[k]) for k in range(COLS)
    ]
    for copy in first_copies:
        copy.start()
    read_panels(gathered_ref, side)
    for part in range(4):
        rows = slice(part * 1024, (part + 1) * 1024)
        total = panel_loads(side, ids, weights, part * 1024, 1024, 512)
        first_copies[part].wait()
        out_ref[rows] = (first[rows] + total).astype(BF16)
        if part == 0:
            for copy in copies:
                copy.start()
    for copy in copies:
        copy.wait()


def all_loads(ids, weights, gathered, first, maps):
    vmem = pl.BlockSpec(memory_space=pltpu.VMEM)
    hbm = pl.BlockSpec(memory_space=pltpu.HBM)
    return pl.pallas_call(
        all_loads_kernel,
        out_shape=(pltpu.VMEM((PATCHES, 256), BF16), pltpu.VMEM(maps.shape, BF16)),
        in_specs=[vmem] * 3 + [hbm] * 2,
        out_specs=(vmem, vmem),
        scratch_shapes=[
            pltpu.VMEM((2048, 256), BF16),
            pltpu.VMEM((PATCHES, 256), F32),
            pltpu.SemaphoreType.DMA((4,)),
            pltpu.SemaphoreType.DMA((COLS,)),
        ],
        compiler_params=PARAMS,
        name="all_loads",
    )(
        ids,
        weights,
        gathered,
        pltpu.with_memory_space_constraint(first, pltpu.HBM),
        pltpu.with_memory_space_constraint(maps, pltpu.HBM),
    )


def stress_kernel(loads_ref, maps_ref, out_ref):
    for first in range(0, 1024, 512):
        rows = slice(first, first + 512)
        real = jnp.zeros((512, 256), F32)
        imag = jnp.zeros((512, 256), F32)
        for block in range(COLS):
            part = loads_ref[block * 512 : (block + 1) * 512]
            real += jnp.dot(maps_ref[block, 0, rows], part, preferred_element_type=F32)
            imag += jnp.dot(maps_ref[block, 1, rows], part, preferred_element_type=F32)
        out_ref[0, rows] = (real[:, :128] - imag[:, 128:]).astype(BF16)
        out_ref[1, rows] = (real[:, 128:] + imag[:, :128]).astype(BF16)


def stress(loads, maps):
    vmem = pl.BlockSpec(memory_space=pltpu.VMEM)
    return pl.pallas_call(
        stress_kernel,
        out_shape=jax.ShapeDtypeStruct((2, 1024, 128), BF16),
        in_specs=[vmem] * 2,
        out_specs=vmem,
        compiler_params=PARAMS,
        name="stress",
    )(
        pltpu.with_memory_space_constraint(loads, pltpu.VMEM),
        pltpu.with_memory_space_constraint(maps, pltpu.VMEM),
    )


def along_axis(value, hop, major):
    pairs = []
    for index in range(ROWS * COLS):
        x, z, rest = index // 32, index // 8 % 4, index % 8
        if major == (rest % 2 == 0):
            x = (x + hop) % 4
        else:
            z = (z + hop) % 4
        pairs.append((index, (x * 4 + z) * 8 + rest))
    return lax.ppermute(value, ("row", "col"), pairs)


def to_rows(copies):
    return lax.all_to_all(copies, "row", 0, 0, tiled=True)


def on_device(
    rhs_first,
    rhs_last,
    inv_first,
    coupling,
    inv_last,
    earlier,
    patch_old,
    weight_old,
    patch_new,
    weight_new,
    stress_map,
):
    row = lax.axis_index("row")
    col = lax.axis_index("col")
    core = col % 2
    x, z = row // 4, row % 4
    place = jnp.stack([x + core * (z - x), z + core * (x - z), core]).astype(jnp.int32)

    factors = lax.all_gather(jnp.stack([inv_first, coupling, inv_last]), "col")
    maps = lax.all_gather(stress_map, "col")
    rhs_all = to_rows(jnp.broadcast_to(rhs_first.reshape(1, 256, 128), (ROWS, 256, 128)))
    old = old_loads(place, patch_old[None], weight_old[None], earlier)
    x_first, copies = rows_product(
        "first_rows", factors, 0, rhs_all, extra=[patch_new, weight_new]
    )
    x_first_all = to_rows(copies)
    old = sum_loads(
        place, [old[0]] + [along_axis(old[hop], hop, False) for hop in (1, 2, 3)], x_first
    )
    old = add_loads([old[0]] + [along_axis(old[hop], hop, True) for hop in (1, 2, 3)])
    reduced, copies = rows_product(
        "reduced_rows", factors, 1, x_first_all, base=rhs_last, ties=(old,)
    )
    reduced_all = to_rows(copies)
    old = pack_loads([old] + [along_axis(old, hop, False) for hop in (1, 2, 3)], reduced)
    x_last, copies = rows_product("last_rows", factors, 2, reduced_all, ties=(old,))
    x_last_all = to_rows(copies)
    old = [old] + [along_axis(old, hop, True) for hop in (1, 2, 3)]
    loads, ids, weights = first_loads(place, x_first_all, old)
    stress_rao = stress(*all_loads(ids, weights, x_last_all, loads, maps))
    return (jnp.stack([x_first, x_last]), stress_rao)


def solution(mesh):
    in_specs = (
        P(None, "row", "col"),
        P(None, "row", "col"),
        P(None, "row", "col"),
        P(None, "row", "col"),
        P(None, "row", "col"),
        P(None, "row", "col"),
        P("row"),
        P("row"),
        P(None, "row"),
        P(None, "row"),
        P(None, "row", "col"),
    )
    out_specs = (P(None, None, "row", "col"), P(None, "row", "col"))
    return jax.shard_map(
        on_device, mesh=mesh, in_specs=in_specs, out_specs=out_specs, check_vma=False
    )
```

time: 552 us -> 150 us (0.27)
  waiting for transfers between devices: 253 us -> 40.9 us
  blocking collectives: 157 us -> 0 us
  local copies, waits for them, and re-layouts: 63.2 us -> 1.24 us
  starting transfers between devices: 0.27 us -> 48.6 us
  Pallas kernels: 0 us -> 40.9 us
  matrix products: 39.7 us -> 0 us
  other arithmetic: 22.7 us -> 2.58 us
    all_gather x6 -> x2, waiting for transfers between devices: 202 us -> 8.13 us  [the longest x1 5.42 us: on_device(): maps = lax.all_gather(stress_map, 'col')]
    psum x1 -> x0, blocking collectives: 102 us -> none  [on_device(): patch_loads = lax.psum(turned, 'row').astype(jnp.bfloat16)]
    all_to_all x1 -> x0, blocking collectives: 54.4 us -> none  [on_device(): lax.all_to_all(partial_loads, 'col', split_axis=1, concat_axis=2, tiled=T...]
    while x53 -> x0, local copies, waits for them, and re-layouts: 52.4 us -> none
    reduce_scatter x1 -> x0, waiting for transfers between devices: 48.7 us -> none  [on_device(): lax.psum_scatter(partial_terms, 'col', scatter_dimension=2, tiled=True)]
    pallas_call x0 -> x10, Pallas kernels: none -> 40.9 us  [the longest x1 9.76 us: all_loads(): pl.pallas_call(all_loads_kernel, out_shape=(pltpu.VMEM((PATCHES, 256), BF...]
    dot_general x42 -> x0, matrix products: 39.7 us -> none  [the longest x13 9.12 us: add_block(): jnp.dot(onehot_block, block_values[1], preferred_element_type=jnp.float32)]
    all_to_all x0 -> x4, starting transfers between devices: none -> 27 us  [to_rows(): return lax.all_to_all(copies, 'row', 0, 0, tiled=True)]
  transfers between devices with their start and end apart: 7 -> 18, of which waited for: 7 -> 7; matrix products, arithmetic and copies ran while one was open for 2% -> 1% of each run, Pallas kernels for 0% -> 17%
where the time goes in v2:
time: 150 us; the launch traced here: 149 us
  starting transfers between devices  48.6 us (32%)
  waiting for transfers between devices  40.9 us (27%)
  Pallas kernels  40.9 us (27%)
  between operations  14.3 us (10%)
  other arithmetic  2.58 us (2%)
    all_to_all x4, starting transfers between devices, to_rows(): return lax.all_to_all(copies, 'row', 0, 0, tiled=True)  27 us
    ppermute x12, starting transfers between devices, along_axis(): return lax.ppermute(value, ('row', 'col'), pairs)  21.5 us
    all_to_all x4, waiting for transfers between devices, to_rows(): return lax.all_to_all(copies, 'row', 0, 0, tiled=True)  20.7 us
    ppermute x12, waiting for transfers between devices, along_axis(): return lax.ppermute(value, ('row', 'col'), pairs)  11.4 us
    pallas_call x1, Pallas kernels, all_loads(): pl.pallas_call(all_loads_kernel, out_shape=(pltpu.VMEM((PATCHES, 256), BF...  9.76 us
    pallas_call x3, Pallas kernels, rows_product(): pl.pallas_call(functools.partial(rows_kernel, pick=pick, base=base is not...  8.54 us
    pallas_call x1, Pallas kernels, old_loads(): pl.pallas_call(functools.partial(old_loads_kernel, chunk=512), out_shape=...  8.42 us
    pallas_call x1, Pallas kernels, first_loads(): pl.pallas_call(first_loads_kernel, out_shape=(pltpu.HBM((PATCHES, 256), F...  7.42 us
  transfers between devices with their start and end apart: 18, of which 7 were waited for; matrix products, arithmetic and copies ran while one was open for 1% of the time, Pallas kernels for 17%

profile of v2, /device:TPU:0, one launch (start us, length us, event | category | flops | bytes accessed | tf_op | source)
XLA Modules:
  0.0 148.6 jit_solution(12277722492032066052)
XLA Ops:
  7.2 0.0 copy-start.5
  7.2 0.0 all-gather.5.cloned.1.call-start
  7.2 1.8 %pad_maximum_fusion = bf16[3,2,128,256]{3,2,1,0:T(8,128)(2,1)} fusion(bf16[1,2,128,256]{3,2,1,0:T(8,128)(2,1)} %bitcast.16, bf16[1,2,128,256]{3,2,1,0:T(8,128)(2,1)} %bitcast.17, bf16[1,2,128,256]{3,2,1,0:T(8,128)(2,1)} %bitcast.18), kind=kLoop, calls=%fused_computation | loop fusion | flops 393216 | bytes 786432 | tf_op jit(solution)/shard_map/stack | solution.py:396
  9.1 0.0 all-gather.5.cloned.1.call-update
  9.1 0.0 all-gather.7.cloned.1.call-start
  9.1 0.7 all-gather.7.cloned.1.call-update
  9.8 0.0 copy-start.6
  9.8 0.0 copy-start
  9.9 0.0 copy-start.1
  9.9 0.0 copy-done.5
  9.9 1.2 broadcast_in_dim.14
  11.1 0.0 copy-start.3
  11.1 8.1 %all-to-all-start = ((bf16[16,256,128]{2,1,0:T(8,128)(2,1)}), bf16[16,256,128]{2,1,0:T(8,128)(2,1)S(1)}, u32[]{:S(2)}, u32[]{:S(2)}) async-start(bf16[16,256,128]{2,1,0:T(8,128)(2,1)} %broadcast_in_dim.14), calls=%async_computation | async-start | bytes 2097152 | tf_op jit(solution)/shard_map/all_to_all | solution.py:374
  19.2 0.0 copy-done.6
  19.2 0.1 pad_add_fusion.place_ref
  19.3 0.0 copy-done
  19.3 0.0 copy-done.1
  19.3 8.4 %old_loads.1 = (bf16[4,512,128]{2,1,0:T(8,128)(2,1)S(1)}, bf16[4,512,128]{2,1,0:T(8,128)(2,1)}, bf16[4,512,128]{2,1,0:T(8,128)(2,1)}, bf16[4,512,128]{2,1,0:T(8,128)(2,1)}) custom-call(s32[3]{0:T(128)S(1)} %pad_add_fusion.place_ref, s32[1,3072]{1,0:T(1,128)S(1)} %bitcast.14, bf16[1,3072]{1,0:T(2,128)(2,1)S(1)} %broadcast_in_dim.16.weights_ref, ...), custom_call_target="tpu_custom_call" | custom-call | tf_op jit(solution)/shard_map/old_loads/pallas_call | solution.py:48
  27.7 1.9 %collective-permute-start = (bf16[4,512,128]{2,1,0:T(8,128)(2,1)}, bf16[4,512,128]{2,1,0:T(8,128)(2,1)S(1)}, u32[]{:S(2)}, u32[]{:S(2)}) collective-permute-start(bf16[4,512,128]{2,1,0:T(8,128)(2,1)} %get-tuple-element.24), channel_id=1, source_target_pairs={{0,8},{1,33},{2,10},{3,35},{4,12},{5,37},{6,14},{7,39},{8,16},{9,4... | collective-permute-start | bytes 1572872 | tf_op jit(solution)/shard_map/ppermute | solution.py:370
  29.6 2.7 %collective-permute-start.1 = (bf16[4,512,128]{2,1,0:T(8,128)(2,1)}, bf16[4,512,128]{2,1,0:T(8,128)(2,1)S(1)}, u32[]{:S(2)}, u32[]{:S(2)}) collective-permute-start(bf16[4,512,128]{2,1,0:T(8,128)(2,1)} %get-tuple-element.25), channel_id=1, source_target_pairs={{0,16},{1,65},{2,18},{3,67},{4,20},{5,69},{6,22},{7,71},{8,24},{9,... | collective-permute-start | bytes 1572872 | tf_op jit(solution)/shard_map/ppermute | solution.py:370
  32.3 1.5 collective-permute-start.2
  33.8 3.5 %all-to-all-done.gathered_ref = bf16[16,256,128]{2,1,0:T(8,128)(2,1)S(1)} async-done(((bf16[16,256,128]{2,1,0:T(8,128)(2,1)}), bf16[16,256,128]{2,1,0:T(8,128)(2,1)S(1)}, u32[]{:S(2)}, u32[]{:S(2)}) %all-to-all-start) | async-done | bytes 1048608 | tf_op jit(solution)/shard_map/all_to_all | solution.py:374
  37.3 2.7 %all-gather.5.cloned.1.call-done = bf16[24,2,128,256]{3,2,1,0:T(8,128)(2,1)} async-done(((bf16[3,2,128,256]{3,2,1,0:T(8,128)(2,1)}), bf16[24,2,128,256]{3,2,1,0:T(8,128)(2,1)}) %all-gather.5.cloned.1.call-update) | async-done | bytes 3145744 | tf_op jit(solution)/shard_map/all_gather | solution.py:396
  40.0 0.0 copy-done.3
  40.0 0.0 copy-done.4
  40.0 2.8 %first_rows.1 = (bf16[2,128,128]{2,1,0:T(8,128)(2,1)S(1)}, bf16[16,272,128]{2,1,0:T(8,128)(2,1)}) custom-call(bf16[8,3,2,128,256]{4,3,2,1,0:T(8,128)(2,1)} %bitcast.20, bf16[16,256,128]{2,1,0:T(8,128)(2,1)S(1)} %all-to-all-done.gathered_ref, s32[2,128]{1,0:T(2,128)S(1)} %copy-done.3, bf16[2,128]{1,0:T(2,128)(2,1)S(1)} %copy-done.4), custom_call_target="tpu_custom_call" | custom-call | flops 30000001024 | bytes 1000 | tf_op jit(solution)/shard_map/first_rows/pallas_call | solution.py:176
  42.8 7.0 %all-to-all-start.1 = ((bf16[16,272,128]{2,1,0:T(8,128)(2,1)}), bf16[16,272,128]{2,1,0:T(8,128)(2,1)S(1)}, u32[]{:S(2)}, u32[]{:S(2)}) async-start(bf16[16,272,128]{2,1,0:T(8,128)(2,1)} %get-tuple-element.22), calls=%async_computation.1 | async-start | bytes 2228224 | tf_op jit(solution)/shard_map/all_to_all | solution.py:374
  49.8 0.0 collective-permute-done.refs_1_
  49.8 0.0 collective-permute-done.1.refs_2_
  49.8 0.0 collective-permute-done.2.refs_3_
  49.8 0.0 copy-start.2
  49.8 1.4 sum_loads.1
  51.2 2.0 %collective-permute-start.3 = (bf16[512,128]{1,0:T(8,128)(2,1)S(1)}, bf16[512,128]{1,0:T(8,128)(2,1)S(1)}, u32[]{:S(2)}, u32[]{:S(2)}) collective-permute-start(bf16[512,128]{1,0:T(8,128)(2,1)S(1)} %get-tuple-element.28), channel_id=1, source_target_pairs={{0,32},{1,9},{2,34},{3,11},{4,36},{5,13},{6,38},{7,15},{8,40},{9,1... | collective-permute-start | bytes 393224 | tf_op jit(solution)/shard_map/ppermute | solution.py:370
  53.2 2.7 %collective-permute-start.4 = (bf16[512,128]{1,0:T(8,128)(2,1)S(1)}, bf16[512,128]{1,0:T(8,128)(2,1)S(1)}, u32[]{:S(2)}, u32[]{:S(2)}) collective-permute-start(bf16[512,128]{1,0:T(8,128)(2,1)S(1)} %get-tuple-element.29), channel_id=1, source_target_pairs={{0,64},{1,17},{2,66},{3,19},{4,68},{5,21},{6,70},{7,23},{8,72},{9,... | collective-permute-start | bytes 393224 | tf_op jit(solution)/shard_map/ppermute | solution.py:370
  55.9 1.5 collective-permute-start.5
  57.4 9.6 %collective-permute-done.3.b_ref = bf16[512,128]{1,0:T(8,128)(2,1)S(1)} collective-permute-done((bf16[512,128]{1,0:T(8,128)(2,1)S(1)}, bf16[512,128]{1,0:T(8,128)(2,1)S(1)}, u32[]{:S(2)}, u32[]{:S(2)}) %collective-permute-start.3) | collective-permute-done | bytes 131104 | tf_op jit(solution)/shard_map/ppermute | solution.py:370
  67.0 1.7 %collective-permute-done.4.c_ref = bf16[512,128]{1,0:T(8,128)(2,1)S(1)} collective-permute-done((bf16[512,128]{1,0:T(8,128)(2,1)S(1)}, bf16[512,128]{1,0:T(8,128)(2,1)S(1)}, u32[]{:S(2)}, u32[]{:S(2)}) %collective-permute-start.4) | collective-permute-done | bytes 131104 | tf_op jit(solution)/shard_map/ppermute | solution.py:370
  68.7 0.0 collective-permute-done.5.d_ref
  68.7 0.1 add_loads.1.rest_1_.a_ref
  68.8 2.7 %collective-permute-start.8 = (bf16[512,128]{1,0:T(8,128)(2,1)S(1)}, bf16[512,128]{1,0:T(8,128)(2,1)S(1)}, u32[]{:S(2)}, u32[]{:S(2)}) collective-permute-start(bf16[512,128]{1,0:T(8,128)(2,1)S(1)} %add_loads.1.rest_1_.a_ref), channel_id=1, source_target_pairs={{0,24},{1,97},{2,26},{3,99},{4,28},{5,101},{6,30},{7,103},{8,0},{9... | collective-permute-start | bytes 393224 | tf_op jit(solution)/shard_map/ppermute | solution.py:370
  71.5 0.9 collective-permute-start.7
  72.4 0.8 collective-permute-start.6
  73.2 0.0 all-to-all-done.1.gathered_ref
  73.2 0.0 copy-done.2
  73.2 2.8 %reduced_rows.1 = (bf16[2,128,128]{2,1,0:T(8,128)(2,1)S(1)}, bf16[16,256,128]{2,1,0:T(8,128)(2,1)}) custom-call(bf16[8,3,2,128,256]{4,3,2,1,0:T(8,128)(2,1)} %bitcast.21, bf16[16,272,128]{2,1,0:T(8,128)(2,1)S(1)} %all-to-all-done.1.gathered_ref, bf16[2,128,128]{2,1,0:T(8,128)(2,1)S(1)} %copy-done.2, bf16[512,128]{1,0:T(8,128)(2,1)S(1)} %add_loads.1.rest_1_.a_ref), custom_call_target="tpu_custom_call" | custom-call | flops 30000001024 | bytes 1000 | tf_op jit(solution)/shard_map/reduced_rows/pallas_call | solution.py:176
  76.1 4.5 %all-to-all-start.2 = ((bf16[16,256,128]{2,1,0:T(8,128)(2,1)}), bf16[16,256,128]{2,1,0:T(8,128)(2,1)S(1)}, u32[]{:S(2)}, u32[]{:S(2)}) async-start(bf16[16,256,128]{2,1,0:T(8,128)(2,1)} %get-tuple-element.31), calls=%async_computation.2 | async-start | bytes 2097152 | tf_op jit(solution)/shard_map/all_to_all | solution.py:374
  80.6 0.0 collective-permute-done.8.d_ref
  80.6 0.0 collective-permute-done.7.c_ref
  80.6 0.0 collective-permute-done.6.b_ref
  80.7 3.2 %collective-permute-start.11 = (bf16[4,512,128]{2,1,0:T(8,128)(2,1)S(1)}, bf16[4,512,128]{2,1,0:T(8,128)(2,1)}, u32[]{:S(2)}, u32[]{:S(2)}) collective-permute-start(bf16[4,512,128]{2,1,0:T(8,128)(2,1)S(1)} %pack_loads.1.rest_0_), channel_id=1, source_target_pairs={{0,96},{1,25},{2,98},{3,27},{4,100},{5,29},{6,102},{7,31},{8,104},... | collective-permute-start | bytes 1572872 | tf_op jit(solution)/shard_map/ppermute | solution.py:370
  83.9 0.9 collective-permute-start.10
  84.7 0.9 collective-permute-start.9
  85.6 12.4 %all-to-all-done.2.gathered_ref = bf16[16,256,128]{2,1,0:T(8,128)(2,1)S(1)} async-done(((bf16[16,256,128]{2,1,0:T(8,128)(2,1)}), bf16[16,256,128]{2,1,0:T(8,128)(2,1)S(1)}, u32[]{:S(2)}, u32[]{:S(2)}) %all-to-all-start.2) | async-done | bytes 1048608 | tf_op jit(solution)/shard_map/all_to_all | solution.py:374
  98.0 2.9 %last_rows.1 = (bf16[2,128,128]{2,1,0:T(8,128)(2,1)S(1)}, bf16[16,256,128]{2,1,0:T(8,128)(2,1)}) custom-call(bf16[8,3,2,128,256]{4,3,2,1,0:T(8,128)(2,1)} %bitcast.22, bf16[16,256,128]{2,1,0:T(8,128)(2,1)S(1)} %all-to-all-done.2.gathered_ref, bf16[4,512,128]{2,1,0:T(8,128)(2,1)S(1)} %pack_loads.1.rest_0_), custom_call_target="tpu_custom_call" | custom-call | flops 30000001024 | bytes 1000 | tf_op jit(solution)/shard_map/last_rows/pallas_call | solution.py:176
  100.9 7.5 %all-to-all-start.3 = ((bf16[16,256,128]{2,1,0:T(8,128)(2,1)}), bf16[16,256,128]{2,1,0:T(8,128)(2,1)S(1)}, u32[]{:S(2)}, u32[]{:S(2)}) async-start(bf16[16,256,128]{2,1,0:T(8,128)(2,1)} %get-tuple-element.36), calls=%async_computation.3 | async-start | bytes 2097152 | tf_op jit(solution)/shard_map/all_to_all | solution.py:374
  108.4 0.0 collective-permute-done.11.rest_3_
  108.4 0.0 collective-permute-done.10.rest_2_
  108.4 0.0 collective-permute-done.9.rest_1_
  108.4 7.4 %first_loads.1 = (f32[4096,256]{1,0:T(8,128)}, s32[1,2048]{1,0:T(1,128)S(1)}, f32[1,2048]{1,0:T(1,128)S(1)}) custom-call(s32[3]{0:T(128)S(1)} %pad_add_fusion.place_ref, bf16[16,272,128]{2,1,0:T(8,128)(2,1)S(1)} %all-to-all-done.1.gathered_ref, bf16[4,512,128]{2,1,0:T(8,128)(2,1)S(1)} %pack_loads.1.rest_0_, ...), custom_call_target="tpu_custom_call" | custom-call | flops 30000001024 | bytes 1000 | tf_op jit(solution)/shard_map/first_loads/pallas_call | solution.py:256
  115.8 0.7 pad_maximum_fusion.1
  116.5 4.8 %all-to-all-done.3.gathered_ref = bf16[16,256,128]{2,1,0:T(8,128)(2,1)S(1)} async-done(((bf16[16,256,128]{2,1,0:T(8,128)(2,1)}), bf16[16,256,128]{2,1,0:T(8,128)(2,1)S(1)}, u32[]{:S(2)}, u32[]{:S(2)}) %all-to-all-start.3) | async-done | bytes 1048608 | tf_op jit(solution)/shard_map/all_to_all | solution.py:374
  121.3 5.4 %all-gather.7.cloned.1.call-done = bf16[16,1024,512]{2,1,0:T(8,128)(2,1)} async-done(((bf16[2,1024,512]{2,1,0:T(8,128)(2,1)}), bf16[16,1024,512]{2,1,0:T(8,128)(2,1)}) %all-gather.7.cloned.1.call-update) | async-done | bytes 16777232 | tf_op jit(solution)/shard_map/all_gather | solution.py:397
  126.7 9.8 %all_loads.1 = (bf16[4096,256]{1,0:T(8,128)(2,1)S(1)}, bf16[8,2,1024,512]{3,2,1,0:T(8,128)(2,1)S(1)}) custom-call(s32[1,2048]{1,0:T(1,128)S(1)} %get-tuple-element.34.ids, f32[1,2048]{1,0:T(1,128)S(1)} %get-tuple-element.35.weights, bf16[16,256,128]{2,1,0:T(8,128)(2,1)S(1)} %all-to-all-done.3.gathered_ref, f32[4096,256]{1,0:T(8,128)} %get-tuple-element.37.first_ref, ...), custom_call_target="tpu_custom_call" | custom-call | tf_op jit(solution)/shard_map/all_loads/pallas_call | solution.py:311
  136.5 5.3 %stress.1 = bf16[2,1024,128]{2,1,0:T(8,128)(2,1)} custom-call(bf16[4096,256]{1,0:T(8,128)(2,1)S(1)} %get-tuple-element.38.loads_ref, bf16[8,2,1024,512]{3,2,1,0:T(8,128)(2,1)S(1)} %get-tuple-element.39.maps_ref), custom_call_target="tpu_custom_call" | custom-call | tf_op jit(solution)/shard_map/stress/pallas_call | solution.py:348
  (3 shorter events, 0.0 us)
Async XLA Ops:
  7.2 2.7 %copy-start.5 = (bf16[2,128,128]{2,1,0:T(8,128)(2,1)S(1)}, bf16[2,128,128]{2,1,0:T(8,128)(2,1)}, u32[]{:S(2)}) copy-start(bf16[2,128,128]{2,1,0:T(8,128)(2,1)} %param.11) | copy-start | bytes 196612
  7.2 32.8 %all-gather.5.cloned.1.call-start = ((), (), s32[]{:S(2)}) async-start(), calls=%async_computation.4 | async-start | bytes 3538944 | tf_op jit(solution)/shard_map/all_gather | solution.py:396
  9.1 117.6 %all-gather.7.cloned.1.call-start = ((), (), s32[]{:S(2)}) async-start(), calls=%async_computation.5 | async-start | bytes 18874368 | tf_op jit(solution)/shard_map/all_gather | solution.py:397
  9.8 9.4 %copy-start.6 = (bf16[3072]{0:T(1024)(128)(2,1)S(1)}, bf16[3072]{0:T(1024)(128)(2,1)}, u32[]{:S(2)}) copy-start(bf16[3072]{0:T(1024)(128)(2,1)} %param.18) | copy-start | bytes 18436
  9.8 9.5 %copy-start = (bf16[2,3072,128]{2,1,0:T(8,128)(2,1)S(1)}, bf16[2,3072,128]{2,1,0:T(8,128)(2,1)}, u32[]{:S(2)}) copy-start(bf16[2,3072,128]{2,1,0:T(8,128)(2,1)} %earlier_ref.1) | copy-start | bytes 4718596
  9.9 9.5 %copy-start.1 = (s32[3072]{0:T(1024)S(1)}, s32[3072]{0:T(1024)}, u32[]{:S(2)}) copy-start(s32[3072]{0:T(1024)} %param.17) | copy-start | bytes 36868
  11.1 28.9 %copy-start.3 = (s32[2,128]{1,0:T(2,128)S(1)}, s32[2,128]{1,0:T(2,128)}, u32[]{:S(2)}) copy-start(s32[2,128]{1,0:T(2,128)} %rest_0_.2) | copy-start | bytes 3076
  11.1 28.9 %copy-start.4 = (bf16[2,128]{1,0:T(2,128)(2,1)S(1)}, bf16[2,128]{1,0:T(2,128)(2,1)}, u32[]{:S(2)}) copy-start(bf16[2,128]{1,0:T(2,128)(2,1)} %rest_1_.1) | copy-start | bytes 1540
  11.1 26.2 %all-to-all-start = ((bf16[16,256,128]{2,1,0:T(8,128)(2,1)}), bf16[16,256,128]{2,1,0:T(8,128)(2,1)S(1)}, u32[]{:S(2)}, u32[]{:S(2)}) async-start(bf16[16,256,128]{2,1,0:T(8,128)(2,1)} %broadcast_in_dim.14), calls=%async_computation | async-start | bytes 2097152 | tf_op jit(solution)/shard_map/all_to_all | solution.py:374
  27.7 22.0 %collective-permute-start = (bf16[4,512,128]{2,1,0:T(8,128)(2,1)}, bf16[4,512,128]{2,1,0:T(8,128)(2,1)S(1)}, u32[]{:S(2)}, u32[]{:S(2)}) collective-permute-start(bf16[4,512,128]{2,1,0:T(8,128)(2,1)} %get-tuple-element.24), channel_id=1, source_target_pairs={{0,8},{1,33},{2,10},{3,35},{4,12},{5,37},{6,14},{7,39},{8,16},{9,4... | collective-permute-start | bytes 1572872 | tf_op jit(solution)/shard_map/ppermute | solution.py:370
  29.6 20.2 %collective-permute-start.1 = (bf16[4,512,128]{2,1,0:T(8,128)(2,1)}, bf16[4,512,128]{2,1,0:T(8,128)(2,1)S(1)}, u32[]{:S(2)}, u32[]{:S(2)}) collective-permute-start(bf16[4,512,128]{2,1,0:T(8,128)(2,1)} %get-tuple-element.25), channel_id=1, source_target_pairs={{0,16},{1,65},{2,18},{3,67},{4,20},{5,69},{6,22},{7,71},{8,24},{9,... | collective-permute-start | bytes 1572872 | tf_op jit(solution)/shard_map/ppermute | solution.py:370
  32.3 17.5 %collective-permute-start.2 = (bf16[4,512,128]{2,1,0:T(8,128)(2,1)}, bf16[4,512,128]{2,1,0:T(8,128)(2,1)}, u32[]{:S(2)}, u32[]{:S(2)}) collective-permute-start(bf16[4,512,128]{2,1,0:T(8,128)(2,1)} %get-tuple-element.26), channel_id=1, source_target_pairs={{0,24},{1,97},{2,26},{3,99},{4,28},{5,101},{6,30},{7,103},{8,0},{9... | collective-permute-start | bytes 1572872 | tf_op jit(solution)/shard_map/ppermute | solution.py:370
  42.8 30.4 %all-to-all-start.1 = ((bf16[16,272,128]{2,1,0:T(8,128)(2,1)}), bf16[16,272,128]{2,1,0:T(8,128)(2,1)S(1)}, u32[]{:S(2)}, u32[]{:S(2)}) async-start(bf16[16,272,128]{2,1,0:T(8,128)(2,1)} %get-tuple-element.22), calls=%async_computation.1 | async-start | bytes 2228224 | tf_op jit(solution)/shard_map/all_to_all | solution.py:374
  49.8 23.4 %copy-start.2 = (bf16[2,128,128]{2,1,0:T(8,128)(2,1)S(1)}, bf16[2,128,128]{2,1,0:T(8,128)(2,1)}, u32[]{:S(2)}) copy-start(bf16[2,128,128]{2,1,0:T(8,128)(2,1)} %rest_0_.3) | copy-start | bytes 196612
  51.2 15.8 %collective-permute-start.3 = (bf16[512,128]{1,0:T(8,128)(2,1)S(1)}, bf16[512,128]{1,0:T(8,128)(2,1)S(1)}, u32[]{:S(2)}, u32[]{:S(2)}) collective-permute-start(bf16[512,128]{1,0:T(8,128)(2,1)S(1)} %get-tuple-element.28), channel_id=1, source_target_pairs={{0,32},{1,9},{2,34},{3,11},{4,36},{5,13},{6,38},{7,15},{8,40},{9,1... | collective-permute-start | bytes 393224 | tf_op jit(solution)/shard_map/ppermute | solution.py:370
  53.2 15.5 %collective-permute-start.4 = (bf16[512,128]{1,0:T(8,128)(2,1)S(1)}, bf16[512,128]{1,0:T(8,128)(2,1)S(1)}, u32[]{:S(2)}, u32[]{:S(2)}) collective-permute-start(bf16[512,128]{1,0:T(8,128)(2,1)S(1)} %get-tuple-element.29), channel_id=1, source_target_pairs={{0,64},{1,17},{2,66},{3,19},{4,68},{5,21},{6,70},{7,23},{8,72},{9,... | collective-permute-start | bytes 393224 | tf_op jit(solution)/shard_map/ppermute | solution.py:370
  55.9 12.8 %collective-permute-start.5 = (bf16[512,128]{1,0:T(8,128)(2,1)S(1)}, bf16[512,128]{1,0:T(8,128)(2,1)S(1)}, u32[]{:S(2)}, u32[]{:S(2)}) collective-permute-start(bf16[512,128]{1,0:T(8,128)(2,1)S(1)} %get-tuple-element.30), channel_id=1, source_target_pairs={{0,96},{1,25},{2,98},{3,27},{4,100},{5,29},{6,102},{7,31},{8,104},... | collective-permute-start | bytes 393224 | tf_op jit(solution)/shard_map/ppermute | solution.py:370
  68.8 11.8 %collective-permute-start.8 = (bf16[512,128]{1,0:T(8,128)(2,1)S(1)}, bf16[512,128]{1,0:T(8,128)(2,1)S(1)}, u32[]{:S(2)}, u32[]{:S(2)}) collective-permute-start(bf16[512,128]{1,0:T(8,128)(2,1)S(1)} %add_loads.1.rest_1_.a_ref), channel_id=1, source_target_pairs={{0,24},{1,97},{2,26},{3,99},{4,28},{5,101},{6,30},{7,103},{8,0},{9... | collective-permute-start | bytes 393224 | tf_op jit(solution)/shard_map/ppermute | solution.py:370
  71.5 9.1 %collective-permute-start.7 = (bf16[512,128]{1,0:T(8,128)(2,1)S(1)}, bf16[512,128]{1,0:T(8,128)(2,1)S(1)}, u32[]{:S(2)}, u32[]{:S(2)}) collective-permute-start(bf16[512,128]{1,0:T(8,128)(2,1)S(1)} %add_loads.1.rest_1_.a_ref), channel_id=1, source_target_pairs={{0,16},{1,65},{2,18},{3,67},{4,20},{5,69},{6,22},{7,71},{8,24},{9,... | collective-permute-start | bytes 393224 | tf_op jit(solution)/shard_map/ppermute | solution.py:370
  72.4 8.2 %collective-permute-start.6 = (bf16[512,128]{1,0:T(8,128)(2,1)S(1)}, bf16[512,128]{1,0:T(8,128)(2,1)S(1)}, u32[]{:S(2)}, u32[]{:S(2)}) collective-permute-start(bf16[512,128]{1,0:T(8,128)(2,1)S(1)} %add_loads.1.rest_1_.a_ref), channel_id=1, source_target_pairs={{0,8},{1,33},{2,10},{3,35},{4,12},{5,37},{6,14},{7,39},{8,16},{9,4... | collective-permute-start | bytes 393224 | tf_op jit(solution)/shard_map/ppermute | solution.py:370
  76.1 21.9 %all-to-all-start.2 = ((bf16[16,256,128]{2,1,0:T(8,128)(2,1)}), bf16[16,256,128]{2,1,0:T(8,128)(2,1)S(1)}, u32[]{:S(2)}, u32[]{:S(2)}) async-start(bf16[16,256,128]{2,1,0:T(8,128)(2,1)} %get-tuple-element.31), calls=%async_computation.2 | async-start | bytes 2097152 | tf_op jit(solution)/shard_map/all_to_all | solution.py:374
  80.7 27.7 %collective-permute-start.11 = (bf16[4,512,128]{2,1,0:T(8,128)(2,1)S(1)}, bf16[4,512,128]{2,1,0:T(8,128)(2,1)}, u32[]{:S(2)}, u32[]{:S(2)}) collective-permute-start(bf16[4,512,128]{2,1,0:T(8,128)(2,1)S(1)} %pack_loads.1.rest_0_), channel_id=1, source_target_pairs={{0,96},{1,25},{2,98},{3,27},{4,100},{5,29},{6,102},{7,31},{8,104},... | collective-permute-start | bytes 1572872 | tf_op jit(solution)/shard_map/ppermute | solution.py:370
  83.9 24.5 %collective-permute-start.10 = (bf16[4,512,128]{2,1,0:T(8,128)(2,1)S(1)}, bf16[4,512,128]{2,1,0:T(8,128)(2,1)}, u32[]{:S(2)}, u32[]{:S(2)}) collective-permute-start(bf16[4,512,128]{2,1,0:T(8,128)(2,1)S(1)} %pack_loads.1.rest_0_), channel_id=1, source_target_pairs={{0,64},{1,17},{2,66},{3,19},{4,68},{5,21},{6,70},{7,23},{8,72},{9,... | collective-permute-start | bytes 1572872 | tf_op jit(solution)/shard_map/ppermute | solution.py:370
  84.7 23.7 %collective-permute-start.9 = (bf16[4,512,128]{2,1,0:T(8,128)(2,1)S(1)}, bf16[4,512,128]{2,1,0:T(8,128)(2,1)}, u32[]{:S(2)}, u32[]{:S(2)}) collective-permute-start(bf16[4,512,128]{2,1,0:T(8,128)(2,1)S(1)} %pack_loads.1.rest_0_), channel_id=1, source_target_pairs={{0,32},{1,9},{2,34},{3,11},{4,36},{5,13},{6,38},{7,15},{8,40},{9,1... | collective-permute-start | bytes 1572872 | tf_op jit(solution)/shard_map/ppermute | solution.py:370
  100.9 20.4 %all-to-all-start.3 = ((bf16[16,256,128]{2,1,0:T(8,128)(2,1)}), bf16[16,256,128]{2,1,0:T(8,128)(2,1)S(1)}, u32[]{:S(2)}, u32[]{:S(2)}) async-start(bf16[16,256,128]{2,1,0:T(8,128)(2,1)} %get-tuple-element.36), calls=%async_computation.3 | async-start | bytes 2097152 | tf_op jit(solution)/shard_map/all_to_all | solution.py:374
Sparse Core Ops, SparseCore 0:
  9.7 30.2 all-gather.4
  41.7 84.9 all-gather.6

commit v3 on v2

--- a/solution.py
+++ b/solution.py
@@ -56,65 +56,24 @@
     )(place, ids, weights, earlier)
 
 
-def sum_loads_kernel(place_ref, *refs):
-    parts, outs = refs[:4], refs[5:]
-    for j in range(4):
-        block = (place_ref[0] + j) % 4
-        total = parts[0][block].astype(F32)
-        for part in parts[1:]:
-            total += part[block].astype(F32)
-        outs[j][...] = total.astype(BF16)
-
-
-def sum_loads(place, parts, tie):
+def sum_loads_kernel(a_ref, b_ref, c_ref, d_ref, tie_ref, out_ref):
+    for block in range(4):
+        total = a_ref[block].astype(F32) + b_ref[block].astype(F32)
+        total += c_ref[block].astype(F32) + d_ref[block].astype(F32)
+        out_ref[block] = total.astype(BF16)
+
+
+def sum_loads(name, parts, tie):
     vmem = pl.BlockSpec(memory_space=pltpu.VMEM)
     return pl.pallas_call(
         sum_loads_kernel,
-        out_shape=[jax.ShapeDtypeStruct((512, 128), BF16)] * 4,
-        in_specs=[pl.BlockSpec(memory_space=pltpu.SMEM)]
-        + [vmem] * 4
-        + [pl.BlockSpec(memory_space=pl.ANY)],
-        out_specs=[vmem] * 4,
-        compiler_params=PARAMS,
-        cost_estimate=COST,
-        name="sum_loads",
-    )(place, *parts, tie)
-
-
-def add_loads_kernel(a_ref, b_ref, c_ref, d_ref, out_ref):
-    total = a_ref[...].astype(F32) + b_ref[...].astype(F32)
-    total += c_ref[...].astype(F32) + d_ref[...].astype(F32)
-    out_ref[...] = total.astype(BF16)
-
-
-def add_loads(parts):
-    vmem = pl.BlockSpec(memory_space=pltpu.VMEM)
-    return pl.pallas_call(
-        add_loads_kernel,
-        out_shape=jax.ShapeDtypeStruct((512, 128), BF16),
-        in_specs=[vmem] * 4,
-        out_specs=vmem,
-        compiler_params=PARAMS,
-        name="add_loads",
-    )(*parts)
-
-
-def pack_kernel(a_ref, b_ref, c_ref, d_ref, tie_ref, out_ref):
-    for k, value_ref in enumerate((a_ref, b_ref, c_ref, d_ref)):
-        out_ref[k] = value_ref[...]
-
-
-def pack_loads(values, tie):
-    vmem = pl.BlockSpec(memory_space=pltpu.VMEM)
-    return pl.pallas_call(
-        pack_kernel,
-        out_shape=jax.ShapeDtypeStruct((4, *values[0].shape), BF16),
+        out_shape=jax.ShapeDtypeStruct(parts[0].shape, BF16),
         in_specs=[vmem] * 4 + [pl.BlockSpec(memory_space=pl.ANY)],
         out_specs=vmem,
         compiler_params=PARAMS,
         cost_estimate=COST,
-        name="pack_loads",
-    )(*values, tie)
+        name=name,
+    )(*parts, tie)
 
 
 def send_copies(source, copies_ref, sems):
@@ -135,15 +94,14 @@
     factor_copy = pltpu.make_async_copy(factors_ref.at[:, pick], factor, factor_sem)
     factor_copy.start()
     read_panels(gathered_ref, side)
-    real = jnp.zeros((128, 256), F32)
-    imag = jnp.zeros((128, 256), F32)
+    total = jnp.zeros((256, 256), F32)
     factor_copy.wait()
     for block in range(COLS):
         part = side[block * 256 : (block + 1) * 256]
-        real += jnp.dot(factor[block, 0], part, preferred_element_type=F32)
-        imag += jnp.dot(factor[block, 1], part, preferred_element_type=F32)
-    out_real = real[:, :128] - imag[:, 128:]
-    out_imag = real[:, 128:] + imag[:, :128]
+        left = factor[block].reshape(256, 256)
+        total += jnp.dot(left, part, preferred_element_type=F32)
+    out_real = total[:128, :128] - total[128:, 128:]
+    out_imag = total[:128, 128:] + total[128:, :128]
     if base:
         out_real = base_ref[0].astype(F32) - out_real
         out_imag = base_ref[1].astype(F32) - out_imag
@@ -235,15 +193,14 @@
     copies = []
     for j in range(4):
         old_copies[j].wait()
-        major = (place_ref[0] - j + 4) % 4
-        for k in range(4):
-            minor = (place_ref[1] - k + 4) % 4
+        minor = (place_ref[1] - j + 4) % 4
+        for major in range(4):
             block = (major * 4 + minor) + place_ref[2] * 3 * (minor - major)
             rows = pl.ds(pl.multiple_of(block * 256, 256), 256)
-            total[rows, :128] += old[j, k, :256].astype(F32)
-            total[rows, 128:] += old[j, k, 256:].astype(F32)
+            total[rows, :128] += old[j, major, :256].astype(F32)
+            total[rows, 128:] += old[j, major, 256:].astype(F32)
             copies.append(
-                pltpu.make_async_copy(total.at[rows], out_ref.at[rows], sems.at[j * 4 + k])
+                pltpu.make_async_copy(total.at[rows], out_ref.at[rows], sems.at[j * 4 + major])
             )
             copies[-1].start()
     for copy in copies:
@@ -278,67 +235,55 @@
     )(place, gathered, *old)
 
 
-def all_loads_kernel(
-    ids, weights, gathered_ref, first_ref, maps_ref, out_ref, held_ref, side, first, first_sems, sems
-):
-    first_copies = []
-    for part in range(4):
-        rows = pl.ds(part * 1024, 1024)
-        first_copies.append(
-            pltpu.make_async_copy(first_ref.at[rows], first.at[rows], first_sems.at[part])
-        )
-    copies = [
-        pltpu.make_async_copy(maps_ref.at[k], held_ref.at[k], sems.at[k]) for k in range(COLS)
-    ]
-    for copy in first_copies:
-        copy.start()
+def all_loads_kernel(ids, weights, gathered_ref, first_ref, out_ref, side, first, total, sem):
+    copy = pltpu.make_async_copy(first_ref, first, sem)
+    copy.start()
     read_panels(gathered_ref, side)
-    for part in range(4):
-        rows = slice(part * 1024, (part + 1) * 1024)
-        total = panel_loads(side, ids, weights, part * 1024, 1024, 512)
-        first_copies[part].wait()
-        out_ref[rows] = (first[rows] + total).astype(BF16)
-        if part == 0:
-            for copy in copies:
-                copy.start()
-    for copy in copies:
-        copy.wait()
-
-
-def all_loads(ids, weights, gathered, first, maps):
+    for start in range(0, PATCHES, 1024):
+        total[start : start + 1024] = panel_loads(side, ids, weights, start, 1024, 512)
+    copy.wait()
+    for start in range(0, PATCHES, 256):
+        rows = slice(start, start + 256)
+        out_ref[rows] = (first[rows] + total[rows]).astype(BF16)
+
+
+def all_loads(ids, weights, gathered, first):
     vmem = pl.BlockSpec(memory_space=pltpu.VMEM)
     hbm = pl.BlockSpec(memory_space=pltpu.HBM)
     return pl.pallas_call(
         all_loads_kernel,
-        out_shape=(pltpu.VMEM((PATCHES, 256), BF16), pltpu.VMEM(maps.shape, BF16)),
-        in_specs=[vmem] * 3 + [hbm] * 2,
-        out_specs=(vmem, vmem),
+        out_shape=jax.ShapeDtypeStruct((PATCHES, 256), BF16),
+        in_specs=[vmem] * 3 + [hbm],
+        out_specs=vmem,
         scratch_shapes=[
             pltpu.VMEM((2048, 256), BF16),
             pltpu.VMEM((PATCHES, 256), F32),
-            pltpu.SemaphoreType.DMA((4,)),
-            pltpu.SemaphoreType.DMA((COLS,)),
+            pltpu.VMEM((PATCHES, 256), F32),
+            pltpu.SemaphoreType.DMA,
         ],
         compiler_params=PARAMS,
         name="all_loads",
-    )(
-        ids,
-        weights,
-        gathered,
-        pltpu.with_memory_space_constraint(first, pltpu.HBM),
-        pltpu.with_memory_space_constraint(maps, pltpu.HBM),
-    )
-
-
-def stress_kernel(loads_ref, maps_ref, out_ref):
-    for first in range(0, 1024, 512):
-        rows = slice(first, first + 512)
-        real = jnp.zeros((512, 256), F32)
-        imag = jnp.zeros((512, 256), F32)
+    )(ids, weights, gathered, pltpu.with_memory_space_constraint(first, pltpu.HBM))
+
+
+def stress_kernel(loads_ref, maps_ref, out_ref, held, sems):
+    copies = []
+    for step in range(4):
+        rows = pl.ds(step * 256, 256)
+        for block in range(COLS):
+            source, target = maps_ref.at[block, :, rows], held.at[block, :, rows]
+            copies.append(pltpu.make_async_copy(source, target, sems.at[step, block]))
+            copies[-1].start()
+    for step in range(4):
+        for copy in copies[step * COLS : (step + 1) * COLS]:
+            copy.wait()
+        rows = slice(step * 256, (step + 1) * 256)
+        real = jnp.zeros((256, 256), F32)
+        imag = jnp.zeros((256, 256), F32)
         for block in range(COLS):
             part = loads_ref[block * 512 : (block + 1) * 512]
-            real += jnp.dot(maps_ref[block, 0, rows], part, preferred_element_type=F32)
-            imag += jnp.dot(maps_ref[block, 1, rows], part, preferred_element_type=F32)
+            real += jnp.dot(held[block, 0, rows], part, preferred_element_type=F32)
+            imag += jnp.dot(held[block, 1, rows], part, preferred_element_type=F32)
         out_ref[0, rows] = (real[:, :128] - imag[:, 128:]).astype(BF16)
         out_ref[1, rows] = (real[:, 128:] + imag[:, :128]).astype(BF16)
 
@@ -348,14 +293,15 @@
     return pl.pallas_call(
         stress_kernel,
         out_shape=jax.ShapeDtypeStruct((2, 1024, 128), BF16),
-        in_specs=[vmem] * 2,
+        in_specs=[vmem, pl.BlockSpec(memory_space=pltpu.HBM)],
         out_specs=vmem,
-        compiler_params=PARAMS,
+        scratch_shapes=[
+            pltpu.VMEM((COLS, 2, 1024, 512), BF16),
+            pltpu.SemaphoreType.DMA((4, COLS)),
+        ],
+        compiler_params=pltpu.CompilerParams(vmem_limit_bytes=32 * 2**20),
         name="stress",
-    )(
-        pltpu.with_memory_space_constraint(loads, pltpu.VMEM),
-        pltpu.with_memory_space_constraint(maps, pltpu.VMEM),
-    )
+    )(loads, pltpu.with_memory_space_constraint(maps, pltpu.HBM))
 
 
 def along_axis(value, hop, major):
@@ -393,28 +339,28 @@
     x, z = row // 4, row % 4
     place = jnp.stack([x + core * (z - x), z + core * (x - z), core]).astype(jnp.int32)
 
+
     factors = lax.all_gather(jnp.stack([inv_first, coupling, inv_last]), "col")
     maps = lax.all_gather(stress_map, "col")
     rhs_all = to_rows(jnp.broadcast_to(rhs_first.reshape(1, 256, 128), (ROWS, 256, 128)))
     old = old_loads(place, patch_old[None], weight_old[None], earlier)
     x_first, copies = rows_product(
-        "first_rows", factors, 0, rhs_all, extra=[patch_new, weight_new]
+        "first_rows", factors, 0, rhs_all, extra=[patch_new, weight_new], ties=(old[0],)
     )
     x_first_all = to_rows(copies)
-    old = sum_loads(
-        place, [old[0]] + [along_axis(old[hop], hop, False) for hop in (1, 2, 3)], x_first
-    )
-    old = add_loads([old[0]] + [along_axis(old[hop], hop, True) for hop in (1, 2, 3)])
+    old = [old[0]] + [along_axis(old[hop], hop, False) for hop in (1, 2, 3)]
+    old = sum_loads("sum_minor", old, x_first)
     reduced, copies = rows_product(
         "reduced_rows", factors, 1, x_first_all, base=rhs_last, ties=(old,)
     )
     reduced_all = to_rows(copies)
-    old = pack_loads([old] + [along_axis(old, hop, False) for hop in (1, 2, 3)], reduced)
+    old = [old] + [along_axis(old, hop, True) for hop in (1, 2, 3)]
+    old = sum_loads("sum_major", old, reduced)
     x_last, copies = rows_product("last_rows", factors, 2, reduced_all, ties=(old,))
     x_last_all = to_rows(copies)
-    old = [old] + [along_axis(old, hop, True) for hop in (1, 2, 3)]
+    old = [old] + [along_axis(old, hop, False) for hop in (1, 2, 3)]
     loads, ids, weights = first_loads(place, x_first_all, old)
-    stress_rao = stress(*all_loads(ids, weights, x_last_all, loads, maps))
+    stress_rao = stress(all_loads(ids, weights, x_last_all, loads), maps)
     return (jnp.stack([x_first, x_last]), stress_rao)
 
 

time: 150 us -> 144 us (0.960)
  waiting for transfers between devices: 40.9 us -> 32.8 us
  starting transfers between devices: 48.6 us -> 44.6 us
  Pallas kernels: 40.9 us -> 44.5 us
  local copies, waits for them, and re-layouts: 1.24 us -> 3.07 us
    ppermute x12 -> x9, waiting for transfers between devices: 11.4 us -> 3.41 us  [along_axis(): return lax.ppermute(value, ('row', 'col'), pairs)]
    ppermute x12 -> x9, starting transfers between devices: 21.5 us -> 17.7 us  [along_axis(): return lax.ppermute(value, ('row', 'col'), pairs)]
    pallas_call x1, Pallas kernels: 5.28 us -> 8.24 us  [stress(): pl.pallas_call(stress_kernel, out_shape=jax.ShapeDtypeStruct((2, 1024, 12...]
    all_gather x1, waiting for transfers between devices: 5.42 us -> 2.73 us  [on_device(): maps = lax.all_gather(stress_map, 'col')]
    all_to_all x4, waiting for transfers between devices: 20.7 us -> 23 us  [to_rows(): return lax.all_to_all(copies, 'row', 0, 0, tiled=True)]
    unnamed x14 -> x22, local copies, waits for them, and re-layouts: 0.04 us -> 1.88 us
    pallas_call x4 -> x3, Pallas kernels: 11.3 us -> 11.9 us  [the longest x1 6.82 us: all_loads(): pl.pallas_call(all_loads_kernel, out_shape=jax.ShapeDtypeStruct((PATCHES,...]
  transfers between devices with their start and end apart: 18 -> 15, of which waited for: 7 -> 8; matrix products, arithmetic and copies ran while one was open for 1% -> 1% of each run, Pallas kernels for 17% -> 26%
where the time goes in v3:
time: 144 us; the launch traced here: 142 us
  starting transfers between devices  44.6 us (31%)
  Pallas kernels  44.5 us (31%)
  waiting for transfers between devices  32.8 us (23%)
  between operations  14.3 us (10%)
  local copies, waits for them, and re-layouts  3.07 us (2%)
  other arithmetic  2.61 us (2%)
    all_to_all x4, starting transfers between devices, to_rows(): return lax.all_to_all(copies, 'row', 0, 0, tiled=True)  26.9 us
    all_to_all x4, waiting for transfers between devices, to_rows(): return lax.all_to_all(copies, 'row', 0, 0, tiled=True)  23 us
    ppermute x9, starting transfers between devices, along_axis(): return lax.ppermute(value, ('row', 'col'), pairs)  17.7 us
    pallas_call x3, Pallas kernels, rows_product(): pl.pallas_call(functools.partial(rows_kernel, pick=pick, base=base is not...  8.51 us
    pallas_call x1, Pallas kernels, old_loads(): pl.pallas_call(functools.partial(old_loads_kernel, chunk=512), out_shape=...  8.43 us
    pallas_call x1, Pallas kernels, stress(): pl.pallas_call(stress_kernel, out_shape=jax.ShapeDtypeStruct((2, 1024, 12...  8.24 us
    pallas_call x1, Pallas kernels, first_loads(): pl.pallas_call(first_loads_kernel, out_shape=(pltpu.HBM((PATCHES, 256), F...  7.39 us
    pallas_call x1, Pallas kernels, all_loads(): pl.pallas_call(all_loads_kernel, out_shape=jax.ShapeDtypeStruct((PATCHES,...  6.82 us
  transfers between devices with their start and end apart: 15, of which 8 were waited for; matrix products, arithmetic and copies ran while one was open for 1% of the time, Pallas kernels for 26%

profile of v3, /device:TPU:0, one launch (start us, length us, event | category | flops | bytes accessed | tf_op | source)
XLA Modules:
  0.0 141.8 jit_solution(6789492908546068298)
XLA Ops:
  7.2 0.0 copy-start.9
  7.2 0.0 all-gather.5.cloned.1.call-start
  7.2 1.9 %pad_maximum_fusion = bf16[3,2,128,256]{3,2,1,0:T(8,128)(2,1)} fusion(bf16[1,2,128,256]{3,2,1,0:T(8,128)(2,1)} %bitcast.16, bf16[1,2,128,256]{3,2,1,0:T(8,128)(2,1)} %bitcast.17, bf16[1,2,128,256]{3,2,1,0:T(8,128)(2,1)} %bitcast.18), kind=kLoop, calls=%fused_computation | loop fusion | flops 393216 | bytes 786432 | tf_op jit(solution)/shard_map/stack | solution.py:343
  9.1 0.0 all-gather.5.cloned.1.call-update
  9.1 0.0 all-gather.7.cloned.1.call-start
  9.2 0.7 all-gather.7.cloned.1.call-update
  9.9 0.0 copy-start.10
  9.9 0.0 copy-start
  9.9 0.0 copy-start.1
  9.9 0.0 copy-done.9
  9.9 1.2 broadcast_in_dim.14
  11.1 0.0 copy-start.7
  11.1 0.0 copy-start.8
  11.1 8.1 %all-to-all-start = ((bf16[16,256,128]{2,1,0:T(8,128)(2,1)}), bf16[16,256,128]{2,1,0:T(8,128)(2,1)S(1)}, u32[]{:S(2)}, u32[]{:S(2)}) async-start(bf16[16,256,128]{2,1,0:T(8,128)(2,1)} %broadcast_in_dim.14), calls=%async_computation | async-start | bytes 2097152 | tf_op jit(solution)/shard_map/all_to_all | solution.py:320
  19.2 0.0 copy-done.10
  19.3 0.1 pad_add_fusion.place_ref
  19.3 0.0 copy-done
  19.3 0.0 copy-done.1
  19.3 8.4 %old_loads.1 = (bf16[4,512,128]{2,1,0:T(8,128)(2,1)S(1)}, bf16[4,512,128]{2,1,0:T(8,128)(2,1)}, bf16[4,512,128]{2,1,0:T(8,128)(2,1)}, bf16[4,512,128]{2,1,0:T(8,128)(2,1)}) custom-call(s32[3]{0:T(128)S(1)} %pad_add_fusion.place_ref, s32[1,3072]{1,0:T(1,128)S(1)} %bitcast.14, bf16[1,3072]{1,0:T(2,128)(2,1)S(1)} %broadcast_in_dim.16.weights_ref, ...), custom_call_target="tpu_custom_call" | custom-call | tf_op jit(solution)/shard_map/old_loads/pallas_call | solution.py:48
  27.8 0.8 copy-done.4
  28.6 1.9 %collective-permute-start = (bf16[4,512,128]{2,1,0:T(8,128)(2,1)}, bf16[4,512,128]{2,1,0:T(8,128)(2,1)}, u32[]{:S(2)}, u32[]{:S(2)}) collective-permute-start(bf16[4,512,128]{2,1,0:T(8,128)(2,1)} %get-tuple-element.18), channel_id=1, source_target_pairs={{0,8},{1,33},{2,10},{3,35},{4,12},{5,37},{6,14},{7,39},{8,16},{9,4... | collective-permute-start | bytes 1572872 | tf_op jit(solution)/shard_map/ppermute | solution.py:316
  30.5 2.7 %collective-permute-start.1 = (bf16[4,512,128]{2,1,0:T(8,128)(2,1)}, bf16[4,512,128]{2,1,0:T(8,128)(2,1)}, u32[]{:S(2)}, u32[]{:S(2)}) collective-permute-start(bf16[4,512,128]{2,1,0:T(8,128)(2,1)} %get-tuple-element.19), channel_id=1, source_target_pairs={{0,16},{1,65},{2,18},{3,67},{4,20},{5,69},{6,22},{7,71},{8,24},{9,... | collective-permute-start | bytes 1572872 | tf_op jit(solution)/shard_map/ppermute | solution.py:316
  33.1 0.0 copy-done.2
  33.1 1.5 %collective-permute-start.2 = (bf16[4,512,128]{2,1,0:T(8,128)(2,1)}, bf16[4,512,128]{2,1,0:T(8,128)(2,1)}, u32[]{:S(2)}, u32[]{:S(2)}) collective-permute-start(bf16[4,512,128]{2,1,0:T(8,128)(2,1)} %get-tuple-element.20), channel_id=1, source_target_pairs={{0,24},{1,97},{2,26},{3,99},{4,28},{5,101},{6,30},{7,103},{8,0},{9... | collective-permute-start | bytes 1572872 | tf_op jit(solution)/shard_map/ppermute | solution.py:316
  34.6 2.4 %all-to-all-done.gathered_ref = bf16[16,256,128]{2,1,0:T(8,128)(2,1)S(1)} async-done(((bf16[16,256,128]{2,1,0:T(8,128)(2,1)}), bf16[16,256,128]{2,1,0:T(8,128)(2,1)S(1)}, u32[]{:S(2)}, u32[]{:S(2)}) %all-to-all-start) | async-done | bytes 1048608 | tf_op jit(solution)/shard_map/all_to_all | solution.py:320
  37.0 2.9 %all-gather.5.cloned.1.call-done = bf16[24,2,128,256]{3,2,1,0:T(8,128)(2,1)} async-done(((bf16[3,2,128,256]{3,2,1,0:T(8,128)(2,1)}), bf16[24,2,128,256]{3,2,1,0:T(8,128)(2,1)}) %all-gather.5.cloned.1.call-update) | async-done | bytes 3145744 | tf_op jit(solution)/shard_map/all_gather | solution.py:343
  40.0 0.0 copy-done.7
  40.0 0.0 copy-done.8
  40.0 1.0 copy-done.5
  41.0 2.8 %first_rows.1 = (bf16[2,128,128]{2,1,0:T(8,128)(2,1)S(1)}, bf16[16,272,128]{2,1,0:T(8,128)(2,1)}) custom-call(bf16[8,3,2,128,256]{4,3,2,1,0:T(8,128)(2,1)} %bitcast.20, bf16[16,256,128]{2,1,0:T(8,128)(2,1)S(1)} %all-to-all-done.gathered_ref, s32[2,128]{1,0:T(2,128)S(1)} %copy-done.7, bf16[2,128]{1,0:T(2,128)(2,1)S(1)} %copy-done.8, ...), custom_call_target="tpu_custom_call" | custom-call | flops 30000001024 | bytes 1000 | tf_op jit(solution)/shard_map/first_rows/pallas_call | solution.py:134
  43.9 7.0 %all-to-all-start.1 = ((bf16[16,272,128]{2,1,0:T(8,128)(2,1)}), bf16[16,272,128]{2,1,0:T(8,128)(2,1)S(1)}, u32[]{:S(2)}, u32[]{:S(2)}) async-start(bf16[16,272,128]{2,1,0:T(8,128)(2,1)} %get-tuple-element.17), calls=%async_computation.1 | async-start | bytes 2228224 | tf_op jit(solution)/shard_map/all_to_all | solution.py:320
  50.8 0.0 collective-permute-done.b_ref
  50.8 0.0 collective-permute-done.1.c_ref
  50.8 0.0 collective-permute-done.2.d_ref
  50.8 0.0 copy-start.6
  50.9 2.6 %sum_minor.1.rest_1_.a_ref = bf16[4,512,128]{2,1,0:T(8,128)(2,1)} custom-call(bf16[4,512,128]{2,1,0:T(8,128)(2,1)S(1)} %copy-done.5, bf16[4,512,128]{2,1,0:T(8,128)(2,1)} %collective-permute-done.b_ref, bf16[4,512,128]{2,1,0:T(8,128)(2,1)} %collective-permute-done.1.c_ref, bf16[4,512,128]{2,1,0:T(8,128)(2,1)} %collective-permute-done.2.d_ref, ...), custom_call_target="tpu_custom_call" | custom-call | flops 30000001024 | bytes 1000 | tf_op jit(solution)/shard_map/sum_minor/pallas_call | solution.py:68
  53.5 1.9 %collective-permute-start.3 = (bf16[4,512,128]{2,1,0:T(8,128)(2,1)}, bf16[4,512,128]{2,1,0:T(8,128)(2,1)S(1)}, u32[]{:S(2)}, u32[]{:S(2)}) collective-permute-start(bf16[4,512,128]{2,1,0:T(8,128)(2,1)} %sum_minor.1.rest_1_.a_ref), channel_id=1, source_target_pairs={{0,32},{1,9},{2,34},{3,11},{4,36},{5,13},{6,38},{7,15},{8,40},{9,1... | collective-permute-start | bytes 1572872 | tf_op jit(solution)/shard_map/ppermute | solution.py:316
  55.4 2.7 %collective-permute-start.4 = (bf16[4,512,128]{2,1,0:T(8,128)(2,1)}, bf16[4,512,128]{2,1,0:T(8,128)(2,1)}, u32[]{:S(2)}, u32[]{:S(2)}) collective-permute-start(bf16[4,512,128]{2,1,0:T(8,128)(2,1)} %sum_minor.1.rest_1_.a_ref), channel_id=1, source_target_pairs={{0,64},{1,17},{2,66},{3,19},{4,68},{5,21},{6,70},{7,23},{8,72},{9,... | collective-permute-start | bytes 1572872 | tf_op jit(solution)/shard_map/ppermute | solution.py:316
  58.1 1.5 %collective-permute-start.5 = (bf16[4,512,128]{2,1,0:T(8,128)(2,1)}, bf16[4,512,128]{2,1,0:T(8,128)(2,1)}, u32[]{:S(2)}, u32[]{:S(2)}) collective-permute-start(bf16[4,512,128]{2,1,0:T(8,128)(2,1)} %sum_minor.1.rest_1_.a_ref), channel_id=1, source_target_pairs={{0,96},{1,25},{2,98},{3,27},{4,100},{5,29},{6,102},{7,31},{8,104},... | collective-permute-start | bytes 1572872 | tf_op jit(solution)/shard_map/ppermute | solution.py:316
  59.6 10.3 %all-to-all-done.1.gathered_ref = bf16[16,272,128]{2,1,0:T(8,128)(2,1)S(1)} async-done(((bf16[16,272,128]{2,1,0:T(8,128)(2,1)}), bf16[16,272,128]{2,1,0:T(8,128)(2,1)S(1)}, u32[]{:S(2)}, u32[]{:S(2)}) %all-to-all-start.1) | async-done | bytes 1114144 | tf_op jit(solution)/shard_map/all_to_all | solution.py:320
  69.9 0.0 copy-done.6
  69.9 2.8 %reduced_rows.1 = (bf16[2,128,128]{2,1,0:T(8,128)(2,1)S(1)}, bf16[16,256,128]{2,1,0:T(8,128)(2,1)}) custom-call(bf16[8,3,2,128,256]{4,3,2,1,0:T(8,128)(2,1)} %bitcast.21, bf16[16,272,128]{2,1,0:T(8,128)(2,1)S(1)} %all-to-all-done.1.gathered_ref, bf16[2,128,128]{2,1,0:T(8,128)(2,1)S(1)} %copy-done.6, bf16[4,512,128]{2,1,0:T(8,128)(2,1)} %sum_minor.1.rest_1_.a_ref), custom_call_target="tpu_custom_call" | custom-call | flops 30000001024 | bytes 1000 | tf_op jit(solution)/shard_map/reduced_rows/pallas_call | solution.py:134
  72.7 3.7 %all-to-all-start.2 = ((bf16[16,256,128]{2,1,0:T(8,128)(2,1)}), bf16[16,256,128]{2,1,0:T(8,128)(2,1)S(1)}, u32[]{:S(2)}, u32[]{:S(2)}) async-start(bf16[16,256,128]{2,1,0:T(8,128)(2,1)} %get-tuple-element.21), calls=%async_computation.2 | async-start | bytes 2097152 | tf_op jit(solution)/shard_map/all_to_all | solution.py:320
  76.4 0.0 collective-permute-done.3.b_ref
  76.4 1.9 %collective-permute-done.4.c_ref = bf16[4,512,128]{2,1,0:T(8,128)(2,1)} collective-permute-done((bf16[4,512,128]{2,1,0:T(8,128)(2,1)}, bf16[4,512,128]{2,1,0:T(8,128)(2,1)}, u32[]{:S(2)}, u32[]{:S(2)}) %collective-permute-start.4) | collective-permute-done | bytes 524320 | tf_op jit(solution)/shard_map/ppermute | solution.py:316
  78.3 0.0 collective-permute-done.5.d_ref
  78.3 2.4 %sum_major.1.rest_0_ = bf16[4,512,128]{2,1,0:T(8,128)(2,1)} custom-call(bf16[4,512,128]{2,1,0:T(8,128)(2,1)} %sum_minor.1.rest_1_.a_ref, bf16[4,512,128]{2,1,0:T(8,128)(2,1)S(1)} %collective-permute-done.3.b_ref, bf16[4,512,128]{2,1,0:T(8,128)(2,1)} %collective-permute-done.4.c_ref, bf16[4,512,128]{2,1,0:T(8,128)(2,1)} %collective-permute-done.5.d_ref, ...), custom_call_target="tpu_custom_call" | custom-call | flops 30000001024 | bytes 1000 | tf_op jit(solution)/shard_map/sum_major/pallas_call | solution.py:68
  80.7 1.5 %collective-permute-start.6 = (bf16[4,512,128]{2,1,0:T(8,128)(2,1)}, bf16[4,512,128]{2,1,0:T(8,128)(2,1)}, u32[]{:S(2)}, u32[]{:S(2)}) collective-permute-start(bf16[4,512,128]{2,1,0:T(8,128)(2,1)} %sum_major.1.rest_0_), channel_id=1, source_target_pairs={{0,8},{1,33},{2,10},{3,35},{4,12},{5,37},{6,14},{7,39},{8,16},{9,4... | collective-permute-start | bytes 1572872 | tf_op jit(solution)/shard_map/ppermute | solution.py:316
  82.2 2.6 %collective-permute-start.7 = (bf16[4,512,128]{2,1,0:T(8,128)(2,1)}, bf16[4,512,128]{2,1,0:T(8,128)(2,1)}, u32[]{:S(2)}, u32[]{:S(2)}) collective-permute-start(bf16[4,512,128]{2,1,0:T(8,128)(2,1)} %sum_major.1.rest_0_), channel_id=1, source_target_pairs={{0,16},{1,65},{2,18},{3,67},{4,20},{5,69},{6,22},{7,71},{8,24},{9,... | collective-permute-start | bytes 1572872 | tf_op jit(solution)/shard_map/ppermute | solution.py:316
  84.8 1.5 %collective-permute-start.8 = (bf16[4,512,128]{2,1,0:T(8,128)(2,1)}, bf16[4,512,128]{2,1,0:T(8,128)(2,1)}, u32[]{:S(2)}, u32[]{:S(2)}) collective-permute-start(bf16[4,512,128]{2,1,0:T(8,128)(2,1)} %sum_major.1.rest_0_), channel_id=1, source_target_pairs={{0,24},{1,97},{2,26},{3,99},{4,28},{5,101},{6,30},{7,103},{8,0},{9... | collective-permute-start | bytes 1572872 | tf_op jit(solution)/shard_map/ppermute | solution.py:316
  86.3 7.1 %all-to-all-done.2.gathered_ref = bf16[16,256,128]{2,1,0:T(8,128)(2,1)S(1)} async-done(((bf16[16,256,128]{2,1,0:T(8,128)(2,1)}), bf16[16,256,128]{2,1,0:T(8,128)(2,1)S(1)}, u32[]{:S(2)}, u32[]{:S(2)}) %all-to-all-start.2) | async-done | bytes 1048608 | tf_op jit(solution)/shard_map/all_to_all | solution.py:320
  93.4 2.9 %last_rows.1 = (bf16[2,128,128]{2,1,0:T(8,128)(2,1)S(1)}, bf16[16,256,128]{2,1,0:T(8,128)(2,1)}) custom-call(bf16[8,3,2,128,256]{4,3,2,1,0:T(8,128)(2,1)} %bitcast.22, bf16[16,256,128]{2,1,0:T(8,128)(2,1)S(1)} %all-to-all-done.2.gathered_ref, bf16[4,512,128]{2,1,0:T(8,128)(2,1)} %sum_major.1.rest_0_), custom_call_target="tpu_custom_call" | custom-call | flops 30000001024 | bytes 1000 | tf_op jit(solution)/shard_map/last_rows/pallas_call | solution.py:134
  96.3 0.0 copy-start.3
  96.3 8.1 %all-to-all-start.3 = ((bf16[16,256,128]{2,1,0:T(8,128)(2,1)}), bf16[16,256,128]{2,1,0:T(8,128)(2,1)S(1)}, u32[]{:S(2)}, u32[]{:S(2)}) async-start(bf16[16,256,128]{2,1,0:T(8,128)(2,1)} %get-tuple-element.26), calls=%async_computation.3 | async-start | bytes 2097152 | tf_op jit(solution)/shard_map/all_to_all | solution.py:320
  104.4 0.0 collective-permute-done.6.rest_1_
  104.4 1.5 %collective-permute-done.7.rest_2_ = bf16[4,512,128]{2,1,0:T(8,128)(2,1)} collective-permute-done((bf16[4,512,128]{2,1,0:T(8,128)(2,1)}, bf16[4,512,128]{2,1,0:T(8,128)(2,1)}, u32[]{:S(2)}, u32[]{:S(2)}) %collective-permute-start.7) | collective-permute-done | bytes 524320 | tf_op jit(solution)/shard_map/ppermute | solution.py:316
  105.9 0.0 collective-permute-done.8.rest_3_
  105.9 0.0 copy-done.3
  105.9 7.4 %first_loads.1 = (f32[4096,256]{1,0:T(8,128)}, s32[1,2048]{1,0:T(1,128)S(1)}, f32[1,2048]{1,0:T(1,128)S(1)}) custom-call(s32[3]{0:T(128)S(1)} %copy-done.3, bf16[16,272,128]{2,1,0:T(8,128)(2,1)S(1)} %all-to-all-done.1.gathered_ref, bf16[4,512,128]{2,1,0:T(8,128)(2,1)} %sum_major.1.rest_0_, bf16[4,512,128]{2,1,0:T(8,128)(2,1)} %collective-permute-done.6.rest_1_, ...), custom_call_target="tpu_custom_call" | custom-call | flops 30000001024 | bytes 1000 | tf_op jit(solution)/shard_map/first_loads/pallas_call | solution.py:213
  113.3 0.7 pad_maximum_fusion.1
  114.0 3.2 %all-to-all-done.3.gathered_ref = bf16[16,256,128]{2,1,0:T(8,128)(2,1)S(1)} async-done(((bf16[16,256,128]{2,1,0:T(8,128)(2,1)}), bf16[16,256,128]{2,1,0:T(8,128)(2,1)S(1)}, u32[]{:S(2)}, u32[]{:S(2)}) %all-to-all-start.3) | async-done | bytes 1048608 | tf_op jit(solution)/shard_map/all_to_all | solution.py:320
  117.2 6.8 %all_loads.1.loads_ref = bf16[4096,256]{1,0:T(8,128)(2,1)S(1)} custom-call(s32[1,2048]{1,0:T(1,128)S(1)} %get-tuple-element.24.ids, f32[1,2048]{1,0:T(1,128)S(1)} %get-tuple-element.25.weights, bf16[16,256,128]{2,1,0:T(8,128)(2,1)S(1)} %all-to-all-done.3.gathered_ref, f32[4096,256]{1,0:T(8,128)} %get-tuple-element.27.first_ref), custom_call_target="tpu_custom_call" | custom-call | tf_op jit(solution)/shard_map/all_loads/pallas_call | solution.py:253
  124.0 2.7 %all-gather.7.cloned.1.call-done = bf16[16,1024,512]{2,1,0:T(8,128)(2,1)} async-done(((bf16[2,1024,512]{2,1,0:T(8,128)(2,1)}), bf16[16,1024,512]{2,1,0:T(8,128)(2,1)}) %all-gather.7.cloned.1.call-update) | async-done | bytes 16777232 | tf_op jit(solution)/shard_map/all_gather | solution.py:344
  126.7 8.2 %stress.1 = bf16[2,1024,128]{2,1,0:T(8,128)(2,1)} custom-call(bf16[4096,256]{1,0:T(8,128)(2,1)S(1)} %all_loads.1.loads_ref, bf16[8,2,1024,512]{3,2,1,0:T(8,128)(2,1)} %bitcast.15), custom_call_target="tpu_custom_call" | custom-call | tf_op jit(solution)/shard_map/stress/pallas_call | solution.py:293
  (4 shorter events, 0.0 us)
Async XLA Ops:
  7.2 2.7 %copy-start.9 = (bf16[2,128,128]{2,1,0:T(8,128)(2,1)S(1)}, bf16[2,128,128]{2,1,0:T(8,128)(2,1)}, u32[]{:S(2)}) copy-start(bf16[2,128,128]{2,1,0:T(8,128)(2,1)} %param.11) | copy-start | bytes 196612
  7.2 32.8 %all-gather.5.cloned.1.call-start = ((), (), s32[]{:S(2)}) async-start(), calls=%async_computation.4 | async-start | bytes 3538944 | tf_op jit(solution)/shard_map/all_gather | solution.py:343
  9.1 117.6 %all-gather.7.cloned.1.call-start = ((), (), s32[]{:S(2)}) async-start(), calls=%async_computation.5 | async-start | bytes 18874368 | tf_op jit(solution)/shard_map/all_gather | solution.py:344
  9.9 9.4 %copy-start.10 = (bf16[3072]{0:T(1024)(128)(2,1)S(1)}, bf16[3072]{0:T(1024)(128)(2,1)}, u32[]{:S(2)}) copy-start(bf16[3072]{0:T(1024)(128)(2,1)} %param.18) | copy-start | bytes 18436
  9.9 9.5 %copy-start = (bf16[2,3072,128]{2,1,0:T(8,128)(2,1)S(1)}, bf16[2,3072,128]{2,1,0:T(8,128)(2,1)}, u32[]{:S(2)}) copy-start(bf16[2,3072,128]{2,1,0:T(8,128)(2,1)} %earlier_ref.1) | copy-start | bytes 4718596
  9.9 9.5 %copy-start.1 = (s32[3072]{0:T(1024)S(1)}, s32[3072]{0:T(1024)}, u32[]{:S(2)}) copy-start(s32[3072]{0:T(1024)} %param.17) | copy-start | bytes 36868
  11.1 28.9 %copy-start.7 = (s32[2,128]{1,0:T(2,128)S(1)}, s32[2,128]{1,0:T(2,128)}, u32[]{:S(2)}) copy-start(s32[2,128]{1,0:T(2,128)} %rest_0_.2) | copy-start | bytes 3076
  11.1 28.9 %copy-start.8 = (bf16[2,128]{1,0:T(2,128)(2,1)S(1)}, bf16[2,128]{1,0:T(2,128)(2,1)}, u32[]{:S(2)}) copy-start(bf16[2,128]{1,0:T(2,128)(2,1)} %rest_1_.1) | copy-start | bytes 1540
  11.1 25.9 %all-to-all-start = ((bf16[16,256,128]{2,1,0:T(8,128)(2,1)}), bf16[16,256,128]{2,1,0:T(8,128)(2,1)S(1)}, u32[]{:S(2)}, u32[]{:S(2)}) async-start(bf16[16,256,128]{2,1,0:T(8,128)(2,1)} %broadcast_in_dim.14), calls=%async_computation | async-start | bytes 2097152 | tf_op jit(solution)/shard_map/all_to_all | solution.py:320
  19.3 13.8 %copy-start.2 = (s32[3]{0:T(128)}, s32[3]{0:T(128)S(1)}, u32[]{:S(2)}) copy-start(s32[3]{0:T(128)S(1)} %pad_add_fusion.place_ref) | copy-start | bytes 40
  27.8 0.8 copy-start.4
  28.6 22.3 %collective-permute-start = (bf16[4,512,128]{2,1,0:T(8,128)(2,1)}, bf16[4,512,128]{2,1,0:T(8,128)(2,1)}, u32[]{:S(2)}, u32[]{:S(2)}) collective-permute-start(bf16[4,512,128]{2,1,0:T(8,128)(2,1)} %get-tuple-element.18), channel_id=1, source_target_pairs={{0,8},{1,33},{2,10},{3,35},{4,12},{5,37},{6,14},{7,39},{8,16},{9,4... | collective-permute-start | bytes 1572872 | tf_op jit(solution)/shard_map/ppermute | solution.py:316
  30.5 20.4 %collective-permute-start.1 = (bf16[4,512,128]{2,1,0:T(8,128)(2,1)}, bf16[4,512,128]{2,1,0:T(8,128)(2,1)}, u32[]{:S(2)}, u32[]{:S(2)}) collective-permute-start(bf16[4,512,128]{2,1,0:T(8,128)(2,1)} %get-tuple-element.19), channel_id=1, source_target_pairs={{0,16},{1,65},{2,18},{3,67},{4,20},{5,69},{6,22},{7,71},{8,24},{9,... | collective-permute-start | bytes 1572872 | tf_op jit(solution)/shard_map/ppermute | solution.py:316
  33.1 17.7 %collective-permute-start.2 = (bf16[4,512,128]{2,1,0:T(8,128)(2,1)}, bf16[4,512,128]{2,1,0:T(8,128)(2,1)}, u32[]{:S(2)}, u32[]{:S(2)}) collective-permute-start(bf16[4,512,128]{2,1,0:T(8,128)(2,1)} %get-tuple-element.20), channel_id=1, source_target_pairs={{0,24},{1,97},{2,26},{3,99},{4,28},{5,101},{6,30},{7,103},{8,0},{9... | collective-permute-start | bytes 1572872 | tf_op jit(solution)/shard_map/ppermute | solution.py:316
  40.0 1.0 copy-start.5
  43.9 26.0 %all-to-all-start.1 = ((bf16[16,272,128]{2,1,0:T(8,128)(2,1)}), bf16[16,272,128]{2,1,0:T(8,128)(2,1)S(1)}, u32[]{:S(2)}, u32[]{:S(2)}) async-start(bf16[16,272,128]{2,1,0:T(8,128)(2,1)} %get-tuple-element.17), calls=%async_computation.1 | async-start | bytes 2228224 | tf_op jit(solution)/shard_map/all_to_all | solution.py:320
  50.8 19.0 %copy-start.6 = (bf16[2,128,128]{2,1,0:T(8,128)(2,1)S(1)}, bf16[2,128,128]{2,1,0:T(8,128)(2,1)}, u32[]{:S(2)}) copy-start(bf16[2,128,128]{2,1,0:T(8,128)(2,1)} %rest_0_.3) | copy-start | bytes 196612
  53.5 22.9 %collective-permute-start.3 = (bf16[4,512,128]{2,1,0:T(8,128)(2,1)}, bf16[4,512,128]{2,1,0:T(8,128)(2,1)S(1)}, u32[]{:S(2)}, u32[]{:S(2)}) collective-permute-start(bf16[4,512,128]{2,1,0:T(8,128)(2,1)} %sum_minor.1.rest_1_.a_ref), channel_id=1, source_target_pairs={{0,32},{1,9},{2,34},{3,11},{4,36},{5,13},{6,38},{7,15},{8,40},{9,1... | collective-permute-start | bytes 1572872 | tf_op jit(solution)/shard_map/ppermute | solution.py:316
  55.4 22.9 %collective-permute-start.4 = (bf16[4,512,128]{2,1,0:T(8,128)(2,1)}, bf16[4,512,128]{2,1,0:T(8,128)(2,1)}, u32[]{:S(2)}, u32[]{:S(2)}) collective-permute-start(bf16[4,512,128]{2,1,0:T(8,128)(2,1)} %sum_minor.1.rest_1_.a_ref), channel_id=1, source_target_pairs={{0,64},{1,17},{2,66},{3,19},{4,68},{5,21},{6,70},{7,23},{8,72},{9,... | collective-permute-start | bytes 1572872 | tf_op jit(solution)/shard_map/ppermute | solution.py:316
  58.1 20.2 %collective-permute-start.5 = (bf16[4,512,128]{2,1,0:T(8,128)(2,1)}, bf16[4,512,128]{2,1,0:T(8,128)(2,1)}, u32[]{:S(2)}, u32[]{:S(2)}) collective-permute-start(bf16[4,512,128]{2,1,0:T(8,128)(2,1)} %sum_minor.1.rest_1_.a_ref), channel_id=1, source_target_pairs={{0,96},{1,25},{2,98},{3,27},{4,100},{5,29},{6,102},{7,31},{8,104},... | collective-permute-start | bytes 1572872 | tf_op jit(solution)/shard_map/ppermute | solution.py:316
  72.7 20.7 %all-to-all-start.2 = ((bf16[16,256,128]{2,1,0:T(8,128)(2,1)}), bf16[16,256,128]{2,1,0:T(8,128)(2,1)S(1)}, u32[]{:S(2)}, u32[]{:S(2)}) async-start(bf16[16,256,128]{2,1,0:T(8,128)(2,1)} %get-tuple-element.21), calls=%async_computation.2 | async-start | bytes 2097152 | tf_op jit(solution)/shard_map/all_to_all | solution.py:320
  80.7 23.7 %collective-permute-start.6 = (bf16[4,512,128]{2,1,0:T(8,128)(2,1)}, bf16[4,512,128]{2,1,0:T(8,128)(2,1)}, u32[]{:S(2)}, u32[]{:S(2)}) collective-permute-start(bf16[4,512,128]{2,1,0:T(8,128)(2,1)} %sum_major.1.rest_0_), channel_id=1, source_target_pairs={{0,8},{1,33},{2,10},{3,35},{4,12},{5,37},{6,14},{7,39},{8,16},{9,4... | collective-permute-start | bytes 1572872 | tf_op jit(solution)/shard_map/ppermute | solution.py:316
  82.2 23.7 %collective-permute-start.7 = (bf16[4,512,128]{2,1,0:T(8,128)(2,1)}, bf16[4,512,128]{2,1,0:T(8,128)(2,1)}, u32[]{:S(2)}, u32[]{:S(2)}) collective-permute-start(bf16[4,512,128]{2,1,0:T(8,128)(2,1)} %sum_major.1.rest_0_), channel_id=1, source_target_pairs={{0,16},{1,65},{2,18},{3,67},{4,20},{5,69},{6,22},{7,71},{8,24},{9,... | collective-permute-start | bytes 1572872 | tf_op jit(solution)/shard_map/ppermute | solution.py:316
  84.8 21.1 %collective-permute-start.8 = (bf16[4,512,128]{2,1,0:T(8,128)(2,1)}, bf16[4,512,128]{2,1,0:T(8,128)(2,1)}, u32[]{:S(2)}, u32[]{:S(2)}) collective-permute-start(bf16[4,512,128]{2,1,0:T(8,128)(2,1)} %sum_major.1.rest_0_), channel_id=1, source_target_pairs={{0,24},{1,97},{2,26},{3,99},{4,28},{5,101},{6,30},{7,103},{8,0},{9... | collective-permute-start | bytes 1572872 | tf_op jit(solution)/shard_map/ppermute | solution.py:316
  96.3 9.6 %copy-start.3 = (s32[3]{0:T(128)S(1)}, s32[3]{0:T(128)}, u32[]{:S(2)}) copy-start(s32[3]{0:T(128)} %copy-done.2) | copy-start | bytes 40
  96.3 20.9 %all-to-all-start.3 = ((bf16[16,256,128]{2,1,0:T(8,128)(2,1)}), bf16[16,256,128]{2,1,0:T(8,128)(2,1)S(1)}, u32[]{:S(2)}, u32[]{:S(2)}) async-start(bf16[16,256,128]{2,1,0:T(8,128)(2,1)} %get-tuple-element.26), calls=%async_computation.3 | async-start | bytes 2097152 | tf_op jit(solution)/shard_map/all_to_all | solution.py:320
Sparse Core Ops, SparseCore 0:
  9.7 30.2 all-gather.4
  41.7 84.9 all-gather.6

commit v4 on v3

--- a/solution.py
+++ b/solution.py
@@ -13,6 +13,8 @@
 BF16 = jnp.bfloat16
 F32 = jnp.float32
 COST = pl.CostEstimate(flops=30_000_000_000, bytes_accessed=1000, transcendentals=0)
+SHORT = pl.CostEstimate(flops=6_000_000_000, bytes_accessed=1000, transcendentals=0)
+BRIEF = pl.CostEstimate(flops=1_000_000_000, bytes_accessed=1000, transcendentals=0)
 PARAMS = pltpu.CompilerParams(vmem_limit_bytes=20 * 2**20)
 
 
@@ -76,6 +78,28 @@
     )(*parts, tie)
 
 
+def pack_factors_kernel(a_ref, b_ref, c_ref, d_ref, tie_ref, *outs):
+    for k, value_ref in enumerate((a_ref, b_ref, c_ref, d_ref)):
+        outs[k // 2][k % 2] = value_ref[0]
+        outs[2][k] = value_ref[1]
+        outs[3][k] = value_ref[2]
+
+
+def pack_factors(values, tie):
+    vmem = pl.BlockSpec(memory_space=pltpu.VMEM)
+    return pl.pallas_call(
+        pack_factors_kernel,
+        out_shape=[
+            jax.ShapeDtypeStruct((count, *values[0].shape[1:]), BF16) for count in (2, 2, 4, 4)
+        ],
+        in_specs=[vmem] * 4 + [pl.BlockSpec(memory_space=pl.ANY)],
+        out_specs=[vmem] * 4,
+        compiler_params=PARAMS,
+        cost_estimate=SHORT,
+        name="pack_factors",
+    )(*values, tie)
+
+
 def send_copies(source, copies_ref, sems):
     copies = [
         pltpu.make_async_copy(source, copies_ref.at[k], sems.at[k]) for k in range(ROWS)
@@ -86,16 +110,31 @@
         copy.wait()
 
 
-def rows_kernel(factors_ref, gathered_ref, *rest, pick, base, extra, ties):
-    rest = list(rest)
+def rows_kernel(*rest, parts, base, extra, ties):
+    factor_refs, gathered_ref, rest = rest[:parts], rest[parts], list(rest[parts + 1 :])
     base_ref = rest.pop(0) if base else None
     ids_ref, weights_ref = (rest.pop(0), rest.pop(0)) if extra else (None, None)
-    out_ref, copies_ref, factor, side, send, notes, factor_sem, sems = rest[ties:]
-    factor_copy = pltpu.make_async_copy(factors_ref.at[:, pick], factor, factor_sem)
-    factor_copy.start()
-    read_panels(gathered_ref, side)
+    out_ref, copies_ref, factor, side, send, notes, factor_sems, sems = rest[ties:]
+    size = COLS // parts
+    factor_copies = [
+        pltpu.make_async_copy(part_ref, factor.at[pl.ds(k * size, size)], factor_sems.at[k])
+        for k, part_ref in enumerate(factor_refs)
+    ]
+    for copy in factor_copies:
+        copy.start()
+    col = lax.axis_index("col")
+    core = col % 2
+    for block in range(COLS):
+        chip = (col // 2 + 4 - block % 4) % 4
+        column = chip * 2 + (core if block < 4 else 1 - core)
+        for half in range(2):
+            source = column * 2 + half
+            rows = slice(block * 256 + half * 128, block * 256 + (half + 1) * 128)
+            side[rows, :128] = gathered_ref[source, :128]
+            side[rows, 128:] = gathered_ref[source, 128:256]
     total = jnp.zeros((256, 256), F32)
-    factor_copy.wait()
+    for copy in factor_copies:
+        copy.wait()
     for block in range(COLS):
         part = side[block * 256 : (block + 1) * 256]
         left = factor[block].reshape(256, 256)
@@ -121,20 +160,20 @@
     send_copies(send, copies_ref, sems)
 
 
-def rows_product(name, factors, pick, gathered, base=None, extra=None, ties=()):
+def rows_product(name, factors, gathered, base=None, extra=None, ties=(), cost=COST):
     vmem = pl.BlockSpec(memory_space=pltpu.VMEM)
     hbm = pl.BlockSpec(memory_space=pltpu.HBM)
     operands = [gathered]
     operands += [] if base is None else [base]
     operands += [] if extra is None else extra
-    specs = [hbm] + [vmem] * len(operands)
+    specs = [hbm] * len(factors) + [vmem] * len(operands)
     specs += [pl.BlockSpec(memory_space=pl.ANY)] * len(ties)
     height = 256 if extra is None else 272
     shapes = [jax.ShapeDtypeStruct((2, 128, 128), BF16), pltpu.HBM((ROWS, height, 128), BF16)]
     return pl.pallas_call(
         functools.partial(
             rows_kernel,
-            pick=pick,
+            parts=len(factors),
             base=base is not None,
             extra=extra is not None,
             ties=len(ties),
@@ -147,13 +186,17 @@
             pltpu.VMEM((2048, 256), BF16),
             pltpu.VMEM((height, 128), BF16),
             pltpu.VMEM((16, 128), F32),
-            pltpu.SemaphoreType.DMA,
+            pltpu.SemaphoreType.DMA((4,)),
             pltpu.SemaphoreType.DMA((ROWS,)),
         ],
         compiler_params=PARAMS,
-        cost_estimate=COST,
+        cost_estimate=cost,
         name=name,
-    )(pltpu.with_memory_space_constraint(factors, pltpu.HBM), *operands, *ties)
+    )(
+        *[pltpu.with_memory_space_constraint(part, pltpu.HBM) for part in factors],
+        *operands,
+        *ties,
+    )
 
 
 def panel_loads(side, ids, weights, first, tile, chunk):
@@ -193,7 +236,7 @@
     copies = []
     for j in range(4):
         old_copies[j].wait()
-        minor = (place_ref[1] - j + 4) % 4
+        minor = (place_ref[1] + j) % 4
         for major in range(4):
             block = (major * 4 + minor) + place_ref[2] * 3 * (minor - major)
             rows = pl.ds(pl.multiple_of(block * 256, 256), 256)
@@ -235,55 +278,62 @@
     )(place, gathered, *old)
 
 
-def all_loads_kernel(ids, weights, gathered_ref, first_ref, out_ref, side, first, total, sem):
-    copy = pltpu.make_async_copy(first_ref, first, sem)
-    copy.start()
+def all_loads_kernel(
+    ids, weights, gathered_ref, first_ref, maps_ref, out_ref, held_ref, side, first, total, sem, sems
+):
+    first_copy = pltpu.make_async_copy(first_ref, first, sem)
+    first_copy.start()
+    copies = [
+        pltpu.make_async_copy(maps_ref.at[k], held_ref.at[k], sems.at[k]) for k in range(COLS)
+    ]
+    for copy in copies:
+        copy.start()
     read_panels(gathered_ref, side)
     for start in range(0, PATCHES, 1024):
         total[start : start + 1024] = panel_loads(side, ids, weights, start, 1024, 512)
-    copy.wait()
+    first_copy.wait()
     for start in range(0, PATCHES, 256):
         rows = slice(start, start + 256)
         out_ref[rows] = (first[rows] + total[rows]).astype(BF16)
-
-
-def all_loads(ids, weights, gathered, first):
+    for copy in copies:
+        copy.wait()
+
+
+def all_loads(ids, weights, gathered, first, maps):
     vmem = pl.BlockSpec(memory_space=pltpu.VMEM)
     hbm = pl.BlockSpec(memory_space=pltpu.HBM)
     return pl.pallas_call(
         all_loads_kernel,
-        out_shape=jax.ShapeDtypeStruct((PATCHES, 256), BF16),
-        in_specs=[vmem] * 3 + [hbm],
-        out_specs=vmem,
+        out_shape=(pltpu.VMEM((PATCHES, 256), BF16), pltpu.VMEM(maps.shape, BF16)),
+        in_specs=[vmem] * 3 + [hbm] * 2,
+        out_specs=(vmem, vmem),
         scratch_shapes=[
             pltpu.VMEM((2048, 256), BF16),
             pltpu.VMEM((PATCHES, 256), F32),
             pltpu.VMEM((PATCHES, 256), F32),
             pltpu.SemaphoreType.DMA,
+            pltpu.SemaphoreType.DMA((COLS,)),
         ],
         compiler_params=PARAMS,
         name="all_loads",
-    )(ids, weights, gathered, pltpu.with_memory_space_constraint(first, pltpu.HBM))
-
-
-def stress_kernel(loads_ref, maps_ref, out_ref, held, sems):
-    copies = []
-    for step in range(4):
-        rows = pl.ds(step * 256, 256)
-        for block in range(COLS):
-            source, target = maps_ref.at[block, :, rows], held.at[block, :, rows]
-            copies.append(pltpu.make_async_copy(source, target, sems.at[step, block]))
-            copies[-1].start()
-    for step in range(4):
-        for copy in copies[step * COLS : (step + 1) * COLS]:
-            copy.wait()
-        rows = slice(step * 256, (step + 1) * 256)
-        real = jnp.zeros((256, 256), F32)
-        imag = jnp.zeros((256, 256), F32)
+    )(
+        ids,
+        weights,
+        gathered,
+        pltpu.with_memory_space_constraint(first, pltpu.HBM),
+        pltpu.with_memory_space_constraint(maps, pltpu.HBM),
+    )
+
+
+def stress_kernel(loads_ref, maps_ref, out_ref):
+    for first in range(0, 1024, 512):
+        rows = slice(first, first + 512)
+        real = jnp.zeros((512, 256), F32)
+        imag = jnp.zeros((512, 256), F32)
         for block in range(COLS):
             part = loads_ref[block * 512 : (block + 1) * 512]
-            real += jnp.dot(held[block, 0, rows], part, preferred_element_type=F32)
-            imag += jnp.dot(held[block, 1, rows], part, preferred_element_type=F32)
+            real += jnp.dot(maps_ref[block, 0, rows], part, preferred_element_type=F32)
+            imag += jnp.dot(maps_ref[block, 1, rows], part, preferred_element_type=F32)
         out_ref[0, rows] = (real[:, :128] - imag[:, 128:]).astype(BF16)
         out_ref[1, rows] = (real[:, 128:] + imag[:, :128]).astype(BF16)
 
@@ -293,22 +343,30 @@
     return pl.pallas_call(
         stress_kernel,
         out_shape=jax.ShapeDtypeStruct((2, 1024, 128), BF16),
-        in_specs=[vmem, pl.BlockSpec(memory_space=pltpu.HBM)],
+        in_specs=[vmem] * 2,
         out_specs=vmem,
-        scratch_shapes=[
-            pltpu.VMEM((COLS, 2, 1024, 512), BF16),
-            pltpu.SemaphoreType.DMA((4, COLS)),
-        ],
-        compiler_params=pltpu.CompilerParams(vmem_limit_bytes=32 * 2**20),
+        compiler_params=PARAMS,
         name="stress",
-    )(loads, pltpu.with_memory_space_constraint(maps, pltpu.HBM))
+    )(
+        pltpu.with_memory_space_constraint(loads, pltpu.VMEM),
+        pltpu.with_memory_space_constraint(maps, pltpu.VMEM),
+    )
+
+
+def along_y(value, hop):
+    pairs = [(i, (i // 2 + hop) % 4 * 2 + i % 2) for i in range(COLS)]
+    return lax.ppermute(value, "col", pairs)
+
+
+def other_core(value):
+    return lax.ppermute(value, "col", [(i, i ^ 1) for i in range(COLS)])
 
 
 def along_axis(value, hop, major):
     pairs = []
     for index in range(ROWS * COLS):
         x, z, rest = index // 32, index // 8 % 4, index % 8
-        if major == (rest % 2 == 0):
+        if major == (rest % 2 == 1):
             x = (x + hop) % 4
         else:
             z = (z + hop) % 4
@@ -337,30 +395,35 @@
     col = lax.axis_index("col")
     core = col % 2
     x, z = row // 4, row % 4
-    place = jnp.stack([x + core * (z - x), z + core * (x - z), core]).astype(jnp.int32)
-
-
-    factors = lax.all_gather(jnp.stack([inv_first, coupling, inv_last]), "col")
+    swap = 1 - core
+    place = jnp.stack([x + swap * (z - x), z + swap * (x - z), swap]).astype(jnp.int32)
+
+
+    rhs_all = to_rows(jnp.broadcast_to(rhs_first.reshape(1, 256, 128), (ROWS, 256, 128)))
     maps = lax.all_gather(stress_map, "col")
-    rhs_all = to_rows(jnp.broadcast_to(rhs_first.reshape(1, 256, 128), (ROWS, 256, 128)))
+    factors = jnp.stack([inv_first, coupling, inv_last])
+    factors = [factors] + [along_y(factors, hop) for hop in (1, 2, 3)]
     old = old_loads(place, patch_old[None], weight_old[None], earlier)
+    own = list(pack_factors(factors, old[0]))
+    other = [other_core(value) for value in own]
+    factors = [own[:2] + other[:2], [own[2], other[2]], [own[3], other[3]]]
     x_first, copies = rows_product(
-        "first_rows", factors, 0, rhs_all, extra=[patch_new, weight_new], ties=(old[0],)
+        "first_rows", factors[0], rhs_all, extra=[patch_new, weight_new], cost=BRIEF
     )
     x_first_all = to_rows(copies)
     old = [old[0]] + [along_axis(old[hop], hop, False) for hop in (1, 2, 3)]
     old = sum_loads("sum_minor", old, x_first)
     reduced, copies = rows_product(
-        "reduced_rows", factors, 1, x_first_all, base=rhs_last, ties=(old,)
+        "reduced_rows", factors[1], x_first_all, base=rhs_last, ties=(old,)
     )
     reduced_all = to_rows(copies)
-    old = [old] + [along_axis(old, hop, True) for hop in (1, 2, 3)]
+    old = [old] + [along_axis(old, hop, True) for hop in (3, 2, 1)]
     old = sum_loads("sum_major", old, reduced)
-    x_last, copies = rows_product("last_rows", factors, 2, reduced_all, ties=(old,))
+    x_last, copies = rows_product("last_rows", factors[2], reduced_all, ties=(old,))
     x_last_all = to_rows(copies)
-    old = [old] + [along_axis(old, hop, False) for hop in (1, 2, 3)]
+    old = [old] + [along_axis(old, hop, False) for hop in (3, 2, 1)]
     loads, ids, weights = first_loads(place, x_first_all, old)
-    stress_rao = stress(all_loads(ids, weights, x_last_all, loads), maps)
+    stress_rao = stress(*all_loads(ids, weights, x_last_all, loads, maps))
     return (jnp.stack([x_first, x_last]), stress_rao)
 
 

time: 144 us -> 139 us (0.965)
  waiting for transfers between devices: 32.8 us -> 27.3 us
  starting transfers between devices: 44.6 us -> 47.7 us
  other arithmetic: 2.61 us -> 0.79 us
    ppermute x0 -> x7, starting transfers between devices: none -> 5.63 us  [the longest x3 4.77 us: along_y(): return lax.ppermute(value, 'col', pairs)]
    pallas_call x1, Pallas kernels: 8.24 us -> 5.28 us  [stress(): pl.pallas_call(stress_kernel, out_shape=jax.ShapeDtypeStruct((2, 1024, 12...]
    all_gather x1 -> x0, waiting for transfers between devices: 2.94 us -> none  [on_device(): factors = lax.all_gather(jnp.stack([inv_first, coupling, inv_last]), 'col')]
    all_gather x1, waiting for transfers between devices: 2.73 us -> 0.01 us  [on_device(): maps = lax.all_gather(stress_map, 'col')]
    all_to_all x4, starting transfers between devices: 26.9 us -> 24.2 us  [to_rows(): return lax.all_to_all(copies, 'row', 0, 0, tiled=True)]
    all_to_all x4, waiting for transfers between devices: 23 us -> 20.9 us  [to_rows(): return lax.all_to_all(copies, 'row', 0, 0, tiled=True)]
    pallas_call x4 -> x5, Pallas kernels: 15.3 us -> 17.1 us  [the longest x3 8.48 us: rows_product(): pl.pallas_call(functools.partial(rows_kernel, parts=len(factors), base=ba...]
    another operation x2, other arithmetic: 1.94 us -> 0.13 us  [the longest x1 0.08 us: on_device(): jnp.stack([x + swap * (z - x), z + swap * (x - z), swap]).astype(jnp.int32)]
  transfers between devices with their start and end apart: 15 -> 21, of which waited for: 8 -> 8; matrix products, arithmetic and copies ran while one was open for 1% -> 1% of each run, Pallas kernels for 26% -> 22%
where the time goes in v4:
time: 139 us; the launch traced here: 137 us
  starting transfers between devices  47.7 us (34%)
  Pallas kernels  43.2 us (31%)
  waiting for transfers between devices  27.3 us (20%)
  between operations  14.4 us (10%)
  local copies, waits for them, and re-layouts  3.96 us (3%)
    all_to_all x4, starting transfers between devices, to_rows(): return lax.all_to_all(copies, 'row', 0, 0, tiled=True)  24.2 us
    all_to_all x4, waiting for transfers between devices, to_rows(): return lax.all_to_all(copies, 'row', 0, 0, tiled=True)  20.9 us
    ppermute x9, starting transfers between devices, along_axis(): return lax.ppermute(value, ('row', 'col'), pairs)  17.8 us
    pallas_call x3, Pallas kernels, rows_product(): pl.pallas_call(functools.partial(rows_kernel, parts=len(factors), base=ba...  8.48 us
    pallas_call x1, Pallas kernels, old_loads(): pl.pallas_call(functools.partial(old_loads_kernel, chunk=512), out_shape=...  8.38 us
    pallas_call x1, Pallas kernels, all_loads(): pl.pallas_call(all_loads_kernel, out_shape=(pltpu.VMEM((PATCHES, 256), BF...  7.4 us
    pallas_call x1, Pallas kernels, first_loads(): pl.pallas_call(first_loads_kernel, out_shape=(pltpu.HBM((PATCHES, 256), F...  7.37 us
    pallas_call x1, Pallas kernels, stress(): pl.pallas_call(stress_kernel, out_shape=jax.ShapeDtypeStruct((2, 1024, 12...  5.28 us
  transfers between devices with their start and end apart: 21, of which 8 were waited for; matrix products, arithmetic and copies ran while one was open for 1% of the time, Pallas kernels for 22%

profile of v4, /device:TPU:0, one launch (start us, length us, event | category | flops | bytes accessed | tf_op | source)
XLA Modules:
  0.0 137.3 jit_solution(2818209806098692025)
XLA Ops:
  7.2 0.0 all-gather.3.cloned.1.call-start
  7.3 0.7 all-gather.3.cloned.1.call-update
  8.0 0.1 copy-done.13
  8.1 0.1 copy-done.14
  8.1 0.1 copy-done.15
  8.2 3.2 %collective-permute-start.2 = (bf16[3,2,128,256]{3,2,1,0:T(8,128)(2,1)S(1)}, bf16[3,2,128,256]{3,2,1,0:T(8,128)(2,1)S(1)}, u32[]{:S(2)}, u32[]{:S(2)}) collective-permute-start(bf16[3,2,128,256]{3,2,1,0:T(8,128)(2,1)S(1)} %pad_maximum_fusion.a_ref), channel_id=1, source_target_pairs={{0,6},{1,7},{2,0},{3,1},{4,2},{5,3},{6,4},{7,5},{8,14},{9,15},{10,... | collective-permute-start | bytes 1179656 | tf_op jit(solution)/shard_map/ppermute | solution.py:358
  11.4 0.6 collective-permute-start.1
  12.0 1.0 collective-permute-start
  13.0 1.2 broadcast_in_dim.16
  14.2 7.9 %all-to-all-start = ((bf16[16,256,128]{2,1,0:T(8,128)(2,1)}), bf16[16,256,128]{2,1,0:T(8,128)(2,1)S(1)}, u32[]{:S(2)}, u32[]{:S(2)}) async-start(bf16[16,256,128]{2,1,0:T(8,128)(2,1)} %broadcast_in_dim.16), calls=%async_computation | async-start | bytes 2097152 | tf_op jit(solution)/shard_map/all_to_all | solution.py:378
  22.2 0.1 pad_add_fusion.place_ref
  22.2 0.0 copy-done.1
  22.3 8.4 %old_loads.1 = (bf16[4,512,128]{2,1,0:T(8,128)(2,1)S(1)}, bf16[4,512,128]{2,1,0:T(8,128)(2,1)}, bf16[4,512,128]{2,1,0:T(8,128)(2,1)}, bf16[4,512,128]{2,1,0:T(8,128)(2,1)}) custom-call(s32[3]{0:T(128)S(1)} %pad_add_fusion.place_ref, s32[1,3072]{1,0:T(1,128)S(1)} %bitcast.13, bf16[1,3072]{1,0:T(2,128)(2,1)S(1)} %broadcast_in_dim.14.weights_ref, ...), custom_call_target="tpu_custom_call" | custom-call | tf_op jit(solution)/shard_map/old_loads/pallas_call | solution.py:50
  30.6 1.9 %collective-permute-start.7 = (bf16[4,512,128]{2,1,0:T(8,128)(2,1)}, bf16[4,512,128]{2,1,0:T(8,128)(2,1)}, u32[]{:S(2)}, u32[]{:S(2)}) collective-permute-start(bf16[4,512,128]{2,1,0:T(8,128)(2,1)} %get-tuple-element.28), channel_id=1, source_target_pairs={{0,32},{1,9},{2,34},{3,11},{4,36},{5,13},{6,38},{7,15},{8,40},{9,1... | collective-permute-start | bytes 1572872 | tf_op jit(solution)/shard_map/ppermute | solution.py:374
  32.5 2.7 %collective-permute-start.8 = (bf16[4,512,128]{2,1,0:T(8,128)(2,1)}, bf16[4,512,128]{2,1,0:T(8,128)(2,1)}, u32[]{:S(2)}, u32[]{:S(2)}) collective-permute-start(bf16[4,512,128]{2,1,0:T(8,128)(2,1)} %get-tuple-element.29), channel_id=1, source_target_pairs={{0,64},{1,17},{2,66},{3,19},{4,68},{5,21},{6,70},{7,23},{8,72},{9,... | collective-permute-start | bytes 1572872 | tf_op jit(solution)/shard_map/ppermute | solution.py:374
  35.2 0.0 collective-permute-done.2.d_ref
  35.2 0.8 copy-done.6
  36.0 1.5 %collective-permute-start.9 = (bf16[4,512,128]{2,1,0:T(8,128)(2,1)}, bf16[4,512,128]{2,1,0:T(8,128)(2,1)}, u32[]{:S(2)}, u32[]{:S(2)}) collective-permute-start(bf16[4,512,128]{2,1,0:T(8,128)(2,1)} %get-tuple-element.30), channel_id=1, source_target_pairs={{0,96},{1,25},{2,98},{3,27},{4,100},{5,29},{6,102},{7,31},{8,104},... | collective-permute-start | bytes 1572872 | tf_op jit(solution)/shard_map/ppermute | solution.py:374
  37.4 0.0 collective-permute-done.1.c_ref
  37.4 0.0 collective-permute-done.b_ref
  37.4 1.0 copy-done.7
  38.4 1.3 pack_factors.1
  39.7 0.0 copy-done.3
  39.8 0.1 collective-permute-start.3
  39.8 0.5 collective-permute-start.4
  40.3 1.0 collective-permute-done.3.rest_2_
  41.4 0.1 collective-permute-start.5
  41.5 0.2 collective-permute-done.4.rest_3_
  41.7 0.7 copy-done.19
  42.4 0.1 collective-permute-start.6
  42.6 0.0 all-to-all-done.rest_4_
  42.6 2.8 %first_rows.1 = (bf16[2,128,128]{2,1,0:T(8,128)(2,1)S(1)}, bf16[16,272,128]{2,1,0:T(8,128)(2,1)}) custom-call(bf16[2,2,128,256]{3,2,1,0:T(8,128)(2,1)} %copy-done.8, bf16[2,2,128,256]{3,2,1,0:T(8,128)(2,1)} %copy-done.9, bf16[2,2,128,256]{3,2,1,0:T(8,128)(2,1)} %copy-done.18, bf16[2,2,128,256]{3,2,1,0:T(8,128)(2,1)} %copy-done.19, ...), custom_call_target="tpu_custom_call" | custom-call | flops 1000000000 | bytes 1000 | tf_op jit(solution)/shard_map/first_rows/pallas_call | solution.py:173
  45.5 7.9 %all-to-all-start.1 = ((bf16[16,272,128]{2,1,0:T(8,128)(2,1)}), bf16[16,272,128]{2,1,0:T(8,128)(2,1)S(1)}, u32[]{:S(2)}, u32[]{:S(2)}) async-start(bf16[16,272,128]{2,1,0:T(8,128)(2,1)} %get-tuple-element.27), calls=%async_computation.1 | async-start | bytes 2228224 | tf_op jit(solution)/shard_map/all_to_all | solution.py:378
  53.4 0.0 collective-permute-done.7.b_ref
  53.4 0.0 collective-permute-done.8.c_ref
  53.4 0.0 collective-permute-done.9.d_ref
  53.5 0.0 copy-start.10
  53.5 2.4 %sum_minor.1.rest_4_.a_ref = bf16[4,512,128]{2,1,0:T(8,128)(2,1)} custom-call(bf16[4,512,128]{2,1,0:T(8,128)(2,1)S(1)} %copy-done.4, bf16[4,512,128]{2,1,0:T(8,128)(2,1)} %collective-permute-done.7.b_ref, bf16[4,512,128]{2,1,0:T(8,128)(2,1)} %collective-permute-done.8.c_ref, bf16[4,512,128]{2,1,0:T(8,128)(2,1)} %collective-permute-done.9.d_ref, ...), custom_call_target="tpu_custom_call" | custom-call | flops 30000001024 | bytes 1000 | tf_op jit(solution)/shard_map/sum_minor/pallas_call | solution.py:70
  55.9 1.9 %collective-permute-start.12 = (bf16[4,512,128]{2,1,0:T(8,128)(2,1)}, bf16[4,512,128]{2,1,0:T(8,128)(2,1)}, u32[]{:S(2)}, u32[]{:S(2)}) collective-permute-start(bf16[4,512,128]{2,1,0:T(8,128)(2,1)} %sum_minor.1.rest_4_.a_ref), channel_id=1, source_target_pairs={{0,8},{1,33},{2,10},{3,35},{4,12},{5,37},{6,14},{7,39},{8,16},{9,4... | collective-permute-start | bytes 1572872 | tf_op jit(solution)/shard_map/ppermute | solution.py:374
  57.8 2.7 %collective-permute-start.11 = (bf16[4,512,128]{2,1,0:T(8,128)(2,1)}, bf16[4,512,128]{2,1,0:T(8,128)(2,1)}, u32[]{:S(2)}, u32[]{:S(2)}) collective-permute-start(bf16[4,512,128]{2,1,0:T(8,128)(2,1)} %sum_minor.1.rest_4_.a_ref), channel_id=1, source_target_pairs={{0,16},{1,65},{2,18},{3,67},{4,20},{5,69},{6,22},{7,71},{8,24},{9,... | collective-permute-start | bytes 1572872 | tf_op jit(solution)/shard_map/ppermute | solution.py:374
  60.5 1.5 %collective-permute-start.10 = (bf16[4,512,128]{2,1,0:T(8,128)(2,1)}, bf16[4,512,128]{2,1,0:T(8,128)(2,1)}, u32[]{:S(2)}, u32[]{:S(2)}) collective-permute-start(bf16[4,512,128]{2,1,0:T(8,128)(2,1)} %sum_minor.1.rest_4_.a_ref), channel_id=1, source_target_pairs={{0,24},{1,97},{2,26},{3,99},{4,28},{5,101},{6,30},{7,103},{8,0},{9... | collective-permute-start | bytes 1572872 | tf_op jit(solution)/shard_map/ppermute | solution.py:374
  62.0 0.0 collective-permute-done.6.rest_1_
  62.0 10.7 %all-to-all-done.1.rest_2_.gathered_ref = bf16[16,272,128]{2,1,0:T(8,128)(2,1)S(1)} async-done(((bf16[16,272,128]{2,1,0:T(8,128)(2,1)}), bf16[16,272,128]{2,1,0:T(8,128)(2,1)S(1)}, u32[]{:S(2)}, u32[]{:S(2)}) %all-to-all-start.1) | async-done | bytes 1114144 | tf_op jit(solution)/shard_map/all_to_all | solution.py:378
  72.6 2.8 %reduced_rows.1 = (bf16[2,128,128]{2,1,0:T(8,128)(2,1)S(1)}, bf16[16,256,128]{2,1,0:T(8,128)(2,1)}) custom-call(bf16[4,2,128,256]{3,2,1,0:T(8,128)(2,1)} %copy-done.5, bf16[4,2,128,256]{3,2,1,0:T(8,128)(2,1)} %collective-permute-done.6.rest_1_, bf16[16,272,128]{2,1,0:T(8,128)(2,1)S(1)} %all-to-all-done.1.rest_2_.gathered_ref, ...), custom_call_target="tpu_custom_call" | custom-call | flops 30000001024 | bytes 1000 | tf_op jit(solution)/shard_map/reduced_rows/pallas_call | solution.py:173
  75.5 3.8 %all-to-all-start.2 = ((bf16[16,256,128]{2,1,0:T(8,128)(2,1)}), bf16[16,256,128]{2,1,0:T(8,128)(2,1)S(1)}, u32[]{:S(2)}, u32[]{:S(2)}) async-start(bf16[16,256,128]{2,1,0:T(8,128)(2,1)} %get-tuple-element.31), calls=%async_computation.2 | async-start | bytes 2097152 | tf_op jit(solution)/shard_map/all_to_all | solution.py:378
  79.3 0.0 collective-permute-done.12.d_ref
  79.3 1.8 %collective-permute-done.11.c_ref = bf16[4,512,128]{2,1,0:T(8,128)(2,1)} collective-permute-done((bf16[4,512,128]{2,1,0:T(8,128)(2,1)}, bf16[4,512,128]{2,1,0:T(8,128)(2,1)}, u32[]{:S(2)}, u32[]{:S(2)}) %collective-permute-start.11) | collective-permute-done | bytes 524320 | tf_op jit(solution)/shard_map/ppermute | solution.py:374
  81.2 0.6 collective-permute-done.10.b_ref
  81.8 2.6 %sum_major.1.rest_3_.rest_0_ = bf16[4,512,128]{2,1,0:T(8,128)(2,1)} custom-call(bf16[4,512,128]{2,1,0:T(8,128)(2,1)} %sum_minor.1.rest_4_.a_ref, bf16[4,512,128]{2,1,0:T(8,128)(2,1)} %collective-permute-done.10.b_ref, bf16[4,512,128]{2,1,0:T(8,128)(2,1)} %collective-permute-done.11.c_ref, bf16[4,512,128]{2,1,0:T(8,128)(2,1)} %collective-permute-done.12.d_ref, ...), custom_call_target="tpu_custom_call" | custom-call | flops 30000001024 | bytes 1000 | tf_op jit(solution)/shard_map/sum_major/pallas_call | solution.py:70
  84.4 0.7 collective-permute-start.15
  85.0 2.7 %collective-permute-start.14 = (bf16[4,512,128]{2,1,0:T(8,128)(2,1)}, bf16[4,512,128]{2,1,0:T(8,128)(2,1)}, u32[]{:S(2)}, u32[]{:S(2)}) collective-permute-start(bf16[4,512,128]{2,1,0:T(8,128)(2,1)} %sum_major.1.rest_3_.rest_0_), channel_id=1, source_target_pairs={{0,64},{1,17},{2,66},{3,19},{4,68},{5,21},{6,70},{7,23},{8,72},{9,... | collective-permute-start | bytes 1572872 | tf_op jit(solution)/shard_map/ppermute | solution.py:374
  87.7 2.4 %collective-permute-start.13 = (bf16[4,512,128]{2,1,0:T(8,128)(2,1)}, bf16[4,512,128]{2,1,0:T(8,128)(2,1)}, u32[]{:S(2)}, u32[]{:S(2)}) collective-permute-start(bf16[4,512,128]{2,1,0:T(8,128)(2,1)} %sum_major.1.rest_3_.rest_0_), channel_id=1, source_target_pairs={{0,96},{1,25},{2,98},{3,27},{4,100},{5,29},{6,102},{7,31},{8,104},... | collective-permute-start | bytes 1572872 | tf_op jit(solution)/shard_map/ppermute | solution.py:374
  90.1 0.0 collective-permute-done.5.rest_1_
  90.1 4.7 %all-to-all-done.2.rest_2_ = bf16[16,256,128]{2,1,0:T(8,128)(2,1)S(1)} async-done(((bf16[16,256,128]{2,1,0:T(8,128)(2,1)}), bf16[16,256,128]{2,1,0:T(8,128)(2,1)S(1)}, u32[]{:S(2)}, u32[]{:S(2)}) %all-to-all-start.2) | async-done | bytes 1048608 | tf_op jit(solution)/shard_map/all_to_all | solution.py:378
  94.9 2.8 %last_rows.1 = (bf16[2,128,128]{2,1,0:T(8,128)(2,1)S(1)}, bf16[16,256,128]{2,1,0:T(8,128)(2,1)}) custom-call(bf16[4,2,128,256]{3,2,1,0:T(8,128)(2,1)} %copy-done.2, bf16[4,2,128,256]{3,2,1,0:T(8,128)(2,1)} %collective-permute-done.5.rest_1_, bf16[16,256,128]{2,1,0:T(8,128)(2,1)S(1)} %all-to-all-done.2.rest_2_, bf16[4,512,128]{2,1,0:T(8,128)(2,1)} %sum_major.1.rest_3_.rest_0_), custom_call_target="tpu_custom_call" | custom-call | flops 30000001024 | bytes 1000 | tf_op jit(solution)/shard_map/last_rows/pallas_call | solution.py:173
  97.7 4.6 %all-to-all-start.3 = ((bf16[16,256,128]{2,1,0:T(8,128)(2,1)}), bf16[16,256,128]{2,1,0:T(8,128)(2,1)S(1)}, u32[]{:S(2)}, u32[]{:S(2)}) async-start(bf16[16,256,128]{2,1,0:T(8,128)(2,1)} %get-tuple-element.36), calls=%async_computation.3 | async-start | bytes 2097152 | tf_op jit(solution)/shard_map/all_to_all | solution.py:378
  102.3 0.0 collective-permute-done.15.rest_3_
  102.3 2.0 %collective-permute-done.14.rest_2_ = bf16[4,512,128]{2,1,0:T(8,128)(2,1)} collective-permute-done((bf16[4,512,128]{2,1,0:T(8,128)(2,1)}, bf16[4,512,128]{2,1,0:T(8,128)(2,1)}, u32[]{:S(2)}, u32[]{:S(2)}) %collective-permute-start.14) | collective-permute-done | bytes 524320 | tf_op jit(solution)/shard_map/ppermute | solution.py:374
  104.2 0.0 collective-permute-done.13.rest_1_
  104.2 7.4 %first_loads.1 = (f32[4096,256]{1,0:T(8,128)}, s32[1,2048]{1,0:T(1,128)S(1)}, f32[1,2048]{1,0:T(1,128)S(1)}) custom-call(s32[3]{0:T(128)S(1)} %pad_add_fusion.place_ref, bf16[16,272,128]{2,1,0:T(8,128)(2,1)S(1)} %all-to-all-done.1.rest_2_.gathered_ref, bf16[4,512,128]{2,1,0:T(8,128)(2,1)} %sum_major.1.rest_3_.rest_0_, ...), custom_call_target="tpu_custom_call" | custom-call | flops 30000001024 | bytes 1000 | tf_op jit(solution)/shard_map/first_loads/pallas_call | solution.py:256
  111.6 0.7 pad_maximum_fusion.1
  112.3 5.5 %all-to-all-done.3.gathered_ref = bf16[16,256,128]{2,1,0:T(8,128)(2,1)S(1)} async-done(((bf16[16,256,128]{2,1,0:T(8,128)(2,1)}), bf16[16,256,128]{2,1,0:T(8,128)(2,1)S(1)}, u32[]{:S(2)}, u32[]{:S(2)}) %all-to-all-start.3) | async-done | bytes 1048608 | tf_op jit(solution)/shard_map/all_to_all | solution.py:378
  117.8 7.4 %all_loads.1 = (bf16[4096,256]{1,0:T(8,128)(2,1)S(1)}, bf16[8,2,1024,512]{3,2,1,0:T(8,128)(2,1)S(1)}) custom-call(s32[1,2048]{1,0:T(1,128)S(1)} %get-tuple-element.34.ids, f32[1,2048]{1,0:T(1,128)S(1)} %get-tuple-element.35.weights, bf16[16,256,128]{2,1,0:T(8,128)(2,1)S(1)} %all-to-all-done.3.gathered_ref, f32[4096,256]{1,0:T(8,128)} %get-tuple-element.37.first_ref, ...), custom_call_target="tpu_custom_call" | custom-call | tf_op jit(solution)/shard_map/all_loads/pallas_call | solution.py:305
  125.2 5.3 %stress.1 = bf16[2,1024,128]{2,1,0:T(8,128)(2,1)} custom-call(bf16[4096,256]{1,0:T(8,128)(2,1)S(1)} %get-tuple-element.38.loads_ref, bf16[8,2,1024,512]{3,2,1,0:T(8,128)(2,1)S(1)} %get-tuple-element.39.maps_ref), custom_call_target="tpu_custom_call" | custom-call | tf_op jit(solution)/shard_map/stress/pallas_call | solution.py:343
  (34 shorter events, 0.1 us)
Async XLA Ops:
  7.2 0.9 copy-start.13
  7.2 1.0 copy-start.14
  7.2 1.0 copy-start.15
  7.2 5.8 %copy-start.16 = (bf16[2,128,128]{2,1,0:T(8,128)(2,1)S(1)}, bf16[2,128,128]{2,1,0:T(8,128)(2,1)}, u32[]{:S(2)}) copy-start(bf16[2,128,128]{2,1,0:T(8,128)(2,1)} %param.11) | copy-start | bytes 196612
  7.2 110.6 %all-gather.3.cloned.1.call-start = ((), (), s32[]{:S(2)}) async-start(), calls=%async_computation.4 | async-start | bytes 18874368 | tf_op jit(solution)/shard_map/all_gather | solution.py:403
  7.9 14.2 %copy-start.17 = (bf16[3072]{0:T(1024)(128)(2,1)S(1)}, bf16[3072]{0:T(1024)(128)(2,1)}, u32[]{:S(2)}) copy-start(bf16[3072]{0:T(1024)(128)(2,1)} %param.18) | copy-start | bytes 18436
  8.0 14.3 %copy-start = (bf16[2,3072,128]{2,1,0:T(8,128)(2,1)S(1)}, bf16[2,3072,128]{2,1,0:T(8,128)(2,1)}, u32[]{:S(2)}) copy-start(bf16[2,3072,128]{2,1,0:T(8,128)(2,1)} %earlier_ref.1) | copy-start | bytes 4718596
  8.0 14.3 %copy-start.1 = (s32[3072]{0:T(1024)S(1)}, s32[3072]{0:T(1024)}, u32[]{:S(2)}) copy-start(s32[3072]{0:T(1024)} %param.17) | copy-start | bytes 36868
  8.2 27.0 %collective-permute-start.2 = (bf16[3,2,128,256]{3,2,1,0:T(8,128)(2,1)S(1)}, bf16[3,2,128,256]{3,2,1,0:T(8,128)(2,1)S(1)}, u32[]{:S(2)}, u32[]{:S(2)}) collective-permute-start(bf16[3,2,128,256]{3,2,1,0:T(8,128)(2,1)S(1)} %pad_maximum_fusion.a_ref), channel_id=1, source_target_pairs={{0,6},{1,7},{2,0},{3,1},{4,2},{5,3},{6,4},{7,5},{8,14},{9,15},{10,... | collective-permute-start | bytes 1179656 | tf_op jit(solution)/shard_map/ppermute | solution.py:358
  11.4 26.0 %collective-permute-start.1 = (bf16[3,2,128,256]{3,2,1,0:T(8,128)(2,1)S(1)}, bf16[3,2,128,256]{3,2,1,0:T(8,128)(2,1)}, u32[]{:S(2)}, u32[]{:S(2)}) collective-permute-start(bf16[3,2,128,256]{3,2,1,0:T(8,128)(2,1)S(1)} %pad_maximum_fusion.a_ref), channel_id=1, source_target_pairs={{0,4},{1,5},{2,6},{3,7},{4,0},{5,1},{6,2},{7,3},{8,12},{9,13},{10,... | collective-permute-start | bytes 1179656 | tf_op jit(solution)/shard_map/ppermute | solution.py:358
  12.0 25.4 %collective-permute-start = (bf16[3,2,128,256]{3,2,1,0:T(8,128)(2,1)S(1)}, bf16[3,2,128,256]{3,2,1,0:T(8,128)(2,1)}, u32[]{:S(2)}, u32[]{:S(2)}) collective-permute-start(bf16[3,2,128,256]{3,2,1,0:T(8,128)(2,1)S(1)} %pad_maximum_fusion.a_ref), channel_id=1, source_target_pairs={{0,2},{1,3},{2,4},{3,5},{4,6},{5,7},{6,0},{7,1},{8,10},{9,11},{10,... | collective-permute-start | bytes 1179656 | tf_op jit(solution)/shard_map/ppermute | solution.py:358
  14.2 28.4 %all-to-all-start = ((bf16[16,256,128]{2,1,0:T(8,128)(2,1)}), bf16[16,256,128]{2,1,0:T(8,128)(2,1)S(1)}, u32[]{:S(2)}, u32[]{:S(2)}) async-start(bf16[16,256,128]{2,1,0:T(8,128)(2,1)} %broadcast_in_dim.16), calls=%async_computation | async-start | bytes 2097152 | tf_op jit(solution)/shard_map/all_to_all | solution.py:378
  30.6 9.1 %copy-start.3 = (bf16[4,512,128]{2,1,0:T(8,128)(2,1)}, bf16[4,512,128]{2,1,0:T(8,128)(2,1)S(1)}, u32[]{:S(2)}) copy-start(bf16[4,512,128]{2,1,0:T(8,128)(2,1)S(1)} %get-tuple-element.21.tie_ref.a_ref) | copy-start | bytes 1572868
  30.6 22.8 %collective-permute-start.7 = (bf16[4,512,128]{2,1,0:T(8,128)(2,1)}, bf16[4,512,128]{2,1,0:T(8,128)(2,1)}, u32[]{:S(2)}, u32[]{:S(2)}) collective-permute-start(bf16[4,512,128]{2,1,0:T(8,128)(2,1)} %get-tuple-element.28), channel_id=1, source_target_pairs={{0,32},{1,9},{2,34},{3,11},{4,36},{5,13},{6,38},{7,15},{8,40},{9,1... | collective-permute-start | bytes 1572872 | tf_op jit(solution)/shard_map/ppermute | solution.py:374
  32.5 20.9 %collective-permute-start.8 = (bf16[4,512,128]{2,1,0:T(8,128)(2,1)}, bf16[4,512,128]{2,1,0:T(8,128)(2,1)}, u32[]{:S(2)}, u32[]{:S(2)}) collective-permute-start(bf16[4,512,128]{2,1,0:T(8,128)(2,1)} %get-tuple-element.29), channel_id=1, source_target_pairs={{0,64},{1,17},{2,66},{3,19},{4,68},{5,21},{6,70},{7,23},{8,72},{9,... | collective-permute-start | bytes 1572872 | tf_op jit(solution)/shard_map/ppermute | solution.py:374
  35.2 0.8 copy-start.6
  36.0 17.5 %collective-permute-start.9 = (bf16[4,512,128]{2,1,0:T(8,128)(2,1)}, bf16[4,512,128]{2,1,0:T(8,128)(2,1)}, u32[]{:S(2)}, u32[]{:S(2)}) collective-permute-start(bf16[4,512,128]{2,1,0:T(8,128)(2,1)} %get-tuple-element.30), channel_id=1, source_target_pairs={{0,96},{1,25},{2,98},{3,27},{4,100},{5,29},{6,102},{7,31},{8,104},... | collective-permute-start | bytes 1572872 | tf_op jit(solution)/shard_map/ppermute | solution.py:374
  37.4 1.0 copy-start.7
  38.4 4.2 %copy-start.11 = (s32[2,128]{1,0:T(2,128)S(1)}, s32[2,128]{1,0:T(2,128)}, u32[]{:S(2)}) copy-start(s32[2,128]{1,0:T(2,128)} %rest_5_.1) | copy-start | bytes 3076
  38.4 4.2 %copy-start.12 = (bf16[2,128]{1,0:T(2,128)(2,1)S(1)}, bf16[2,128]{1,0:T(2,128)(2,1)}, u32[]{:S(2)}) copy-start(bf16[2,128]{1,0:T(2,128)(2,1)} %rest_6_.1) | copy-start | bytes 1540
  39.7 2.9 %copy-start.8 = (bf16[2,2,128,256]{3,2,1,0:T(8,128)(2,1)}, bf16[2,2,128,256]{3,2,1,0:T(8,128)(2,1)S(1)}, u32[]{:S(2)}) copy-start(bf16[2,2,128,256]{3,2,1,0:T(8,128)(2,1)S(1)} %get-tuple-element.22.rest_0_) | copy-start | bytes 786436
  39.7 2.9 %copy-start.9 = (bf16[2,2,128,256]{3,2,1,0:T(8,128)(2,1)}, bf16[2,2,128,256]{3,2,1,0:T(8,128)(2,1)S(1)}, u32[]{:S(2)}) copy-start(bf16[2,2,128,256]{3,2,1,0:T(8,128)(2,1)S(1)} %get-tuple-element.23.rest_1_) | copy-start | bytes 786436
  39.7 5.7 %copy-start.2 = (bf16[4,2,128,256]{3,2,1,0:T(8,128)(2,1)}, bf16[4,2,128,256]{3,2,1,0:T(8,128)(2,1)S(1)}, u32[]{:S(2)}) copy-start(bf16[4,2,128,256]{3,2,1,0:T(8,128)(2,1)S(1)} %get-tuple-element.25.rest_0_) | copy-start | bytes 1572868
  39.7 5.7 %copy-start.5 = (bf16[4,2,128,256]{3,2,1,0:T(8,128)(2,1)}, bf16[4,2,128,256]{3,2,1,0:T(8,128)(2,1)S(1)}, u32[]{:S(2)}) copy-start(bf16[4,2,128,256]{3,2,1,0:T(8,128)(2,1)S(1)} %get-tuple-element.26.rest_0_) | copy-start | bytes 1572868
  39.8 1.6 %collective-permute-start.3 = (bf16[2,2,128,256]{3,2,1,0:T(8,128)(2,1)S(1)}, bf16[2,2,128,256]{3,2,1,0:T(8,128)(2,1)S(1)}, u32[]{:S(2)}, u32[]{:S(2)}) collective-permute-start(bf16[2,2,128,256]{3,2,1,0:T(8,128)(2,1)S(1)} %get-tuple-element.22.rest_0_), channel_id=1, source_target_pairs={{0,1},{1,0},{2,3},{3,2},{4,5},{5,4},{6,7},{7,6},{8,9},{9,8},{10,11... | collective-permute-start | bytes 786440 | tf_op jit(solution)/shard_map/ppermute | solution.py:362
  39.8 1.9 %collective-permute-start.4 = (bf16[2,2,128,256]{3,2,1,0:T(8,128)(2,1)S(1)}, bf16[2,2,128,256]{3,2,1,0:T(8,128)(2,1)S(1)}, u32[]{:S(2)}, u32[]{:S(2)}) collective-permute-start(bf16[2,2,128,256]{3,2,1,0:T(8,128)(2,1)S(1)} %get-tuple-element.23.rest_1_), channel_id=1, source_target_pairs={{0,1},{1,0},{2,3},{3,2},{4,5},{5,4},{6,7},{7,6},{8,9},{9,8},{10,11... | collective-permute-start | bytes 786440 | tf_op jit(solution)/shard_map/ppermute | solution.py:362
  41.4 1.2 copy-start.18
  41.4 48.7 %collective-permute-start.5 = (bf16[4,2,128,256]{3,2,1,0:T(8,128)(2,1)S(1)}, bf16[4,2,128,256]{3,2,1,0:T(8,128)(2,1)}, u32[]{:S(2)}, u32[]{:S(2)}) collective-permute-start(bf16[4,2,128,256]{3,2,1,0:T(8,128)(2,1)S(1)} %get-tuple-element.25.rest_0_), channel_id=1, source_target_pairs={{0,1},{1,0},{2,3},{3,2},{4,5},{5,4},{6,7},{7,6},{8,9},{9,8},{10,11... | collective-permute-start | bytes 1572872 | tf_op jit(solution)/shard_map/ppermute | solution.py:362
  41.7 0.7 copy-start.19
  42.4 11.0 %copy-start.4 = (bf16[4,512,128]{2,1,0:T(8,128)(2,1)S(1)}, bf16[4,512,128]{2,1,0:T(8,128)(2,1)}, u32[]{:S(2)}) copy-start(bf16[4,512,128]{2,1,0:T(8,128)(2,1)} %copy-done.3) | copy-start | bytes 1572868
  42.4 19.5 %collective-permute-start.6 = (bf16[4,2,128,256]{3,2,1,0:T(8,128)(2,1)S(1)}, bf16[4,2,128,256]{3,2,1,0:T(8,128)(2,1)}, u32[]{:S(2)}, u32[]{:S(2)}) collective-permute-start(bf16[4,2,128,256]{3,2,1,0:T(8,128)(2,1)S(1)} %get-tuple-element.26.rest_0_), channel_id=1, source_target_pairs={{0,1},{1,0},{2,3},{3,2},{4,5},{5,4},{6,7},{7,6},{8,9},{9,8},{10,11... | collective-permute-start | bytes 1572872 | tf_op jit(solution)/shard_map/ppermute | solution.py:362
  45.5 27.1 %all-to-all-start.1 = ((bf16[16,272,128]{2,1,0:T(8,128)(2,1)}), bf16[16,272,128]{2,1,0:T(8,128)(2,1)S(1)}, u32[]{:S(2)}, u32[]{:S(2)}) async-start(bf16[16,272,128]{2,1,0:T(8,128)(2,1)} %get-tuple-element.27), calls=%async_computation.1 | async-start | bytes 2228224 | tf_op jit(solution)/shard_map/all_to_all | solution.py:378
  53.5 19.2 %copy-start.10 = (bf16[2,128,128]{2,1,0:T(8,128)(2,1)S(1)}, bf16[2,128,128]{2,1,0:T(8,128)(2,1)}, u32[]{:S(2)}) copy-start(bf16[2,128,128]{2,1,0:T(8,128)(2,1)} %rest_3_.1) | copy-start | bytes 196612
  55.9 23.4 %collective-permute-start.12 = (bf16[4,512,128]{2,1,0:T(8,128)(2,1)}, bf16[4,512,128]{2,1,0:T(8,128)(2,1)}, u32[]{:S(2)}, u32[]{:S(2)}) collective-permute-start(bf16[4,512,128]{2,1,0:T(8,128)(2,1)} %sum_minor.1.rest_4_.a_ref), channel_id=1, source_target_pairs={{0,8},{1,33},{2,10},{3,35},{4,12},{5,37},{6,14},{7,39},{8,16},{9,4... | collective-permute-start | bytes 1572872 | tf_op jit(solution)/shard_map/ppermute | solution.py:374
  57.8 23.3 %collective-permute-start.11 = (bf16[4,512,128]{2,1,0:T(8,128)(2,1)}, bf16[4,512,128]{2,1,0:T(8,128)(2,1)}, u32[]{:S(2)}, u32[]{:S(2)}) collective-permute-start(bf16[4,512,128]{2,1,0:T(8,128)(2,1)} %sum_minor.1.rest_4_.a_ref), channel_id=1, source_target_pairs={{0,16},{1,65},{2,18},{3,67},{4,20},{5,69},{6,22},{7,71},{8,24},{9,... | collective-permute-start | bytes 1572872 | tf_op jit(solution)/shard_map/ppermute | solution.py:374
  60.5 21.3 %collective-permute-start.10 = (bf16[4,512,128]{2,1,0:T(8,128)(2,1)}, bf16[4,512,128]{2,1,0:T(8,128)(2,1)}, u32[]{:S(2)}, u32[]{:S(2)}) collective-permute-start(bf16[4,512,128]{2,1,0:T(8,128)(2,1)} %sum_minor.1.rest_4_.a_ref), channel_id=1, source_target_pairs={{0,24},{1,97},{2,26},{3,99},{4,28},{5,101},{6,30},{7,103},{8,0},{9... | collective-permute-start | bytes 1572872 | tf_op jit(solution)/shard_map/ppermute | solution.py:374
  75.5 19.4 %all-to-all-start.2 = ((bf16[16,256,128]{2,1,0:T(8,128)(2,1)}), bf16[16,256,128]{2,1,0:T(8,128)(2,1)S(1)}, u32[]{:S(2)}, u32[]{:S(2)}) async-start(bf16[16,256,128]{2,1,0:T(8,128)(2,1)} %get-tuple-element.31), calls=%async_computation.2 | async-start | bytes 2097152 | tf_op jit(solution)/shard_map/all_to_all | solution.py:378
  84.4 17.9 %collective-permute-start.15 = (bf16[4,512,128]{2,1,0:T(8,128)(2,1)}, bf16[4,512,128]{2,1,0:T(8,128)(2,1)}, u32[]{:S(2)}, u32[]{:S(2)}) collective-permute-start(bf16[4,512,128]{2,1,0:T(8,128)(2,1)} %sum_major.1.rest_3_.rest_0_), channel_id=1, source_target_pairs={{0,32},{1,9},{2,34},{3,11},{4,36},{5,13},{6,38},{7,15},{8,40},{9,1... | collective-permute-start | bytes 1572872 | tf_op jit(solution)/shard_map/ppermute | solution.py:374
  85.0 19.2 %collective-permute-start.14 = (bf16[4,512,128]{2,1,0:T(8,128)(2,1)}, bf16[4,512,128]{2,1,0:T(8,128)(2,1)}, u32[]{:S(2)}, u32[]{:S(2)}) collective-permute-start(bf16[4,512,128]{2,1,0:T(8,128)(2,1)} %sum_major.1.rest_3_.rest_0_), channel_id=1, source_target_pairs={{0,64},{1,17},{2,66},{3,19},{4,68},{5,21},{6,70},{7,23},{8,72},{9,... | collective-permute-start | bytes 1572872 | tf_op jit(solution)/shard_map/ppermute | solution.py:374
  87.7 16.5 %collective-permute-start.13 = (bf16[4,512,128]{2,1,0:T(8,128)(2,1)}, bf16[4,512,128]{2,1,0:T(8,128)(2,1)}, u32[]{:S(2)}, u32[]{:S(2)}) collective-permute-start(bf16[4,512,128]{2,1,0:T(8,128)(2,1)} %sum_major.1.rest_3_.rest_0_), channel_id=1, source_target_pairs={{0,96},{1,25},{2,98},{3,27},{4,100},{5,29},{6,102},{7,31},{8,104},... | collective-permute-start | bytes 1572872 | tf_op jit(solution)/shard_map/ppermute | solution.py:374
  97.7 20.1 %all-to-all-start.3 = ((bf16[16,256,128]{2,1,0:T(8,128)(2,1)}), bf16[16,256,128]{2,1,0:T(8,128)(2,1)S(1)}, u32[]{:S(2)}, u32[]{:S(2)}) async-start(bf16[16,256,128]{2,1,0:T(8,128)(2,1)} %get-tuple-element.36), calls=%async_computation.3 | async-start | bytes 2097152 | tf_op jit(solution)/shard_map/all_to_all | solution.py:378
Sparse Core Ops, SparseCore 0:
  9.8 91.7 all-gather.2

commit v5 on v4

--- a/solution.py
+++ b/solution.py
@@ -23,15 +23,23 @@
     return jnp.where(patch == ids - first, weights, jnp.zeros((), BF16))
 
 
-def old_loads_kernel(place_ref, ids_ref, weights_ref, earlier_ref, *rest, chunk):
+def minor_place():
+    row = lax.axis_index("row")
+    x, z = row // 4, row % 4
+    swap = 1 - lax.axis_index("col") % 2
+    return z + swap * (x - z), swap
+
+
+def old_loads_kernel(ids_ref, weights_ref, earlier_ref, *rest, chunk):
     outs, side = rest[:4], rest[4]
     side[:, :128] = earlier_ref[0]
     side[:, 128:] = earlier_ref[1]
     ids = ids_ref[...]
     x, z = ids >> 10, (ids >> 8) & 3
-    major = x + place_ref[2] * (z - x)
-    minor = z + place_ref[2] * (x - z)
-    labels = ((minor - place_ref[1]) & 3) * 1024 + major * 256 + (ids & 255)
+    place, swap = minor_place()
+    major = x + swap * (z - x)
+    minor = z + swap * (x - z)
+    labels = ((minor - place) & 3) * 1024 + major * 256 + (ids & 255)
     for k in range(4):
         total = jnp.zeros((1024, 256), F32)
         for start in range(0, side.shape[0], chunk):
@@ -44,18 +52,18 @@
             outs[k][block, 256:] = total[rows, 128:].astype(BF16)
 
 
-def old_loads(place, ids, weights, earlier):
+def old_loads(ids, weights, earlier):
     panels = earlier.shape[1]
     vmem = pl.BlockSpec(memory_space=pltpu.VMEM)
     return pl.pallas_call(
         functools.partial(old_loads_kernel, chunk=512),
         out_shape=[jax.ShapeDtypeStruct((4, 512, 128), BF16)] * 4,
-        in_specs=[pl.BlockSpec(memory_space=pltpu.SMEM)] + [vmem] * 3,
+        in_specs=[vmem] * 3,
         out_specs=[vmem] * 4,
         scratch_shapes=[pltpu.VMEM((panels, 256), BF16)],
         compiler_params=PARAMS,
         name="old_loads",
-    )(place, ids, weights, earlier)
+    )(ids, weights, earlier)
 
 
 def sum_loads_kernel(a_ref, b_ref, c_ref, d_ref, tie_ref, out_ref):
@@ -78,11 +86,16 @@
     )(*parts, tie)
 
 
-def pack_factors_kernel(a_ref, b_ref, c_ref, d_ref, tie_ref, *outs):
-    for k, value_ref in enumerate((a_ref, b_ref, c_ref, d_ref)):
-        outs[k // 2][k % 2] = value_ref[0]
-        outs[2][k] = value_ref[1]
-        outs[3][k] = value_ref[2]
+def pack_factors_kernel(*refs):
+    values, outs, sems = refs[:4], refs[5:9], refs[9]
+    copies = []
+    for k in range(4):
+        targets = (outs[k // 2].at[k % 2], outs[2].at[k], outs[3].at[k])
+        for m in range(3):
+            copies.append(pltpu.make_async_copy(values[k].at[m], targets[m], sems.at[k, m]))
+            copies[-1].start()
+    for copy in copies:
+        copy.wait()
 
 
 def pack_factors(values, tie):
@@ -92,12 +105,17 @@
         out_shape=[
             jax.ShapeDtypeStruct((count, *values[0].shape[1:]), BF16) for count in (2, 2, 4, 4)
         ],
-        in_specs=[vmem] * 4 + [pl.BlockSpec(memory_space=pl.ANY)],
+        in_specs=[pl.BlockSpec(memory_space=pl.ANY)] * 5,
         out_specs=[vmem] * 4,
+        scratch_shapes=[pltpu.SemaphoreType.DMA((4, 3))],
         compiler_params=PARAMS,
         cost_estimate=SHORT,
         name="pack_factors",
-    )(*values, tie)
+    )(
+        values[0],
+        *[pltpu.with_memory_space_constraint(value, pltpu.HBM) for value in values[1:]],
+        tie,
+    )
 
 
 def send_copies(source, copies_ref, sems):
@@ -166,7 +184,7 @@
     operands = [gathered]
     operands += [] if base is None else [base]
     operands += [] if extra is None else extra
-    specs = [hbm] * len(factors) + [vmem] * len(operands)
+    specs = [pl.BlockSpec(memory_space=pl.ANY)] * len(factors) + [vmem] * len(operands)
     specs += [pl.BlockSpec(memory_space=pl.ANY)] * len(ties)
     height = 256 if extra is None else 272
     shapes = [jax.ShapeDtypeStruct((2, 128, 128), BF16), pltpu.HBM((ROWS, height, 128), BF16)]
@@ -193,7 +211,7 @@
         cost_estimate=cost,
         name=name,
     )(
-        *[pltpu.with_memory_space_constraint(part, pltpu.HBM) for part in factors],
+        *factors,
         *operands,
         *ties,
     )
@@ -215,7 +233,7 @@
         side[rows, 128:] = gathered_ref[source, 128:256]
 
 
-def first_loads_kernel(place_ref, gathered_ref, *rest):
+def first_loads_kernel(gathered_ref, *rest):
     old_refs = rest[:4]
     out_ref, ids_ref, weights_ref, side, ids, weights, old, total, old_sems, sems = rest[4:]
     old_copies = [
@@ -234,11 +252,12 @@
     for first in range(0, PATCHES, 1024):
         total[first : first + 1024] = panel_loads(side, ids, weights, first, 1024, 512)
     copies = []
+    place, swap = minor_place()
     for j in range(4):
         old_copies[j].wait()
-        minor = (place_ref[1] + j) % 4
+        minor = (place + j) % 4
         for major in range(4):
-            block = (major * 4 + minor) + place_ref[2] * 3 * (minor - major)
+            block = (major * 4 + minor) + swap * 3 * (minor - major)
             rows = pl.ds(pl.multiple_of(block * 256, 256), 256)
             total[rows, :128] += old[j, major, :256].astype(F32)
             total[rows, 128:] += old[j, major, 256:].astype(F32)
@@ -250,7 +269,7 @@
         copy.wait()
 
 
-def first_loads(place, gathered, old):
+def first_loads(gathered, old):
     vmem = pl.BlockSpec(memory_space=pltpu.VMEM)
     hbm = pl.BlockSpec(memory_space=pltpu.HBM)
     return pl.pallas_call(
@@ -260,8 +279,7 @@
             jax.ShapeDtypeStruct((1, 2048), jnp.int32),
             jax.ShapeDtypeStruct((1, 2048), F32),
         ),
-        in_specs=[pl.BlockSpec(memory_space=pltpu.SMEM), vmem]
-        + [pl.BlockSpec(memory_space=pl.ANY)] * 4,
+        in_specs=[vmem] + [pl.BlockSpec(memory_space=pl.ANY)] * 4,
         out_specs=(hbm, vmem, vmem),
         scratch_shapes=[
             pltpu.VMEM((2048, 256), BF16),
@@ -275,7 +293,7 @@
         compiler_params=PARAMS,
         cost_estimate=COST,
         name="first_loads",
-    )(place, gathered, *old)
+    )(gathered, *old)
 
 
 def all_loads_kernel(
@@ -391,19 +409,11 @@
     weight_new,
     stress_map,
 ):
-    row = lax.axis_index("row")
-    col = lax.axis_index("col")
-    core = col % 2
-    x, z = row // 4, row % 4
-    swap = 1 - core
-    place = jnp.stack([x + swap * (z - x), z + swap * (x - z), swap]).astype(jnp.int32)
-
-
     rhs_all = to_rows(jnp.broadcast_to(rhs_first.reshape(1, 256, 128), (ROWS, 256, 128)))
     maps = lax.all_gather(stress_map, "col")
     factors = jnp.stack([inv_first, coupling, inv_last])
     factors = [factors] + [along_y(factors, hop) for hop in (1, 2, 3)]
-    old = old_loads(place, patch_old[None], weight_old[None], earlier)
+    old = old_loads(patch_old[None], weight_old[None], earlier)
     own = list(pack_factors(factors, old[0]))
     other = [other_core(value) for value in own]
     factors = [own[:2] + other[:2], [own[2], other[2]], [own[3], other[3]]]
@@ -422,7 +432,7 @@
     x_last, copies = rows_product("last_rows", factors[2], reduced_all, ties=(old,))
     x_last_all = to_rows(copies)
     old = [old] + [along_axis(old, hop, False) for hop in (3, 2, 1)]
-    loads, ids, weights = first_loads(place, x_first_all, old)
+    loads, ids, weights = first_loads(x_first_all, old)
     stress_rao = stress(*all_loads(ids, weights, x_last_all, loads, maps))
     return (jnp.stack([x_first, x_last]), stress_rao)
 

time: 139 us -> 138 us (level)
  starting transfers between devices: 47.7 us -> 49.3 us
  Pallas kernels: 43.2 us -> 41.7 us
  transfers between devices with their start and end apart: 21 -> 21, of which waited for: 8 -> 8; matrix products, arithmetic and copies ran while one was open for 1% -> 1% of each run, Pallas kernels for 22% -> 21%
where the time goes in v5:
time: 138 us; the launch traced here: 137 us
  starting transfers between devices  49.3 us (36%)
  Pallas kernels  41.7 us (30%)
  waiting for transfers between devices  27.8 us (20%)
  between operations  14.3 us (10%)
  local copies, waits for them, and re-layouts  3.14 us (2%)
    all_to_all x4, starting transfers between devices, to_rows(): return lax.all_to_all(copies, 'row', 0, 0, tiled=True)  25.3 us
    all_to_all x4, waiting for transfers between devices, to_rows(): return lax.all_to_all(copies, 'row', 0, 0, tiled=True)  21 us
    ppermute x9, starting transfers between devices, along_axis(): return lax.ppermute(value, ('row', 'col'), pairs)  17.9 us
    pallas_call x1, Pallas kernels, old_loads(): pl.pallas_call(functools.partial(old_loads_kernel, chunk=512), out_shape=...  7.88 us
    pallas_call x1, Pallas kernels, all_loads(): pl.pallas_call(all_loads_kernel, out_shape=(pltpu.VMEM((PATCHES, 256), BF...  7.4 us
    pallas_call x3, Pallas kernels, rows_product(): pl.pallas_call(functools.partial(rows_kernel, parts=len(factors), base=ba...  7.31 us
    pallas_call x1, Pallas kernels, first_loads(): pl.pallas_call(first_loads_kernel, out_shape=(pltpu.HBM((PATCHES, 256), F...  6.83 us
    pallas_call x1, Pallas kernels, stress(): pl.pallas_call(stress_kernel, out_shape=jax.ShapeDtypeStruct((2, 1024, 12...  5.28 us
  transfers between devices with their start and end apart: 21, of which 8 were waited for; matrix products, arithmetic and copies ran while one was open for 1% of the time, Pallas kernels for 21%

profile of v5, /device:TPU:0, one launch (start us, length us, event | category | flops | bytes accessed | tf_op | source)
XLA Modules:
  0.0 136.9 jit_solution(9544969721029120723)
XLA Ops:
  7.2 0.0 copy-start.9
  7.2 0.0 copy-start.10
  7.2 0.0 all-gather.3.cloned.1.call-start
  7.3 0.7 all-gather.3.cloned.1.call-update
  8.0 0.1 copy-done.9
  8.1 0.1 copy-done.10
  8.1 0.1 copy-done.11
  8.2 3.2 %collective-permute-start.2 = (bf16[3,2,128,256]{3,2,1,0:T(8,128)(2,1)S(1)}, bf16[3,2,128,256]{3,2,1,0:T(8,128)(2,1)S(1)}, u32[]{:S(2)}, u32[]{:S(2)}) collective-permute-start(bf16[3,2,128,256]{3,2,1,0:T(8,128)(2,1)S(1)} %pad_maximum_fusion.refs_0_), channel_id=1, source_target_pairs={{0,6},{1,7},{2,0},{3,1},{4,2},{5,3},{6,4},{7,5},{8,14},{9,15},{10,... | collective-permute-start | bytes 1179656 | tf_op jit(solution)/shard_map/ppermute | solution.py:376
  11.4 0.6 collective-permute-start.1
  12.0 1.0 collective-permute-start
  13.0 1.2 broadcast_in_dim.16
  14.2 7.9 %all-to-all-start = ((bf16[16,256,128]{2,1,0:T(8,128)(2,1)}), bf16[16,256,128]{2,1,0:T(8,128)(2,1)S(1)}, u32[]{:S(2)}, u32[]{:S(2)}) async-start(bf16[16,256,128]{2,1,0:T(8,128)(2,1)} %broadcast_in_dim.16), calls=%async_computation | async-start | bytes 2097152 | tf_op jit(solution)/shard_map/all_to_all | solution.py:396
  22.2 7.9 %old_loads.1 = (bf16[4,512,128]{2,1,0:T(8,128)(2,1)S(1)}, bf16[4,512,128]{2,1,0:T(8,128)(2,1)}, bf16[4,512,128]{2,1,0:T(8,128)(2,1)}, bf16[4,512,128]{2,1,0:T(8,128)(2,1)}) custom-call(s32[1,3072]{1,0:T(1,128)S(1)} %bitcast.10, bf16[1,3072]{1,0:T(2,128)(2,1)S(1)} %broadcast_in_dim.14.weights_ref, bf16[2,3072,128]{2,1,0:T(8,128)(2,1)S(1)} %copy-done), custom_call_target="tpu_custom_call" | custom-call | tf_op jit(solution)/shard_map/old_loads/pallas_call | solution.py:58
  30.0 1.9 %collective-permute-start.7 = (bf16[4,512,128]{2,1,0:T(8,128)(2,1)}, bf16[4,512,128]{2,1,0:T(8,128)(2,1)}, u32[]{:S(2)}, u32[]{:S(2)}) collective-permute-start(bf16[4,512,128]{2,1,0:T(8,128)(2,1)} %get-tuple-element.28), channel_id=1, source_target_pairs={{0,32},{1,9},{2,34},{3,11},{4,36},{5,13},{6,38},{7,15},{8,40},{9,1... | collective-permute-start | bytes 1572872 | tf_op jit(solution)/shard_map/ppermute | solution.py:392
  32.0 2.7 %collective-permute-start.8 = (bf16[4,512,128]{2,1,0:T(8,128)(2,1)}, bf16[4,512,128]{2,1,0:T(8,128)(2,1)}, u32[]{:S(2)}, u32[]{:S(2)}) collective-permute-start(bf16[4,512,128]{2,1,0:T(8,128)(2,1)} %get-tuple-element.29), channel_id=1, source_target_pairs={{0,64},{1,17},{2,66},{3,19},{4,68},{5,21},{6,70},{7,23},{8,72},{9,... | collective-permute-start | bytes 1572872 | tf_op jit(solution)/shard_map/ppermute | solution.py:392
  34.6 0.0 collective-permute-done.2.refs_3_
  34.7 1.5 %collective-permute-start.9 = (bf16[4,512,128]{2,1,0:T(8,128)(2,1)}, bf16[4,512,128]{2,1,0:T(8,128)(2,1)}, u32[]{:S(2)}, u32[]{:S(2)}) collective-permute-start(bf16[4,512,128]{2,1,0:T(8,128)(2,1)} %get-tuple-element.30), channel_id=1, source_target_pairs={{0,96},{1,25},{2,98},{3,27},{4,100},{5,29},{6,102},{7,31},{8,104},... | collective-permute-start | bytes 1572872 | tf_op jit(solution)/shard_map/ppermute | solution.py:392
  36.1 0.0 collective-permute-done.1.refs_2_
  36.1 0.2 collective-permute-done.refs_1_
  36.3 1.9 %pack_factors.1 = (bf16[2,2,128,256]{3,2,1,0:T(8,128)(2,1)S(1)}, bf16[2,2,128,256]{3,2,1,0:T(8,128)(2,1)S(1)}, bf16[4,2,128,256]{3,2,1,0:T(8,128)(2,1)S(1)}, bf16[4,2,128,256]{3,2,1,0:T(8,128)(2,1)S(1)}) custom-call(bf16[3,2,128,256]{3,2,1,0:T(8,128)(2,1)S(1)} %pad_maximum_fusion.refs_0_, bf16[3,2,128,256]{3,2,1,0:T(8,128)(2,1)} %collective-permute-done.refs_1_, ...), custom_call_target="tpu_custom_call" | custom-call | flops 6000000000 | bytes 1000 | tf_op jit(solution)/shard_map/pack_factors/pallas_call | solution.py:103
  38.3 0.1 collective-permute-start.3
  38.4 0.5 collective-permute-start.4
  38.9 1.0 collective-permute-done.3.rest_2_
  39.9 0.3 collective-permute-start.5
  40.2 0.0 collective-permute-done.4.rest_3_
  40.3 0.7 copy-done.4
  41.0 0.3 collective-permute-start.6
  41.3 0.0 all-to-all-done.rest_4_
  41.3 0.0 copy-done.8
  41.3 0.9 copy-done.5
  42.3 1.9 %first_rows.1 = (bf16[2,128,128]{2,1,0:T(8,128)(2,1)S(1)}, bf16[16,272,128]{2,1,0:T(8,128)(2,1)}) custom-call(bf16[2,2,128,256]{3,2,1,0:T(8,128)(2,1)S(1)} %get-tuple-element.22.rest_0_, bf16[2,2,128,256]{3,2,1,0:T(8,128)(2,1)S(1)} %get-tuple-element.23.rest_1_, bf16[2,2,128,256]{3,2,1,0:T(8,128)(2,1)S(1)} %collective-permute-done.3.rest_2_, ...), custom_call_target="tpu_custom_call" | custom-call | flops 1000000000 | bytes 1000 | tf_op jit(solution)/shard_map/first_rows/pallas_call | solution.py:191
  44.2 9.1 %all-to-all-start.1 = ((bf16[16,272,128]{2,1,0:T(8,128)(2,1)}), bf16[16,272,128]{2,1,0:T(8,128)(2,1)S(1)}, u32[]{:S(2)}, u32[]{:S(2)}) async-start(bf16[16,272,128]{2,1,0:T(8,128)(2,1)} %get-tuple-element.27), calls=%async_computation.1 | async-start | bytes 2228224 | tf_op jit(solution)/shard_map/all_to_all | solution.py:396
  53.3 0.0 collective-permute-done.7.b_ref
  53.3 0.0 collective-permute-done.8.c_ref
  53.3 0.0 collective-permute-done.9.d_ref
  53.3 0.0 copy-done.3
  53.3 0.0 copy-start.6
  53.3 2.4 %sum_minor.1.rest_4_.a_ref = bf16[4,512,128]{2,1,0:T(8,128)(2,1)} custom-call(bf16[4,512,128]{2,1,0:T(8,128)(2,1)S(1)} %copy-done.3, bf16[4,512,128]{2,1,0:T(8,128)(2,1)} %collective-permute-done.7.b_ref, bf16[4,512,128]{2,1,0:T(8,128)(2,1)} %collective-permute-done.8.c_ref, bf16[4,512,128]{2,1,0:T(8,128)(2,1)} %collective-permute-done.9.d_ref, ...), custom_call_target="tpu_custom_call" | custom-call | flops 30000001024 | bytes 1000 | tf_op jit(solution)/shard_map/sum_minor/pallas_call | solution.py:78
  55.7 1.9 %collective-permute-start.12 = (bf16[4,512,128]{2,1,0:T(8,128)(2,1)}, bf16[4,512,128]{2,1,0:T(8,128)(2,1)}, u32[]{:S(2)}, u32[]{:S(2)}) collective-permute-start(bf16[4,512,128]{2,1,0:T(8,128)(2,1)} %sum_minor.1.rest_4_.a_ref), channel_id=1, source_target_pairs={{0,8},{1,33},{2,10},{3,35},{4,12},{5,37},{6,14},{7,39},{8,16},{9,4... | collective-permute-start | bytes 1572872 | tf_op jit(solution)/shard_map/ppermute | solution.py:392
  57.7 2.7 %collective-permute-start.11 = (bf16[4,512,128]{2,1,0:T(8,128)(2,1)}, bf16[4,512,128]{2,1,0:T(8,128)(2,1)}, u32[]{:S(2)}, u32[]{:S(2)}) collective-permute-start(bf16[4,512,128]{2,1,0:T(8,128)(2,1)} %sum_minor.1.rest_4_.a_ref), channel_id=1, source_target_pairs={{0,16},{1,65},{2,18},{3,67},{4,20},{5,69},{6,22},{7,71},{8,24},{9,... | collective-permute-start | bytes 1572872 | tf_op jit(solution)/shard_map/ppermute | solution.py:392
  60.3 1.5 %collective-permute-start.10 = (bf16[4,512,128]{2,1,0:T(8,128)(2,1)}, bf16[4,512,128]{2,1,0:T(8,128)(2,1)}, u32[]{:S(2)}, u32[]{:S(2)}) collective-permute-start(bf16[4,512,128]{2,1,0:T(8,128)(2,1)} %sum_minor.1.rest_4_.a_ref), channel_id=1, source_target_pairs={{0,24},{1,97},{2,26},{3,99},{4,28},{5,101},{6,30},{7,103},{8,0},{9... | collective-permute-start | bytes 1572872 | tf_op jit(solution)/shard_map/ppermute | solution.py:392
  61.8 0.0 collective-permute-done.6.rest_1_
  61.8 10.7 %all-to-all-done.1.rest_2_.gathered_ref = bf16[16,272,128]{2,1,0:T(8,128)(2,1)S(1)} async-done(((bf16[16,272,128]{2,1,0:T(8,128)(2,1)}), bf16[16,272,128]{2,1,0:T(8,128)(2,1)S(1)}, u32[]{:S(2)}, u32[]{:S(2)}) %all-to-all-start.1) | async-done | bytes 1114144 | tf_op jit(solution)/shard_map/all_to_all | solution.py:396
  72.5 2.7 %reduced_rows.1 = (bf16[2,128,128]{2,1,0:T(8,128)(2,1)S(1)}, bf16[16,256,128]{2,1,0:T(8,128)(2,1)}) custom-call(bf16[4,2,128,256]{3,2,1,0:T(8,128)(2,1)S(1)} %get-tuple-element.26.rest_0_, bf16[4,2,128,256]{3,2,1,0:T(8,128)(2,1)} %collective-permute-done.6.rest_1_, bf16[16,272,128]{2,1,0:T(8,128)(2,1)S(1)} %all-to-all-done.1.rest_2_.gathered_ref, ...), custom_call_target="tpu_custom_call" | custom-call | flops 30000001024 | bytes 1000 | tf_op jit(solution)/shard_map/reduced_rows/pallas_call | solution.py:191
  75.2 3.8 %all-to-all-start.2 = ((bf16[16,256,128]{2,1,0:T(8,128)(2,1)}), bf16[16,256,128]{2,1,0:T(8,128)(2,1)S(1)}, u32[]{:S(2)}, u32[]{:S(2)}) async-start(bf16[16,256,128]{2,1,0:T(8,128)(2,1)} %get-tuple-element.31), calls=%async_computation.2 | async-start | bytes 2097152 | tf_op jit(solution)/shard_map/all_to_all | solution.py:396
  79.0 0.0 collective-permute-done.12.d_ref
  79.0 1.9 %collective-permute-done.11.c_ref = bf16[4,512,128]{2,1,0:T(8,128)(2,1)} collective-permute-done((bf16[4,512,128]{2,1,0:T(8,128)(2,1)}, bf16[4,512,128]{2,1,0:T(8,128)(2,1)}, u32[]{:S(2)}, u32[]{:S(2)}) %collective-permute-start.11) | collective-permute-done | bytes 524320 | tf_op jit(solution)/shard_map/ppermute | solution.py:392
  81.0 0.8 collective-permute-done.10.b_ref
  81.7 2.6 %sum_major.1.rest_3_.rest_0_ = bf16[4,512,128]{2,1,0:T(8,128)(2,1)} custom-call(bf16[4,512,128]{2,1,0:T(8,128)(2,1)} %sum_minor.1.rest_4_.a_ref, bf16[4,512,128]{2,1,0:T(8,128)(2,1)} %collective-permute-done.10.b_ref, bf16[4,512,128]{2,1,0:T(8,128)(2,1)} %collective-permute-done.11.c_ref, bf16[4,512,128]{2,1,0:T(8,128)(2,1)} %collective-permute-done.12.d_ref, ...), custom_call_target="tpu_custom_call" | custom-call | flops 30000001024 | bytes 1000 | tf_op jit(solution)/shard_map/sum_major/pallas_call | solution.py:78
  84.3 0.5 collective-permute-start.15
  84.9 2.7 %collective-permute-start.14 = (bf16[4,512,128]{2,1,0:T(8,128)(2,1)}, bf16[4,512,128]{2,1,0:T(8,128)(2,1)}, u32[]{:S(2)}, u32[]{:S(2)}) collective-permute-start(bf16[4,512,128]{2,1,0:T(8,128)(2,1)} %sum_major.1.rest_3_.rest_0_), channel_id=1, source_target_pairs={{0,64},{1,17},{2,66},{3,19},{4,68},{5,21},{6,70},{7,23},{8,72},{9,... | collective-permute-start | bytes 1572872 | tf_op jit(solution)/shard_map/ppermute | solution.py:392
  87.6 2.5 %collective-permute-start.13 = (bf16[4,512,128]{2,1,0:T(8,128)(2,1)}, bf16[4,512,128]{2,1,0:T(8,128)(2,1)}, u32[]{:S(2)}, u32[]{:S(2)}) collective-permute-start(bf16[4,512,128]{2,1,0:T(8,128)(2,1)} %sum_major.1.rest_3_.rest_0_), channel_id=1, source_target_pairs={{0,96},{1,25},{2,98},{3,27},{4,100},{5,29},{6,102},{7,31},{8,104},... | collective-permute-start | bytes 1572872 | tf_op jit(solution)/shard_map/ppermute | solution.py:392
  90.1 0.0 collective-permute-done.5.rest_1_
  90.1 4.5 %all-to-all-done.2.rest_2_ = bf16[16,256,128]{2,1,0:T(8,128)(2,1)S(1)} async-done(((bf16[16,256,128]{2,1,0:T(8,128)(2,1)}), bf16[16,256,128]{2,1,0:T(8,128)(2,1)S(1)}, u32[]{:S(2)}, u32[]{:S(2)}) %all-to-all-start.2) | async-done | bytes 1048608 | tf_op jit(solution)/shard_map/all_to_all | solution.py:396
  94.6 2.7 %last_rows.1 = (bf16[2,128,128]{2,1,0:T(8,128)(2,1)S(1)}, bf16[16,256,128]{2,1,0:T(8,128)(2,1)}) custom-call(bf16[4,2,128,256]{3,2,1,0:T(8,128)(2,1)S(1)} %get-tuple-element.25.rest_0_, bf16[4,2,128,256]{3,2,1,0:T(8,128)(2,1)} %collective-permute-done.5.rest_1_, bf16[16,256,128]{2,1,0:T(8,128)(2,1)S(1)} %all-to-all-done.2.rest_2_, ...), custom_call_target="tpu_custom_call" | custom-call | flops 30000001024 | bytes 1000 | tf_op jit(solution)/shard_map/last_rows/pallas_call | solution.py:191
  97.3 4.6 %all-to-all-start.3 = ((bf16[16,256,128]{2,1,0:T(8,128)(2,1)}), bf16[16,256,128]{2,1,0:T(8,128)(2,1)S(1)}, u32[]{:S(2)}, u32[]{:S(2)}) async-start(bf16[16,256,128]{2,1,0:T(8,128)(2,1)} %get-tuple-element.36), calls=%async_computation.3 | async-start | bytes 2097152 | tf_op jit(solution)/shard_map/all_to_all | solution.py:396
  101.8 0.0 collective-permute-done.15.rest_3_
  101.8 2.2 %collective-permute-done.14.rest_2_ = bf16[4,512,128]{2,1,0:T(8,128)(2,1)} collective-permute-done((bf16[4,512,128]{2,1,0:T(8,128)(2,1)}, bf16[4,512,128]{2,1,0:T(8,128)(2,1)}, u32[]{:S(2)}, u32[]{:S(2)}) %collective-permute-start.14) | collective-permute-done | bytes 524320 | tf_op jit(solution)/shard_map/ppermute | solution.py:392
  104.0 0.0 collective-permute-done.13.rest_1_
  104.0 6.8 %first_loads.1 = (f32[4096,256]{1,0:T(8,128)}, s32[1,2048]{1,0:T(1,128)S(1)}, f32[1,2048]{1,0:T(1,128)S(1)}) custom-call(bf16[16,272,128]{2,1,0:T(8,128)(2,1)S(1)} %all-to-all-done.1.rest_2_.gathered_ref, bf16[4,512,128]{2,1,0:T(8,128)(2,1)} %sum_major.1.rest_3_.rest_0_, bf16[4,512,128]{2,1,0:T(8,128)(2,1)} %collective-permute-done.13.rest_1_, ...), custom_call_target="tpu_custom_call" | custom-call | flops 30000001024 | bytes 1000 | tf_op jit(solution)/shard_map/first_loads/pallas_call | solution.py:275
  110.8 0.7 pad_maximum_fusion.1
  111.5 5.9 %all-to-all-done.3.gathered_ref = bf16[16,256,128]{2,1,0:T(8,128)(2,1)S(1)} async-done(((bf16[16,256,128]{2,1,0:T(8,128)(2,1)}), bf16[16,256,128]{2,1,0:T(8,128)(2,1)S(1)}, u32[]{:S(2)}, u32[]{:S(2)}) %all-to-all-start.3) | async-done | bytes 1048608 | tf_op jit(solution)/shard_map/all_to_all | solution.py:396
  117.4 7.4 %all_loads.1 = (bf16[4096,256]{1,0:T(8,128)(2,1)S(1)}, bf16[8,2,1024,512]{3,2,1,0:T(8,128)(2,1)S(1)}) custom-call(s32[1,2048]{1,0:T(1,128)S(1)} %get-tuple-element.34.ids, f32[1,2048]{1,0:T(1,128)S(1)} %get-tuple-element.35.weights, bf16[16,256,128]{2,1,0:T(8,128)(2,1)S(1)} %all-to-all-done.3.gathered_ref, f32[4096,256]{1,0:T(8,128)} %get-tuple-element.37.first_ref, ...), custom_call_target="tpu_custom_call" | custom-call | tf_op jit(solution)/shard_map/all_loads/pallas_call | solution.py:323
  124.8 5.3 %stress.1 = bf16[2,1024,128]{2,1,0:T(8,128)(2,1)} custom-call(bf16[4096,256]{1,0:T(8,128)(2,1)S(1)} %get-tuple-element.38.loads_ref, bf16[8,2,1024,512]{3,2,1,0:T(8,128)(2,1)S(1)} %get-tuple-element.39.maps_ref), custom_call_target="tpu_custom_call" | custom-call | tf_op jit(solution)/shard_map/stress/pallas_call | solution.py:361
  (23 shorter events, 0.1 us)
Async XLA Ops:
  7.2 0.9 copy-start.9
  7.2 1.0 copy-start.10
  7.2 1.0 copy-start.11
  7.2 5.8 %copy-start.12 = (bf16[2,128,128]{2,1,0:T(8,128)(2,1)S(1)}, bf16[2,128,128]{2,1,0:T(8,128)(2,1)}, u32[]{:S(2)}) copy-start(bf16[2,128,128]{2,1,0:T(8,128)(2,1)} %param.11) | copy-start | bytes 196612
  7.2 110.2 %all-gather.3.cloned.1.call-start = ((), (), s32[]{:S(2)}) async-start(), calls=%async_computation.4 | async-start | bytes 18874368 | tf_op jit(solution)/shard_map/all_gather | solution.py:413
  7.9 14.2 %copy-start.13 = (bf16[3072]{0:T(1024)(128)(2,1)S(1)}, bf16[3072]{0:T(1024)(128)(2,1)}, u32[]{:S(2)}) copy-start(bf16[3072]{0:T(1024)(128)(2,1)} %param.18) | copy-start | bytes 18436
  8.0 14.2 %copy-start = (bf16[2,3072,128]{2,1,0:T(8,128)(2,1)S(1)}, bf16[2,3072,128]{2,1,0:T(8,128)(2,1)}, u32[]{:S(2)}) copy-start(bf16[2,3072,128]{2,1,0:T(8,128)(2,1)} %earlier_ref.1) | copy-start | bytes 4718596
  8.0 14.2 %copy-start.1 = (s32[3072]{0:T(1024)S(1)}, s32[3072]{0:T(1024)}, u32[]{:S(2)}) copy-start(s32[3072]{0:T(1024)} %param.17) | copy-start | bytes 36868
  8.2 26.4 %collective-permute-start.2 = (bf16[3,2,128,256]{3,2,1,0:T(8,128)(2,1)S(1)}, bf16[3,2,128,256]{3,2,1,0:T(8,128)(2,1)S(1)}, u32[]{:S(2)}, u32[]{:S(2)}) collective-permute-start(bf16[3,2,128,256]{3,2,1,0:T(8,128)(2,1)S(1)} %pad_maximum_fusion.refs_0_), channel_id=1, source_target_pairs={{0,6},{1,7},{2,0},{3,1},{4,2},{5,3},{6,4},{7,5},{8,14},{9,15},{10,... | collective-permute-start | bytes 1179656 | tf_op jit(solution)/shard_map/ppermute | solution.py:376
  11.4 24.7 %collective-permute-start.1 = (bf16[3,2,128,256]{3,2,1,0:T(8,128)(2,1)S(1)}, bf16[3,2,128,256]{3,2,1,0:T(8,128)(2,1)}, u32[]{:S(2)}, u32[]{:S(2)}) collective-permute-start(bf16[3,2,128,256]{3,2,1,0:T(8,128)(2,1)S(1)} %pad_maximum_fusion.refs_0_), channel_id=1, source_target_pairs={{0,4},{1,5},{2,6},{3,7},{4,0},{5,1},{6,2},{7,3},{8,12},{9,13},{10,... | collective-permute-start | bytes 1179656 | tf_op jit(solution)/shard_map/ppermute | solution.py:376
  12.0 24.3 %collective-permute-start = (bf16[3,2,128,256]{3,2,1,0:T(8,128)(2,1)S(1)}, bf16[3,2,128,256]{3,2,1,0:T(8,128)(2,1)}, u32[]{:S(2)}, u32[]{:S(2)}) collective-permute-start(bf16[3,2,128,256]{3,2,1,0:T(8,128)(2,1)S(1)} %pad_maximum_fusion.refs_0_), channel_id=1, source_target_pairs={{0,2},{1,3},{2,4},{3,5},{4,6},{5,7},{6,0},{7,1},{8,10},{9,11},{10,... | collective-permute-start | bytes 1179656 | tf_op jit(solution)/shard_map/ppermute | solution.py:376
  14.2 27.1 %all-to-all-start = ((bf16[16,256,128]{2,1,0:T(8,128)(2,1)}), bf16[16,256,128]{2,1,0:T(8,128)(2,1)S(1)}, u32[]{:S(2)}, u32[]{:S(2)}) async-start(bf16[16,256,128]{2,1,0:T(8,128)(2,1)} %broadcast_in_dim.16), calls=%async_computation | async-start | bytes 2097152 | tf_op jit(solution)/shard_map/all_to_all | solution.py:396
  30.0 8.2 %copy-start.2 = (bf16[4,512,128]{2,1,0:T(8,128)(2,1)}, bf16[4,512,128]{2,1,0:T(8,128)(2,1)S(1)}, u32[]{:S(2)}) copy-start(bf16[4,512,128]{2,1,0:T(8,128)(2,1)S(1)} %get-tuple-element.21.refs_4_.a_ref) | copy-start | bytes 1572868
  30.0 23.2 %collective-permute-start.7 = (bf16[4,512,128]{2,1,0:T(8,128)(2,1)}, bf16[4,512,128]{2,1,0:T(8,128)(2,1)}, u32[]{:S(2)}, u32[]{:S(2)}) collective-permute-start(bf16[4,512,128]{2,1,0:T(8,128)(2,1)} %get-tuple-element.28), channel_id=1, source_target_pairs={{0,32},{1,9},{2,34},{3,11},{4,36},{5,13},{6,38},{7,15},{8,40},{9,1... | collective-permute-start | bytes 1572872 | tf_op jit(solution)/shard_map/ppermute | solution.py:392
  32.0 21.3 %collective-permute-start.8 = (bf16[4,512,128]{2,1,0:T(8,128)(2,1)}, bf16[4,512,128]{2,1,0:T(8,128)(2,1)}, u32[]{:S(2)}, u32[]{:S(2)}) collective-permute-start(bf16[4,512,128]{2,1,0:T(8,128)(2,1)} %get-tuple-element.29), channel_id=1, source_target_pairs={{0,64},{1,17},{2,66},{3,19},{4,68},{5,21},{6,70},{7,23},{8,72},{9,... | collective-permute-start | bytes 1572872 | tf_op jit(solution)/shard_map/ppermute | solution.py:392
  34.6 1.7 %copy-start.14 = (bf16[3,2,128,256]{3,2,1,0:T(8,128)(2,1)}, bf16[3,2,128,256]{3,2,1,0:T(8,128)(2,1)S(1)}, u32[]{:S(2)}) copy-start(bf16[3,2,128,256]{3,2,1,0:T(8,128)(2,1)S(1)} %collective-permute-done.2.refs_3_) | copy-start | bytes 1179652
  34.7 18.6 %collective-permute-start.9 = (bf16[4,512,128]{2,1,0:T(8,128)(2,1)}, bf16[4,512,128]{2,1,0:T(8,128)(2,1)}, u32[]{:S(2)}, u32[]{:S(2)}) collective-permute-start(bf16[4,512,128]{2,1,0:T(8,128)(2,1)} %get-tuple-element.30), channel_id=1, source_target_pairs={{0,96},{1,25},{2,98},{3,27},{4,100},{5,29},{6,102},{7,31},{8,104},... | collective-permute-start | bytes 1572872 | tf_op jit(solution)/shard_map/ppermute | solution.py:392
  36.3 5.0 %copy-start.7 = (s32[2,128]{1,0:T(2,128)S(1)}, s32[2,128]{1,0:T(2,128)}, u32[]{:S(2)}) copy-start(s32[2,128]{1,0:T(2,128)} %rest_5_.1) | copy-start | bytes 3076
  36.3 5.0 %copy-start.8 = (bf16[2,128]{1,0:T(2,128)(2,1)S(1)}, bf16[2,128]{1,0:T(2,128)(2,1)}, u32[]{:S(2)}) copy-start(bf16[2,128]{1,0:T(2,128)(2,1)} %rest_6_.1) | copy-start | bytes 1540
  38.3 1.6 %collective-permute-start.3 = (bf16[2,2,128,256]{3,2,1,0:T(8,128)(2,1)S(1)}, bf16[2,2,128,256]{3,2,1,0:T(8,128)(2,1)S(1)}, u32[]{:S(2)}, u32[]{:S(2)}) collective-permute-start(bf16[2,2,128,256]{3,2,1,0:T(8,128)(2,1)S(1)} %get-tuple-element.22.rest_0_), channel_id=1, source_target_pairs={{0,1},{1,0},{2,3},{3,2},{4,5},{5,4},{6,7},{7,6},{8,9},{9,8},{10,11... | collective-permute-start | bytes 786440 | tf_op jit(solution)/shard_map/ppermute | solution.py:380
  38.4 1.9 %collective-permute-start.4 = (bf16[2,2,128,256]{3,2,1,0:T(8,128)(2,1)S(1)}, bf16[2,2,128,256]{3,2,1,0:T(8,128)(2,1)S(1)}, u32[]{:S(2)}, u32[]{:S(2)}) collective-permute-start(bf16[2,2,128,256]{3,2,1,0:T(8,128)(2,1)S(1)} %get-tuple-element.23.rest_1_), channel_id=1, source_target_pairs={{0,1},{1,0},{2,3},{3,2},{4,5},{5,4},{6,7},{7,6},{8,9},{9,8},{10,11... | collective-permute-start | bytes 786440 | tf_op jit(solution)/shard_map/ppermute | solution.py:380
  39.9 50.2 %collective-permute-start.5 = (bf16[4,2,128,256]{3,2,1,0:T(8,128)(2,1)S(1)}, bf16[4,2,128,256]{3,2,1,0:T(8,128)(2,1)}, u32[]{:S(2)}, u32[]{:S(2)}) collective-permute-start(bf16[4,2,128,256]{3,2,1,0:T(8,128)(2,1)S(1)} %get-tuple-element.25.rest_0_), channel_id=1, source_target_pairs={{0,1},{1,0},{2,3},{3,2},{4,5},{5,4},{6,7},{7,6},{8,9},{9,8},{10,11... | collective-permute-start | bytes 1572872 | tf_op jit(solution)/shard_map/ppermute | solution.py:380
  40.3 0.7 copy-start.4
  41.0 12.3 %copy-start.3 = (bf16[4,512,128]{2,1,0:T(8,128)(2,1)S(1)}, bf16[4,512,128]{2,1,0:T(8,128)(2,1)}, u32[]{:S(2)}) copy-start(bf16[4,512,128]{2,1,0:T(8,128)(2,1)} %copy-done.2) | copy-start | bytes 1572868
  41.0 20.8 %collective-permute-start.6 = (bf16[4,2,128,256]{3,2,1,0:T(8,128)(2,1)S(1)}, bf16[4,2,128,256]{3,2,1,0:T(8,128)(2,1)}, u32[]{:S(2)}, u32[]{:S(2)}) collective-permute-start(bf16[4,2,128,256]{3,2,1,0:T(8,128)(2,1)S(1)} %get-tuple-element.26.rest_0_), channel_id=1, source_target_pairs={{0,1},{1,0},{2,3},{3,2},{4,5},{5,4},{6,7},{7,6},{8,9},{9,8},{10,11... | collective-permute-start | bytes 1572872 | tf_op jit(solution)/shard_map/ppermute | solution.py:380
  41.3 1.0 copy-start.5
  44.2 28.3 %all-to-all-start.1 = ((bf16[16,272,128]{2,1,0:T(8,128)(2,1)}), bf16[16,272,128]{2,1,0:T(8,128)(2,1)S(1)}, u32[]{:S(2)}, u32[]{:S(2)}) async-start(bf16[16,272,128]{2,1,0:T(8,128)(2,1)} %get-tuple-element.27), calls=%async_computation.1 | async-start | bytes 2228224 | tf_op jit(solution)/shard_map/all_to_all | solution.py:396
  53.3 19.2 %copy-start.6 = (bf16[2,128,128]{2,1,0:T(8,128)(2,1)S(1)}, bf16[2,128,128]{2,1,0:T(8,128)(2,1)}, u32[]{:S(2)}) copy-start(bf16[2,128,128]{2,1,0:T(8,128)(2,1)} %rest_3_.1) | copy-start | bytes 196612
  55.7 23.3 %collective-permute-start.12 = (bf16[4,512,128]{2,1,0:T(8,128)(2,1)}, bf16[4,512,128]{2,1,0:T(8,128)(2,1)}, u32[]{:S(2)}, u32[]{:S(2)}) collective-permute-start(bf16[4,512,128]{2,1,0:T(8,128)(2,1)} %sum_minor.1.rest_4_.a_ref), channel_id=1, source_target_pairs={{0,8},{1,33},{2,10},{3,35},{4,12},{5,37},{6,14},{7,39},{8,16},{9,4... | collective-permute-start | bytes 1572872 | tf_op jit(solution)/shard_map/ppermute | solution.py:392
  57.7 23.3 %collective-permute-start.11 = (bf16[4,512,128]{2,1,0:T(8,128)(2,1)}, bf16[4,512,128]{2,1,0:T(8,128)(2,1)}, u32[]{:S(2)}, u32[]{:S(2)}) collective-permute-start(bf16[4,512,128]{2,1,0:T(8,128)(2,1)} %sum_minor.1.rest_4_.a_ref), channel_id=1, source_target_pairs={{0,16},{1,65},{2,18},{3,67},{4,20},{5,69},{6,22},{7,71},{8,24},{9,... | collective-permute-start | bytes 1572872 | tf_op jit(solution)/shard_map/ppermute | solution.py:392
  60.3 21.4 %collective-permute-start.10 = (bf16[4,512,128]{2,1,0:T(8,128)(2,1)}, bf16[4,512,128]{2,1,0:T(8,128)(2,1)}, u32[]{:S(2)}, u32[]{:S(2)}) collective-permute-start(bf16[4,512,128]{2,1,0:T(8,128)(2,1)} %sum_minor.1.rest_4_.a_ref), channel_id=1, source_target_pairs={{0,24},{1,97},{2,26},{3,99},{4,28},{5,101},{6,30},{7,103},{8,0},{9... | collective-permute-start | bytes 1572872 | tf_op jit(solution)/shard_map/ppermute | solution.py:392
  75.2 19.4 %all-to-all-start.2 = ((bf16[16,256,128]{2,1,0:T(8,128)(2,1)}), bf16[16,256,128]{2,1,0:T(8,128)(2,1)S(1)}, u32[]{:S(2)}, u32[]{:S(2)}) async-start(bf16[16,256,128]{2,1,0:T(8,128)(2,1)} %get-tuple-element.31), calls=%async_computation.2 | async-start | bytes 2097152 | tf_op jit(solution)/shard_map/all_to_all | solution.py:396
  84.3 17.5 %collective-permute-start.15 = (bf16[4,512,128]{2,1,0:T(8,128)(2,1)}, bf16[4,512,128]{2,1,0:T(8,128)(2,1)}, u32[]{:S(2)}, u32[]{:S(2)}) collective-permute-start(bf16[4,512,128]{2,1,0:T(8,128)(2,1)} %sum_major.1.rest_3_.rest_0_), channel_id=1, source_target_pairs={{0,32},{1,9},{2,34},{3,11},{4,36},{5,13},{6,38},{7,15},{8,40},{9,1... | collective-permute-start | bytes 1572872 | tf_op jit(solution)/shard_map/ppermute | solution.py:392
  84.9 19.2 %collective-permute-start.14 = (bf16[4,512,128]{2,1,0:T(8,128)(2,1)}, bf16[4,512,128]{2,1,0:T(8,128)(2,1)}, u32[]{:S(2)}, u32[]{:S(2)}) collective-permute-start(bf16[4,512,128]{2,1,0:T(8,128)(2,1)} %sum_major.1.rest_3_.rest_0_), channel_id=1, source_target_pairs={{0,64},{1,17},{2,66},{3,19},{4,68},{5,21},{6,70},{7,23},{8,72},{9,... | collective-permute-start | bytes 1572872 | tf_op jit(solution)/shard_map/ppermute | solution.py:392
  87.6 16.4 %collective-permute-start.13 = (bf16[4,512,128]{2,1,0:T(8,128)(2,1)}, bf16[4,512,128]{2,1,0:T(8,128)(2,1)}, u32[]{:S(2)}, u32[]{:S(2)}) collective-permute-start(bf16[4,512,128]{2,1,0:T(8,128)(2,1)} %sum_major.1.rest_3_.rest_0_), channel_id=1, source_target_pairs={{0,96},{1,25},{2,98},{3,27},{4,100},{5,29},{6,102},{7,31},{8,104},... | collective-permute-start | bytes 1572872 | tf_op jit(solution)/shard_map/ppermute | solution.py:392
  97.3 20.1 %all-to-all-start.3 = ((bf16[16,256,128]{2,1,0:T(8,128)(2,1)}), bf16[16,256,128]{2,1,0:T(8,128)(2,1)S(1)}, u32[]{:S(2)}, u32[]{:S(2)}) async-start(bf16[16,256,128]{2,1,0:T(8,128)(2,1)} %get-tuple-element.36), calls=%async_computation.3 | async-start | bytes 2097152 | tf_op jit(solution)/shard_map/all_to_all | solution.py:396
Sparse Core Ops, SparseCore 0:
  9.8 91.7 all-gather.2

commit v6 on v5

--- a/solution.py
+++ b/solution.py
@@ -66,24 +66,44 @@
     )(ids, weights, earlier)
 
 
-def sum_loads_kernel(a_ref, b_ref, c_ref, d_ref, tie_ref, out_ref):
+def sum_loads_kernel(*refs):
+    parts, (out_ref, held, sems) = refs[:4], refs[5:]
+    copies = [
+        [
+            pltpu.make_async_copy(parts[k].at[block], held.at[k, block], sems.at[k, block])
+            for k in range(4)
+        ]
+        for block in range(4)
+    ]
     for block in range(4):
-        total = a_ref[block].astype(F32) + b_ref[block].astype(F32)
-        total += c_ref[block].astype(F32) + d_ref[block].astype(F32)
+        for copy in copies[block]:
+            copy.start()
+    for block in range(4):
+        for copy in copies[block]:
+            copy.wait()
+        total = held[0, block].astype(F32) + held[1, block].astype(F32)
+        total += held[2, block].astype(F32) + held[3, block].astype(F32)
         out_ref[block] = total.astype(BF16)
 
 
 def sum_loads(name, parts, tie):
-    vmem = pl.BlockSpec(memory_space=pltpu.VMEM)
     return pl.pallas_call(
         sum_loads_kernel,
         out_shape=jax.ShapeDtypeStruct(parts[0].shape, BF16),
-        in_specs=[vmem] * 4 + [pl.BlockSpec(memory_space=pl.ANY)],
-        out_specs=vmem,
+        in_specs=[pl.BlockSpec(memory_space=pl.ANY)] * 5,
+        out_specs=pl.BlockSpec(memory_space=pltpu.VMEM),
+        scratch_shapes=[
+            pltpu.VMEM((4, *parts[0].shape), BF16),
+            pltpu.SemaphoreType.DMA((4, 4)),
+        ],
         compiler_params=PARAMS,
         cost_estimate=COST,
         name=name,
-    )(*parts, tie)
+    )(
+        parts[0],
+        *[pltpu.with_memory_space_constraint(part, pltpu.HBM) for part in parts[1:]],
+        tie,
+    )
 
 
 def pack_factors_kernel(*refs):

time: 138 us -> 138 us (level)
  no operation moved by 1% of the time
where the time goes in v6:
time: 138 us; the launch traced here: 137 us
  starting transfers between devices  49.6 us (36%)
  Pallas kernels  42 us (30%)
  waiting for transfers between devices  27.1 us (20%)
  between operations  14.3 us (10%)
  local copies, waits for them, and re-layouts  3.14 us (2%)
    all_to_all x4, starting transfers between devices, to_rows(): return lax.all_to_all(copies, 'row', 0, 0, tiled=True)  25.3 us
    all_to_all x4, waiting for transfers between devices, to_rows(): return lax.all_to_all(copies, 'row', 0, 0, tiled=True)  20.3 us
    ppermute x9, starting transfers between devices, along_axis(): return lax.ppermute(value, ('row', 'col'), pairs)  18.2 us
    pallas_call x1, Pallas kernels, old_loads(): pl.pallas_call(functools.partial(old_loads_kernel, chunk=512), out_shape=...  7.88 us
    pallas_call x1, Pallas kernels, all_loads(): pl.pallas_call(all_loads_kernel, out_shape=(pltpu.VMEM((PATCHES, 256), BF...  7.4 us
    pallas_call x3, Pallas kernels, rows_product(): pl.pallas_call(functools.partial(rows_kernel, parts=len(factors), base=ba...  7.31 us
    pallas_call x1, Pallas kernels, first_loads(): pl.pallas_call(first_loads_kernel, out_shape=(pltpu.HBM((PATCHES, 256), F...  6.82 us
    pallas_call x2, Pallas kernels, sum_loads(): pl.pallas_call(sum_loads_kernel, out_shape=jax.ShapeDtypeStruct(parts[0]....  5.39 us
  transfers between devices with their start and end apart: 21, of which 8 were waited for; matrix products, arithmetic and copies ran while one was open for 1% of the time, Pallas kernels for 21%

profile of v6, /device:TPU:0, one launch (start us, length us, event | category | flops | bytes accessed | tf_op | source)
XLA Modules:
  0.0 136.9 jit_solution(11588937105020064199)
XLA Ops:
  7.2 0.0 copy-start.9
  7.2 0.0 copy-start.10
  7.2 0.0 all-gather.3.cloned.1.call-start
  7.3 0.7 all-gather.3.cloned.1.call-update
  8.0 0.1 copy-done.9
  8.1 0.1 copy-done.10
  8.1 0.1 copy-done.11
  8.2 3.2 %collective-permute-start.2 = (bf16[3,2,128,256]{3,2,1,0:T(8,128)(2,1)S(1)}, bf16[3,2,128,256]{3,2,1,0:T(8,128)(2,1)S(1)}, u32[]{:S(2)}, u32[]{:S(2)}) collective-permute-start(bf16[3,2,128,256]{3,2,1,0:T(8,128)(2,1)S(1)} %pad_maximum_fusion.refs_0_), channel_id=1, source_target_pairs={{0,6},{1,7},{2,0},{3,1},{4,2},{5,3},{6,4},{7,5},{8,14},{9,15},{10,... | collective-permute-start | bytes 1179656 | tf_op jit(solution)/shard_map/ppermute | solution.py:396
  11.4 0.6 collective-permute-start.1
  12.0 1.0 collective-permute-start
  13.0 1.2 broadcast_in_dim.16
  14.2 7.9 %all-to-all-start = ((bf16[16,256,128]{2,1,0:T(8,128)(2,1)}), bf16[16,256,128]{2,1,0:T(8,128)(2,1)S(1)}, u32[]{:S(2)}, u32[]{:S(2)}) async-start(bf16[16,256,128]{2,1,0:T(8,128)(2,1)} %broadcast_in_dim.16), calls=%async_computation | async-start | bytes 2097152 | tf_op jit(solution)/shard_map/all_to_all | solution.py:416
  22.2 7.9 %old_loads.1 = (bf16[4,512,128]{2,1,0:T(8,128)(2,1)S(1)}, bf16[4,512,128]{2,1,0:T(8,128)(2,1)}, bf16[4,512,128]{2,1,0:T(8,128)(2,1)}, bf16[4,512,128]{2,1,0:T(8,128)(2,1)}) custom-call(s32[1,3072]{1,0:T(1,128)S(1)} %bitcast.10, bf16[1,3072]{1,0:T(2,128)(2,1)S(1)} %broadcast_in_dim.14.weights_ref, bf16[2,3072,128]{2,1,0:T(8,128)(2,1)S(1)} %copy-done), custom_call_target="tpu_custom_call" | custom-call | tf_op jit(solution)/shard_map/old_loads/pallas_call | solution.py:58
  30.0 1.9 %collective-permute-start.7 = (bf16[4,512,128]{2,1,0:T(8,128)(2,1)}, bf16[4,512,128]{2,1,0:T(8,128)(2,1)}, u32[]{:S(2)}, u32[]{:S(2)}) collective-permute-start(bf16[4,512,128]{2,1,0:T(8,128)(2,1)} %get-tuple-element.28), channel_id=1, source_target_pairs={{0,32},{1,9},{2,34},{3,11},{4,36},{5,13},{6,38},{7,15},{8,40},{9,1... | collective-permute-start | bytes 1572872 | tf_op jit(solution)/shard_map/ppermute | solution.py:412
  32.0 2.7 %collective-permute-start.8 = (bf16[4,512,128]{2,1,0:T(8,128)(2,1)}, bf16[4,512,128]{2,1,0:T(8,128)(2,1)}, u32[]{:S(2)}, u32[]{:S(2)}) collective-permute-start(bf16[4,512,128]{2,1,0:T(8,128)(2,1)} %get-tuple-element.29), channel_id=1, source_target_pairs={{0,64},{1,17},{2,66},{3,19},{4,68},{5,21},{6,70},{7,23},{8,72},{9,... | collective-permute-start | bytes 1572872 | tf_op jit(solution)/shard_map/ppermute | solution.py:412
  34.6 0.0 collective-permute-done.2.refs_3_
  34.7 1.5 %collective-permute-start.9 = (bf16[4,512,128]{2,1,0:T(8,128)(2,1)}, bf16[4,512,128]{2,1,0:T(8,128)(2,1)}, u32[]{:S(2)}, u32[]{:S(2)}) collective-permute-start(bf16[4,512,128]{2,1,0:T(8,128)(2,1)} %get-tuple-element.30), channel_id=1, source_target_pairs={{0,96},{1,25},{2,98},{3,27},{4,100},{5,29},{6,102},{7,31},{8,104},... | collective-permute-start | bytes 1572872 | tf_op jit(solution)/shard_map/ppermute | solution.py:412
  36.1 0.0 collective-permute-done.1.refs_2_
  36.1 0.2 collective-permute-done.refs_1_
  36.3 1.9 %pack_factors.1 = (bf16[2,2,128,256]{3,2,1,0:T(8,128)(2,1)S(1)}, bf16[2,2,128,256]{3,2,1,0:T(8,128)(2,1)S(1)}, bf16[4,2,128,256]{3,2,1,0:T(8,128)(2,1)S(1)}, bf16[4,2,128,256]{3,2,1,0:T(8,128)(2,1)S(1)}) custom-call(bf16[3,2,128,256]{3,2,1,0:T(8,128)(2,1)S(1)} %pad_maximum_fusion.refs_0_, bf16[3,2,128,256]{3,2,1,0:T(8,128)(2,1)} %collective-permute-done.refs_1_, ...), custom_call_target="tpu_custom_call" | custom-call | flops 6000000000 | bytes 1000 | tf_op jit(solution)/shard_map/pack_factors/pallas_call | solution.py:123
  38.3 0.1 collective-permute-start.3
  38.4 0.5 collective-permute-start.4
  38.9 1.0 collective-permute-done.3.rest_2_
  39.9 0.3 collective-permute-start.5
  40.2 0.0 collective-permute-done.4.rest_3_
  40.3 0.7 copy-done.4
  41.0 0.3 collective-permute-start.6
  41.3 0.0 all-to-all-done.rest_4_
  41.3 0.0 copy-done.8
  41.3 0.9 copy-done.5
  42.3 1.9 %first_rows.1 = (bf16[2,128,128]{2,1,0:T(8,128)(2,1)S(1)}, bf16[16,272,128]{2,1,0:T(8,128)(2,1)}) custom-call(bf16[2,2,128,256]{3,2,1,0:T(8,128)(2,1)S(1)} %get-tuple-element.22.rest_0_, bf16[2,2,128,256]{3,2,1,0:T(8,128)(2,1)S(1)} %get-tuple-element.23.rest_1_, bf16[2,2,128,256]{3,2,1,0:T(8,128)(2,1)S(1)} %collective-permute-done.3.rest_2_, ...), custom_call_target="tpu_custom_call" | custom-call | flops 1000000000 | bytes 1000 | tf_op jit(solution)/shard_map/first_rows/pallas_call | solution.py:211
  44.2 9.1 %all-to-all-start.1 = ((bf16[16,272,128]{2,1,0:T(8,128)(2,1)}), bf16[16,272,128]{2,1,0:T(8,128)(2,1)S(1)}, u32[]{:S(2)}, u32[]{:S(2)}) async-start(bf16[16,272,128]{2,1,0:T(8,128)(2,1)} %get-tuple-element.27), calls=%async_computation.1 | async-start | bytes 2228224 | tf_op jit(solution)/shard_map/all_to_all | solution.py:416
  53.3 0.0 collective-permute-done.7.refs_1_
  53.3 0.0 collective-permute-done.8.refs_2_
  53.3 0.0 collective-permute-done.9.refs_3_
  53.3 0.0 copy-done.3
  53.3 0.0 copy-start.6
  53.3 2.8 %sum_minor.1.rest_4_.refs_0_ = bf16[4,512,128]{2,1,0:T(8,128)(2,1)} custom-call(bf16[4,512,128]{2,1,0:T(8,128)(2,1)S(1)} %copy-done.3, bf16[4,512,128]{2,1,0:T(8,128)(2,1)} %collective-permute-done.7.refs_1_, bf16[4,512,128]{2,1,0:T(8,128)(2,1)} %collective-permute-done.8.refs_2_, bf16[4,512,128]{2,1,0:T(8,128)(2,1)} %collective-permute-done.9.refs_3_, ...), custom_call_target="tpu_custom_call" | custom-call | flops 30000001024 | bytes 1000 | tf_op jit(solution)/shard_map/sum_minor/pallas_call | solution.py:90
  56.1 2.2 %collective-permute-start.12 = (bf16[4,512,128]{2,1,0:T(8,128)(2,1)}, bf16[4,512,128]{2,1,0:T(8,128)(2,1)}, u32[]{:S(2)}, u32[]{:S(2)}) collective-permute-start(bf16[4,512,128]{2,1,0:T(8,128)(2,1)} %sum_minor.1.rest_4_.refs_0_), channel_id=1, source_target_pairs={{0,8},{1,33},{2,10},{3,35},{4,12},{5,37},{6,14},{7,39},{8,16},{9,4... | collective-permute-start | bytes 1572872 | tf_op jit(solution)/shard_map/ppermute | solution.py:412
  58.3 2.7 %collective-permute-start.11 = (bf16[4,512,128]{2,1,0:T(8,128)(2,1)}, bf16[4,512,128]{2,1,0:T(8,128)(2,1)}, u32[]{:S(2)}, u32[]{:S(2)}) collective-permute-start(bf16[4,512,128]{2,1,0:T(8,128)(2,1)} %sum_minor.1.rest_4_.refs_0_), channel_id=1, source_target_pairs={{0,16},{1,65},{2,18},{3,67},{4,20},{5,69},{6,22},{7,71},{8,24},{9,... | collective-permute-start | bytes 1572872 | tf_op jit(solution)/shard_map/ppermute | solution.py:412
  60.9 1.5 %collective-permute-start.10 = (bf16[4,512,128]{2,1,0:T(8,128)(2,1)}, bf16[4,512,128]{2,1,0:T(8,128)(2,1)}, u32[]{:S(2)}, u32[]{:S(2)}) collective-permute-start(bf16[4,512,128]{2,1,0:T(8,128)(2,1)} %sum_minor.1.rest_4_.refs_0_), channel_id=1, source_target_pairs={{0,24},{1,97},{2,26},{3,99},{4,28},{5,101},{6,30},{7,103},{8,0},{9... | collective-permute-start | bytes 1572872 | tf_op jit(solution)/shard_map/ppermute | solution.py:412
  62.4 0.0 collective-permute-done.6.rest_1_
  62.4 10.1 %all-to-all-done.1.rest_2_.gathered_ref = bf16[16,272,128]{2,1,0:T(8,128)(2,1)S(1)} async-done(((bf16[16,272,128]{2,1,0:T(8,128)(2,1)}), bf16[16,272,128]{2,1,0:T(8,128)(2,1)S(1)}, u32[]{:S(2)}, u32[]{:S(2)}) %all-to-all-start.1) | async-done | bytes 1114144 | tf_op jit(solution)/shard_map/all_to_all | solution.py:416
  72.5 2.7 %reduced_rows.1 = (bf16[2,128,128]{2,1,0:T(8,128)(2,1)S(1)}, bf16[16,256,128]{2,1,0:T(8,128)(2,1)}) custom-call(bf16[4,2,128,256]{3,2,1,0:T(8,128)(2,1)S(1)} %get-tuple-element.26.rest_0_, bf16[4,2,128,256]{3,2,1,0:T(8,128)(2,1)} %collective-permute-done.6.rest_1_, bf16[16,272,128]{2,1,0:T(8,128)(2,1)S(1)} %all-to-all-done.1.rest_2_.gathered_ref, ...), custom_call_target="tpu_custom_call" | custom-call | flops 30000001024 | bytes 1000 | tf_op jit(solution)/shard_map/reduced_rows/pallas_call | solution.py:211
  75.2 3.8 %all-to-all-start.2 = ((bf16[16,256,128]{2,1,0:T(8,128)(2,1)}), bf16[16,256,128]{2,1,0:T(8,128)(2,1)S(1)}, u32[]{:S(2)}, u32[]{:S(2)}) async-start(bf16[16,256,128]{2,1,0:T(8,128)(2,1)} %get-tuple-element.31), calls=%async_computation.2 | async-start | bytes 2097152 | tf_op jit(solution)/shard_map/all_to_all | solution.py:416
  79.0 0.0 collective-permute-done.12.refs_3_
  79.0 2.1 %collective-permute-done.11.refs_2_ = bf16[4,512,128]{2,1,0:T(8,128)(2,1)} collective-permute-done((bf16[4,512,128]{2,1,0:T(8,128)(2,1)}, bf16[4,512,128]{2,1,0:T(8,128)(2,1)}, u32[]{:S(2)}, u32[]{:S(2)}) %collective-permute-start.11) | collective-permute-done | bytes 524320 | tf_op jit(solution)/shard_map/ppermute | solution.py:412
  81.1 0.6 collective-permute-done.10.refs_1_
  81.7 2.6 %sum_major.1.rest_3_.rest_0_ = bf16[4,512,128]{2,1,0:T(8,128)(2,1)} custom-call(bf16[4,512,128]{2,1,0:T(8,128)(2,1)} %sum_minor.1.rest_4_.refs_0_, bf16[4,512,128]{2,1,0:T(8,128)(2,1)} %collective-permute-done.10.refs_1_, bf16[4,512,128]{2,1,0:T(8,128)(2,1)} %collective-permute-done.11.refs_2_, bf16[4,512,128]{2,1,0:T(8,128)(2,1)} %collective-permute-done.12.refs_3_, ...), custom_call_target="tpu_custom_call" | custom-call | flops 30000001024 | bytes 1000 | tf_op jit(solution)/shard_map/sum_major/pallas_call | solution.py:90
  84.4 0.6 collective-permute-start.15
  85.0 2.7 %collective-permute-start.14 = (bf16[4,512,128]{2,1,0:T(8,128)(2,1)}, bf16[4,512,128]{2,1,0:T(8,128)(2,1)}, u32[]{:S(2)}, u32[]{:S(2)}) collective-permute-start(bf16[4,512,128]{2,1,0:T(8,128)(2,1)} %sum_major.1.rest_3_.rest_0_), channel_id=1, source_target_pairs={{0,64},{1,17},{2,66},{3,19},{4,68},{5,21},{6,70},{7,23},{8,72},{9,... | collective-permute-start | bytes 1572872 | tf_op jit(solution)/shard_map/ppermute | solution.py:412
  87.7 2.5 %collective-permute-start.13 = (bf16[4,512,128]{2,1,0:T(8,128)(2,1)}, bf16[4,512,128]{2,1,0:T(8,128)(2,1)}, u32[]{:S(2)}, u32[]{:S(2)}) collective-permute-start(bf16[4,512,128]{2,1,0:T(8,128)(2,1)} %sum_major.1.rest_3_.rest_0_), channel_id=1, source_target_pairs={{0,96},{1,25},{2,98},{3,27},{4,100},{5,29},{6,102},{7,31},{8,104},... | collective-permute-start | bytes 1572872 | tf_op jit(solution)/shard_map/ppermute | solution.py:412
  90.2 0.0 collective-permute-done.5.rest_1_
  90.2 4.4 %all-to-all-done.2.rest_2_ = bf16[16,256,128]{2,1,0:T(8,128)(2,1)S(1)} async-done(((bf16[16,256,128]{2,1,0:T(8,128)(2,1)}), bf16[16,256,128]{2,1,0:T(8,128)(2,1)S(1)}, u32[]{:S(2)}, u32[]{:S(2)}) %all-to-all-start.2) | async-done | bytes 1048608 | tf_op jit(solution)/shard_map/all_to_all | solution.py:416
  94.6 2.7 %last_rows.1 = (bf16[2,128,128]{2,1,0:T(8,128)(2,1)S(1)}, bf16[16,256,128]{2,1,0:T(8,128)(2,1)}) custom-call(bf16[4,2,128,256]{3,2,1,0:T(8,128)(2,1)S(1)} %get-tuple-element.25.rest_0_, bf16[4,2,128,256]{3,2,1,0:T(8,128)(2,1)} %collective-permute-done.5.rest_1_, bf16[16,256,128]{2,1,0:T(8,128)(2,1)S(1)} %all-to-all-done.2.rest_2_, ...), custom_call_target="tpu_custom_call" | custom-call | flops 30000001024 | bytes 1000 | tf_op jit(solution)/shard_map/last_rows/pallas_call | solution.py:211
  97.3 4.6 %all-to-all-start.3 = ((bf16[16,256,128]{2,1,0:T(8,128)(2,1)}), bf16[16,256,128]{2,1,0:T(8,128)(2,1)S(1)}, u32[]{:S(2)}, u32[]{:S(2)}) async-start(bf16[16,256,128]{2,1,0:T(8,128)(2,1)} %get-tuple-element.36), calls=%async_computation.3 | async-start | bytes 2097152 | tf_op jit(solution)/shard_map/all_to_all | solution.py:416
  101.8 0.0 collective-permute-done.15.rest_3_
  101.8 2.2 %collective-permute-done.14.rest_2_ = bf16[4,512,128]{2,1,0:T(8,128)(2,1)} collective-permute-done((bf16[4,512,128]{2,1,0:T(8,128)(2,1)}, bf16[4,512,128]{2,1,0:T(8,128)(2,1)}, u32[]{:S(2)}, u32[]{:S(2)}) %collective-permute-start.14) | collective-permute-done | bytes 524320 | tf_op jit(solution)/shard_map/ppermute | solution.py:412
  104.0 0.0 collective-permute-done.13.rest_1_
  104.0 6.8 %first_loads.1 = (f32[4096,256]{1,0:T(8,128)}, s32[1,2048]{1,0:T(1,128)S(1)}, f32[1,2048]{1,0:T(1,128)S(1)}) custom-call(bf16[16,272,128]{2,1,0:T(8,128)(2,1)S(1)} %all-to-all-done.1.rest_2_.gathered_ref, bf16[4,512,128]{2,1,0:T(8,128)(2,1)} %sum_major.1.rest_3_.rest_0_, bf16[4,512,128]{2,1,0:T(8,128)(2,1)} %collective-permute-done.13.rest_1_, ...), custom_call_target="tpu_custom_call" | custom-call | flops 30000001024 | bytes 1000 | tf_op jit(solution)/shard_map/first_loads/pallas_call | solution.py:295
  110.8 0.7 pad_maximum_fusion.1
  111.5 5.9 %all-to-all-done.3.gathered_ref = bf16[16,256,128]{2,1,0:T(8,128)(2,1)S(1)} async-done(((bf16[16,256,128]{2,1,0:T(8,128)(2,1)}), bf16[16,256,128]{2,1,0:T(8,128)(2,1)S(1)}, u32[]{:S(2)}, u32[]{:S(2)}) %all-to-all-start.3) | async-done | bytes 1048608 | tf_op jit(solution)/shard_map/all_to_all | solution.py:416
  117.4 7.4 %all_loads.1 = (bf16[4096,256]{1,0:T(8,128)(2,1)S(1)}, bf16[8,2,1024,512]{3,2,1,0:T(8,128)(2,1)S(1)}) custom-call(s32[1,2048]{1,0:T(1,128)S(1)} %get-tuple-element.34.ids, f32[1,2048]{1,0:T(1,128)S(1)} %get-tuple-element.35.weights, bf16[16,256,128]{2,1,0:T(8,128)(2,1)S(1)} %all-to-all-done.3.gathered_ref, f32[4096,256]{1,0:T(8,128)} %get-tuple-element.37.first_ref, ...), custom_call_target="tpu_custom_call" | custom-call | tf_op jit(solution)/shard_map/all_loads/pallas_call | solution.py:343
  124.8 5.3 %stress.1 = bf16[2,1024,128]{2,1,0:T(8,128)(2,1)} custom-call(bf16[4096,256]{1,0:T(8,128)(2,1)S(1)} %get-tuple-element.38.loads_ref, bf16[8,2,1024,512]{3,2,1,0:T(8,128)(2,1)S(1)} %get-tuple-element.39.maps_ref), custom_call_target="tpu_custom_call" | custom-call | tf_op jit(solution)/shard_map/stress/pallas_call | solution.py:381
  (23 shorter events, 0.1 us)
Async XLA Ops:
  7.2 0.9 copy-start.9
  7.2 1.0 copy-start.10
  7.2 1.0 copy-start.11
  7.2 5.8 %copy-start.12 = (bf16[2,128,128]{2,1,0:T(8,128)(2,1)S(1)}, bf16[2,128,128]{2,1,0:T(8,128)(2,1)}, u32[]{:S(2)}) copy-start(bf16[2,128,128]{2,1,0:T(8,128)(2,1)} %param.11) | copy-start | bytes 196612
  7.2 110.2 %all-gather.3.cloned.1.call-start = ((), (), s32[]{:S(2)}) async-start(), calls=%async_computation.4 | async-start | bytes 18874368 | tf_op jit(solution)/shard_map/all_gather | solution.py:433
  7.9 14.2 %copy-start.13 = (bf16[3072]{0:T(1024)(128)(2,1)S(1)}, bf16[3072]{0:T(1024)(128)(2,1)}, u32[]{:S(2)}) copy-start(bf16[3072]{0:T(1024)(128)(2,1)} %param.18) | copy-start | bytes 18436
  8.0 14.2 %copy-start = (bf16[2,3072,128]{2,1,0:T(8,128)(2,1)S(1)}, bf16[2,3072,128]{2,1,0:T(8,128)(2,1)}, u32[]{:S(2)}) copy-start(bf16[2,3072,128]{2,1,0:T(8,128)(2,1)} %earlier_ref.1) | copy-start | bytes 4718596
  8.0 14.2 %copy-start.1 = (s32[3072]{0:T(1024)S(1)}, s32[3072]{0:T(1024)}, u32[]{:S(2)}) copy-start(s32[3072]{0:T(1024)} %param.17) | copy-start | bytes 36868
  8.2 26.4 %collective-permute-start.2 = (bf16[3,2,128,256]{3,2,1,0:T(8,128)(2,1)S(1)}, bf16[3,2,128,256]{3,2,1,0:T(8,128)(2,1)S(1)}, u32[]{:S(2)}, u32[]{:S(2)}) collective-permute-start(bf16[3,2,128,256]{3,2,1,0:T(8,128)(2,1)S(1)} %pad_maximum_fusion.refs_0_), channel_id=1, source_target_pairs={{0,6},{1,7},{2,0},{3,1},{4,2},{5,3},{6,4},{7,5},{8,14},{9,15},{10,... | collective-permute-start | bytes 1179656 | tf_op jit(solution)/shard_map/ppermute | solution.py:396
  11.4 24.7 %collective-permute-start.1 = (bf16[3,2,128,256]{3,2,1,0:T(8,128)(2,1)S(1)}, bf16[3,2,128,256]{3,2,1,0:T(8,128)(2,1)}, u32[]{:S(2)}, u32[]{:S(2)}) collective-permute-start(bf16[3,2,128,256]{3,2,1,0:T(8,128)(2,1)S(1)} %pad_maximum_fusion.refs_0_), channel_id=1, source_target_pairs={{0,4},{1,5},{2,6},{3,7},{4,0},{5,1},{6,2},{7,3},{8,12},{9,13},{10,... | collective-permute-start | bytes 1179656 | tf_op jit(solution)/shard_map/ppermute | solution.py:396
  12.0 24.3 %collective-permute-start = (bf16[3,2,128,256]{3,2,1,0:T(8,128)(2,1)S(1)}, bf16[3,2,128,256]{3,2,1,0:T(8,128)(2,1)}, u32[]{:S(2)}, u32[]{:S(2)}) collective-permute-start(bf16[3,2,128,256]{3,2,1,0:T(8,128)(2,1)S(1)} %pad_maximum_fusion.refs_0_), channel_id=1, source_target_pairs={{0,2},{1,3},{2,4},{3,5},{4,6},{5,7},{6,0},{7,1},{8,10},{9,11},{10,... | collective-permute-start | bytes 1179656 | tf_op jit(solution)/shard_map/ppermute | solution.py:396
  14.2 27.1 %all-to-all-start = ((bf16[16,256,128]{2,1,0:T(8,128)(2,1)}), bf16[16,256,128]{2,1,0:T(8,128)(2,1)S(1)}, u32[]{:S(2)}, u32[]{:S(2)}) async-start(bf16[16,256,128]{2,1,0:T(8,128)(2,1)} %broadcast_in_dim.16), calls=%async_computation | async-start | bytes 2097152 | tf_op jit(solution)/shard_map/all_to_all | solution.py:416
  30.0 8.2 %copy-start.2 = (bf16[4,512,128]{2,1,0:T(8,128)(2,1)}, bf16[4,512,128]{2,1,0:T(8,128)(2,1)S(1)}, u32[]{:S(2)}) copy-start(bf16[4,512,128]{2,1,0:T(8,128)(2,1)S(1)} %get-tuple-element.21.refs_4_.refs_0_) | copy-start | bytes 1572868
  30.0 23.2 %collective-permute-start.7 = (bf16[4,512,128]{2,1,0:T(8,128)(2,1)}, bf16[4,512,128]{2,1,0:T(8,128)(2,1)}, u32[]{:S(2)}, u32[]{:S(2)}) collective-permute-start(bf16[4,512,128]{2,1,0:T(8,128)(2,1)} %get-tuple-element.28), channel_id=1, source_target_pairs={{0,32},{1,9},{2,34},{3,11},{4,36},{5,13},{6,38},{7,15},{8,40},{9,1... | collective-permute-start | bytes 1572872 | tf_op jit(solution)/shard_map/ppermute | solution.py:412
  32.0 21.3 %collective-permute-start.8 = (bf16[4,512,128]{2,1,0:T(8,128)(2,1)}, bf16[4,512,128]{2,1,0:T(8,128)(2,1)}, u32[]{:S(2)}, u32[]{:S(2)}) collective-permute-start(bf16[4,512,128]{2,1,0:T(8,128)(2,1)} %get-tuple-element.29), channel_id=1, source_target_pairs={{0,64},{1,17},{2,66},{3,19},{4,68},{5,21},{6,70},{7,23},{8,72},{9,... | collective-permute-start | bytes 1572872 | tf_op jit(solution)/shard_map/ppermute | solution.py:412
  34.6 1.7 %copy-start.14 = (bf16[3,2,128,256]{3,2,1,0:T(8,128)(2,1)}, bf16[3,2,128,256]{3,2,1,0:T(8,128)(2,1)S(1)}, u32[]{:S(2)}) copy-start(bf16[3,2,128,256]{3,2,1,0:T(8,128)(2,1)S(1)} %collective-permute-done.2.refs_3_) | copy-start | bytes 1179652
  34.7 18.6 %collective-permute-start.9 = (bf16[4,512,128]{2,1,0:T(8,128)(2,1)}, bf16[4,512,128]{2,1,0:T(8,128)(2,1)}, u32[]{:S(2)}, u32[]{:S(2)}) collective-permute-start(bf16[4,512,128]{2,1,0:T(8,128)(2,1)} %get-tuple-element.30), channel_id=1, source_target_pairs={{0,96},{1,25},{2,98},{3,27},{4,100},{5,29},{6,102},{7,31},{8,104},... | collective-permute-start | bytes 1572872 | tf_op jit(solution)/shard_map/ppermute | solution.py:412
  36.3 5.0 %copy-start.7 = (s32[2,128]{1,0:T(2,128)S(1)}, s32[2,128]{1,0:T(2,128)}, u32[]{:S(2)}) copy-start(s32[2,128]{1,0:T(2,128)} %rest_5_.1) | copy-start | bytes 3076
  36.3 5.0 %copy-start.8 = (bf16[2,128]{1,0:T(2,128)(2,1)S(1)}, bf16[2,128]{1,0:T(2,128)(2,1)}, u32[]{:S(2)}) copy-start(bf16[2,128]{1,0:T(2,128)(2,1)} %rest_6_.1) | copy-start | bytes 1540
  38.3 1.6 %collective-permute-start.3 = (bf16[2,2,128,256]{3,2,1,0:T(8,128)(2,1)S(1)}, bf16[2,2,128,256]{3,2,1,0:T(8,128)(2,1)S(1)}, u32[]{:S(2)}, u32[]{:S(2)}) collective-permute-start(bf16[2,2,128,256]{3,2,1,0:T(8,128)(2,1)S(1)} %get-tuple-element.22.rest_0_), channel_id=1, source_target_pairs={{0,1},{1,0},{2,3},{3,2},{4,5},{5,4},{6,7},{7,6},{8,9},{9,8},{10,11... | collective-permute-start | bytes 786440 | tf_op jit(solution)/shard_map/ppermute | solution.py:400
  38.4 1.9 %collective-permute-start.4 = (bf16[2,2,128,256]{3,2,1,0:T(8,128)(2,1)S(1)}, bf16[2,2,128,256]{3,2,1,0:T(8,128)(2,1)S(1)}, u32[]{:S(2)}, u32[]{:S(2)}) collective-permute-start(bf16[2,2,128,256]{3,2,1,0:T(8,128)(2,1)S(1)} %get-tuple-element.23.rest_1_), channel_id=1, source_target_pairs={{0,1},{1,0},{2,3},{3,2},{4,5},{5,4},{6,7},{7,6},{8,9},{9,8},{10,11... | collective-permute-start | bytes 786440 | tf_op jit(solution)/shard_map/ppermute | solution.py:400
  39.9 50.3 %collective-permute-start.5 = (bf16[4,2,128,256]{3,2,1,0:T(8,128)(2,1)S(1)}, bf16[4,2,128,256]{3,2,1,0:T(8,128)(2,1)}, u32[]{:S(2)}, u32[]{:S(2)}) collective-permute-start(bf16[4,2,128,256]{3,2,1,0:T(8,128)(2,1)S(1)} %get-tuple-element.25.rest_0_), channel_id=1, source_target_pairs={{0,1},{1,0},{2,3},{3,2},{4,5},{5,4},{6,7},{7,6},{8,9},{9,8},{10,11... | collective-permute-start | bytes 1572872 | tf_op jit(solution)/shard_map/ppermute | solution.py:400
  40.3 0.7 copy-start.4
  41.0 12.3 %copy-start.3 = (bf16[4,512,128]{2,1,0:T(8,128)(2,1)S(1)}, bf16[4,512,128]{2,1,0:T(8,128)(2,1)}, u32[]{:S(2)}) copy-start(bf16[4,512,128]{2,1,0:T(8,128)(2,1)} %copy-done.2) | copy-start | bytes 1572868
  41.0 21.4 %collective-permute-start.6 = (bf16[4,2,128,256]{3,2,1,0:T(8,128)(2,1)S(1)}, bf16[4,2,128,256]{3,2,1,0:T(8,128)(2,1)}, u32[]{:S(2)}, u32[]{:S(2)}) collective-permute-start(bf16[4,2,128,256]{3,2,1,0:T(8,128)(2,1)S(1)} %get-tuple-element.26.rest_0_), channel_id=1, source_target_pairs={{0,1},{1,0},{2,3},{3,2},{4,5},{5,4},{6,7},{7,6},{8,9},{9,8},{10,11... | collective-permute-start | bytes 1572872 | tf_op jit(solution)/shard_map/ppermute | solution.py:400
  41.3 1.0 copy-start.5
  44.2 28.3 %all-to-all-start.1 = ((bf16[16,272,128]{2,1,0:T(8,128)(2,1)}), bf16[16,272,128]{2,1,0:T(8,128)(2,1)S(1)}, u32[]{:S(2)}, u32[]{:S(2)}) async-start(bf16[16,272,128]{2,1,0:T(8,128)(2,1)} %get-tuple-element.27), calls=%async_computation.1 | async-start | bytes 2228224 | tf_op jit(solution)/shard_map/all_to_all | solution.py:416
  53.3 19.2 %copy-start.6 = (bf16[2,128,128]{2,1,0:T(8,128)(2,1)S(1)}, bf16[2,128,128]{2,1,0:T(8,128)(2,1)}, u32[]{:S(2)}) copy-start(bf16[2,128,128]{2,1,0:T(8,128)(2,1)} %rest_3_.1) | copy-start | bytes 196612
  56.1 22.9 %collective-permute-start.12 = (bf16[4,512,128]{2,1,0:T(8,128)(2,1)}, bf16[4,512,128]{2,1,0:T(8,128)(2,1)}, u32[]{:S(2)}, u32[]{:S(2)}) collective-permute-start(bf16[4,512,128]{2,1,0:T(8,128)(2,1)} %sum_minor.1.rest_4_.refs_0_), channel_id=1, source_target_pairs={{0,8},{1,33},{2,10},{3,35},{4,12},{5,37},{6,14},{7,39},{8,16},{9,4... | collective-permute-start | bytes 1572872 | tf_op jit(solution)/shard_map/ppermute | solution.py:412
  58.3 22.9 %collective-permute-start.11 = (bf16[4,512,128]{2,1,0:T(8,128)(2,1)}, bf16[4,512,128]{2,1,0:T(8,128)(2,1)}, u32[]{:S(2)}, u32[]{:S(2)}) collective-permute-start(bf16[4,512,128]{2,1,0:T(8,128)(2,1)} %sum_minor.1.rest_4_.refs_0_), channel_id=1, source_target_pairs={{0,16},{1,65},{2,18},{3,67},{4,20},{5,69},{6,22},{7,71},{8,24},{9,... | collective-permute-start | bytes 1572872 | tf_op jit(solution)/shard_map/ppermute | solution.py:412
  60.9 20.8 %collective-permute-start.10 = (bf16[4,512,128]{2,1,0:T(8,128)(2,1)}, bf16[4,512,128]{2,1,0:T(8,128)(2,1)}, u32[]{:S(2)}, u32[]{:S(2)}) collective-permute-start(bf16[4,512,128]{2,1,0:T(8,128)(2,1)} %sum_minor.1.rest_4_.refs_0_), channel_id=1, source_target_pairs={{0,24},{1,97},{2,26},{3,99},{4,28},{5,101},{6,30},{7,103},{8,0},{9... | collective-permute-start | bytes 1572872 | tf_op jit(solution)/shard_map/ppermute | solution.py:412
  75.2 19.4 %all-to-all-start.2 = ((bf16[16,256,128]{2,1,0:T(8,128)(2,1)}), bf16[16,256,128]{2,1,0:T(8,128)(2,1)S(1)}, u32[]{:S(2)}, u32[]{:S(2)}) async-start(bf16[16,256,128]{2,1,0:T(8,128)(2,1)} %get-tuple-element.31), calls=%async_computation.2 | async-start | bytes 2097152 | tf_op jit(solution)/shard_map/all_to_all | solution.py:416
  84.4 17.5 %collective-permute-start.15 = (bf16[4,512,128]{2,1,0:T(8,128)(2,1)}, bf16[4,512,128]{2,1,0:T(8,128)(2,1)}, u32[]{:S(2)}, u32[]{:S(2)}) collective-permute-start(bf16[4,512,128]{2,1,0:T(8,128)(2,1)} %sum_major.1.rest_3_.rest_0_), channel_id=1, source_target_pairs={{0,32},{1,9},{2,34},{3,11},{4,36},{5,13},{6,38},{7,15},{8,40},{9,1... | collective-permute-start | bytes 1572872 | tf_op jit(solution)/shard_map/ppermute | solution.py:412
  85.0 19.1 %collective-permute-start.14 = (bf16[4,512,128]{2,1,0:T(8,128)(2,1)}, bf16[4,512,128]{2,1,0:T(8,128)(2,1)}, u32[]{:S(2)}, u32[]{:S(2)}) collective-permute-start(bf16[4,512,128]{2,1,0:T(8,128)(2,1)} %sum_major.1.rest_3_.rest_0_), channel_id=1, source_target_pairs={{0,64},{1,17},{2,66},{3,19},{4,68},{5,21},{6,70},{7,23},{8,72},{9,... | collective-permute-start | bytes 1572872 | tf_op jit(solution)/shard_map/ppermute | solution.py:412
  87.7 16.3 %collective-permute-start.13 = (bf16[4,512,128]{2,1,0:T(8,128)(2,1)}, bf16[4,512,128]{2,1,0:T(8,128)(2,1)}, u32[]{:S(2)}, u32[]{:S(2)}) collective-permute-start(bf16[4,512,128]{2,1,0:T(8,128)(2,1)} %sum_major.1.rest_3_.rest_0_), channel_id=1, source_target_pairs={{0,96},{1,25},{2,98},{3,27},{4,100},{5,29},{6,102},{7,31},{8,104},... | collective-permute-start | bytes 1572872 | tf_op jit(solution)/shard_map/ppermute | solution.py:412
  97.3 20.1 %all-to-all-start.3 = ((bf16[16,256,128]{2,1,0:T(8,128)(2,1)}), bf16[16,256,128]{2,1,0:T(8,128)(2,1)S(1)}, u32[]{:S(2)}, u32[]{:S(2)}) async-start(bf16[16,256,128]{2,1,0:T(8,128)(2,1)} %get-tuple-element.36), calls=%async_computation.3 | async-start | bytes 2097152 | tf_op jit(solution)/shard_map/all_to_all | solution.py:416
Sparse Core Ops, SparseCore 0:
  9.8 91.7 all-gather.2
